TPU v7x, 32 devices: a whole 2x2x4 slice. The times are simulated.
32 devices in a mesh: grp: 2 (over y), lat: 4 (over z), lon: 2 (over x), role: 2 (over core).
Axes of the slice: x: 2, y: 2, z: 4, core: 2. Of those that a mesh axis runs over, the one named last changes fastest.
Arguments:
- eastern_edge_current: float32 [8, 128, 256], P('lon', ('grp', 'lat', 'role')), parts along dimension 1, may hold values from -1.5 to 1.5
- northern_edge_current: float32 [8, 128, 256], P('lon', ('grp', 'lat', 'role')), parts along dimension 1, may hold values from -1.5 to 1.5
- thermal_anomaly: float32 [8, 128, 256], P('lon', ('grp', 'lat', 'role')), parts along dimension 1, may hold values from -6 to 6
- prior_warming: float32 [8, 128, 256], P('lon', ('grp', 'lat', 'role')), parts along dimension 1, may hold values from 0 to 0.5
- solute_fields: float32 [24, 8, 128, 256], P(None, None, ('grp', 'lat', 'role'), 'lon'), parts along dimension 2, may hold values from -6 to 6
- submerged_layer_count: int32 [128, 256], P(('grp', 'lat', 'role')), parts along dimension 0, may hold values from 0 to 8
- reaction_rates: float32 [24, 24], replicated, may hold values from -1.25 to 1.25
Outputs:
- u_out: float32 [8, 128, 256], P('lon', ('grp', 'lat', 'role')), parts along dimension 1
- v_out: float32 [8, 128, 256], P('lon', ('grp', 'lat', 'role')), parts along dimension 1
- temp_out: float32 [8, 128, 256], P('lon', ('grp', 'lat', 'role')), parts along dimension 1
- heating_out: float32 [8, 128, 256], P('lon', ('grp', 'lat', 'role')), parts along dimension 1
- tracers_out: float32 [24, 8, 128, 256], P(None, None, ('grp', 'lat', 'role'), 'lon'), parts along dimension 2
There are 2 independent parts, one for each index of `grp`. A program takes and returns all parts, laid end to end along the dimension named above; an argument that names none is the same for every part. Nothing has to cross between parts.
All inputs are finite; a program needn't handle non-finite values.
Results may differ from a plain program's by a relative error of at most 0.0001.
Values sent between devices are 32-bit elements; how exact they have to be, the bound alone decides.
No kernel may reach another device: no remote copies, remote signals or barrier semaphores. Data moves between devices by JAX's collectives and lax.ppermute only.
A program may use at most 64 MiB of HBM per device.

v0:
```python
import jax
import jax.numpy as jnp
from jax import lax
from jax.sharding import PartitionSpec as P

DEPTH_LAYERS = 8
STEPS = 2


def padded(shard, sides, width):
    for axis, dim in sides:
        count, length = (lax.axis_size(axis), shard.shape[dim])
        up = [(i, (i + 1) % count) for i in range(count - 1)]
        down = [(j, i) for i, j in up]
        last = lax.slice_in_dim(shard, length - width, length, axis=dim)
        leading = lax.slice_in_dim(shard, 0, width, axis=dim)
        before = lax.ppermute(last, axis, up)
        after = lax.ppermute(leading, axis, down)
        shard = jnp.concatenate([before, shard, after], axis=dim)
    return shard


def passed_along(shard, axis, by):
    count = lax.axis_size(axis)
    pairs = [(i, i + by) for i in range(count) if 0 <= i + by < count]
    return lax.ppermute(shard, axis, pairs)


def flow_advance(extended, wet_ext, thermal_energy, coriolis_parameter):

    def inner(q):
        return q[..., 1:-1, 1:-1]

    def east_of(q):
        return q[..., 1:-1, 2:]

    def west_of(q):
        return q[..., 1:-1, :-2]

    def north_of(q):
        return q[..., 2:, 1:-1]

    def south_of(q):
        return q[..., :-2, 1:-1]

    def diffusion_operator(q):
        return east_of(q) + west_of(q) + north_of(q) + south_of(q) - 4.0 * inner(q)

    u_ext, v_ext, temp_ext = (extended[0], extended[1], extended[2])
    ocean_mask = inner(wet_ext)
    ocean_mask_eastward = ocean_mask * east_of(wet_ext)
    ocean_mask_poleward = ocean_mask * north_of(wet_ext)
    u_here, v_here, temp_here = (inner(u_ext), inner(v_ext), inner(temp_ext))
    updated_eastward_flow = ocean_mask_eastward * (
        u_here
        + 0.1 * diffusion_operator(u_ext)
        + 0.3 * coriolis_parameter * v_here
        - 0.2 * (east_of(temp_ext) - temp_here)
    )
    updated_poleward_flow = ocean_mask_poleward * (
        v_here
        + 0.1 * diffusion_operator(v_ext)
        - 0.3 * coriolis_parameter * u_here
        - 0.2 * (north_of(temp_ext) - temp_here)
    )
    temp_new = ocean_mask * (temp_here + 0.1 * diffusion_operator(temp_ext) + 0.5 * thermal_energy)
    return (updated_eastward_flow, updated_poleward_flow, temp_new)


def tracer_step(solute_fields, faces, ocean_mask, reaction_rates):
    count = solute_fields.shape[0]
    layered_bundle = jnp.concatenate([solute_fields, faces], axis=0)
    extended = padded(layered_bundle, ((("lat", "role"), 2), ("lon", 3)), 1)
    solute_amount = extended[:count]
    east_u = extended[count]
    north_v = extended[count + 1]
    face_u = east_u[:, 1:-1, :-1]
    flux_x = (
        jnp.maximum(face_u, 0.0) * solute_amount[:, :, 1:-1, :-1]
        + jnp.minimum(face_u, 0.0) * solute_amount[:, :, 1:-1, 1:]
    )
    face_v = north_v[:, :-1, 1:-1]
    flux_y = (
        jnp.maximum(face_v, 0.0) * solute_amount[:, :, :-1, 1:-1]
        + jnp.minimum(face_v, 0.0) * solute_amount[:, :, 1:, 1:-1]
    )
    here = solute_amount[:, :, 1:-1, 1:-1]
    advected = here - 0.5 * (
        flux_x[..., 1:] - flux_x[..., :-1] + (flux_y[..., 1:, :] - flux_y[..., :-1, :])
    )
    atten = 0.1 + 0.3 * jnp.maximum(advected[0], 0.0)
    summed = jnp.cumsum(atten, axis=0)
    depth_tau = jnp.concatenate([jnp.zeros_like(atten[:1]), summed[:-1]], axis=0)
    top = jnp.exp(-depth_tau)
    thermal_energy = 2.0 * ocean_mask * (top - jnp.exp(-(depth_tau + atten)))
    react = jnp.einsum("ab,bzyx->azyx", reaction_rates, advected, precision=lax.Precision.HIGHEST)
    return (ocean_mask * (advected + 0.5 * top * react), thermal_energy)


def shards(
    eastern_edge_current,
    northern_edge_current,
    thermal_anomaly,
    prior_warming,
    solute_fields,
    submerged_layer_count,
    reaction_rates,
):
    level_share = eastern_edge_current.shape[0]
    rows = eastern_edge_current.shape[1]
    width = solute_fields.shape[3]
    strip = lax.axis_index(("lat", "role"))
    column = lax.axis_index("lon")
    total_rows = rows * lax.axis_size(("lat", "role"))
    row_ids = (strip * rows + jnp.arange(rows, dtype=jnp.int32)).astype(jnp.float32)
    coriolis_parameter = (2.0 * (row_ids + 0.5) / total_rows - 1.0)[:, None]
    northern_row = passed_along(submerged_layer_count[:1], ("lat", "role"), -1)
    depth_ext = jnp.concatenate(
        [jnp.zeros_like(submerged_layer_count[:1]), submerged_layer_count, northern_row], axis=0
    )
    depth_pad = jnp.pad(depth_ext, ((0, 0), (1, 1)))
    tile_depth = lax.dynamic_slice_in_dim(depth_pad, column * width, width + 2, 1)
    all_levels = jnp.arange(DEPTH_LAYERS, dtype=jnp.int32)
    wet_tile_ext = (all_levels[:, None, None] < tile_depth[None, :, :]).astype(jnp.float32)
    wet_tile = wet_tile_ext[:, 1:-1, 1:-1]
    solute_amount = solute_fields
    own_levels = column * level_share + jnp.arange(level_share, dtype=jnp.int32)
    wet_strip_ext = (own_levels[:, None, None] < depth_pad[None, :, :]).astype(jnp.float32)
    eastward_current, poleward_current, seawater_warmth, thermal_energy = (
        eastern_edge_current,
        northern_edge_current,
        thermal_anomaly,
        prior_warming,
    )
    for step in range(STEPS):
        layered_bundle = jnp.stack([eastward_current, poleward_current, seawater_warmth])
        extended = padded(layered_bundle, ((("lat", "role"), 2),), 1)
        extended = jnp.pad(extended, ((0, 0), (0, 0), (0, 0), (1, 1)))
        eastward_current, poleward_current, seawater_warmth = flow_advance(
            extended, wet_strip_ext, thermal_energy, coriolis_parameter
        )
        faces = lax.all_to_all(
            jnp.stack([eastward_current, poleward_current]),
            "lon",
            split_axis=3,
            concat_axis=1,
            tiled=True,
        )
        solute_amount, heat_tile = tracer_step(solute_amount, faces, wet_tile, reaction_rates)
        thermal_energy = lax.all_to_all(heat_tile, "lon", split_axis=0, concat_axis=2, tiled=True)
    return (eastward_current, poleward_current, seawater_warmth, thermal_energy, solute_amount)


def solution(mesh):
    return jax.shard_map(
        shards,
        mesh=mesh,
        in_specs=(
            P("lon", ("grp", "lat", "role"), None),
            P("lon", ("grp", "lat", "role"), None),
            P("lon", ("grp", "lat", "role"), None),
            P("lon", ("grp", "lat", "role"), None),
            P(None, None, ("grp", "lat", "role"), "lon"),
            P(("grp", "lat", "role"), None),
            P(),
        ),
        out_specs=(
            P("lon", ("grp", "lat", "role"), None),
            P("lon", ("grp", "lat", "role"), None),
            P("lon", ("grp", "lat", "role"), None),
            P("lon", ("grp", "lat", "role"), None),
            P(None, None, ("grp", "lat", "role"), "lon"),
        ),
        check_vma=False,
    )
```

profile of v0, /device:TPU:0, one launch (start us, length us, event | category | flops | bytes accessed | tf_op | source)
XLA Modules:
  0.0 117.5 jit_solution(12957497192411766998)
XLA Ops:
  3.5 3.0 %collective-permute-start.1 = (f32[3,4,1,256]{3,1,2,0:T(4,128)S(1)}, f32[3,4,1,256]{3,1,2,0:T(4,128)S(1)}, u32[]{:S(2)}, u32[]{:S(2)}) collective-permute-start(f32[3,4,1,256]{3,1,2,0:T(4,128)S(1)} %get-tuple-element.62), channel_id=1, source_target_pairs={{0,1},{1,4},{4,5},{5,8},{8,9},{9,12},{12,13},{2,3},{3,6},{6,7},{7,... | collective-permute-start | bytes 36872 | tf_op jit(solution)/shard_map/ppermute | solution.py:17
  9.6 2.2 %collective-permute-done.2 = f32[3,4,1,256]{3,1,2,0:T(4,128)S(1)} collective-permute-done((f32[3,4,1,256]{3,1,2,0:T(4,128)S(1)}, f32[3,4,1,256]{3,1,2,0:T(4,128)S(1)}, u32[]{:S(2)}, u32[]{:S(2)}) %collective-permute-start.2) | collective-permute-done | bytes 12320 | tf_op jit(solution)/shard_map/ppermute | solution.py:18
  12.5 4.3 %collective-permute-start.3 = (f32[3,4,1,256]{3,1,2,0:T(4,128)S(1)}, f32[3,4,1,256]{3,1,2,0:T(4,128)S(1)}, u32[]{:S(2)}, u32[]{:S(2)}) collective-permute-start(f32[3,4,1,256]{3,1,2,0:T(4,128)S(1)} %get-tuple-element.60), channel_id=1, source_target_pairs={{0,1},{1,4},{4,5},{5,8},{8,9},{9,12},{12,13},{2,3},{3,6},{6,7},{7,... | collective-permute-start | bytes 36872 | tf_op jit(solution)/shard_map/ppermute | solution.py:17
  18.7 1.8 %reshape.56 = f32[2,1,8192]{2,1,0:T(1,128)} reshape(f32[256,2,4,8]{3,2,1,0:T(4,128)S(1)} %bitcast.80) | data formatting | bytes 131072
  20.5 3.4 %all-to-all-start = ((f32[2,1,8192]{2,1,0:T(1,128)}), f32[2,1,8192]{2,1,0:T(1,128)S(1)}, u32[]{:S(2)}, u32[]{:S(2)}) async-start(f32[2,1,8192]{2,1,0:T(1,128)} %reshape.56), calls=%async_computation | async-start | bytes 131072 | tf_op jit(solution)/shard_map/all_to_all | solution.py:142
  24.1 4.1 %all-to-all-done = f32[2,1,8192]{2,1,0:T(1,128)S(1)} async-done(((f32[2,1,8192]{2,1,0:T(1,128)}), f32[2,1,8192]{2,1,0:T(1,128)S(1)}, u32[]{:S(2)}, u32[]{:S(2)}) %all-to-all-start) | async-done | bytes 65568 | tf_op jit(solution)/shard_map/all_to_all | solution.py:142
  31.4 2.0 %collective-permute-start.5 = (f32[26,8,1,128]{3,2,1,0:T(1,128)S(1)}, f32[26,8,1,128]{3,2,1,0:T(1,128)S(1)}, u32[]{:S(2)}, u32[]{:S(2)}) collective-permute-start(f32[26,8,1,128]{3,2,1,0:T(1,128)S(1)} %get-tuple-element.40), channel_id=1, source_target_pairs={{0,1},{1,4},{4,5},{5,8},{8,9},{9,12},{12,13},{2,3},{3,6},{6,7},{7,... | collective-permute-start | bytes 319496 | tf_op jit(solution)/shard_map/ppermute | solution.py:17
  34.8 3.8 %collective-permute-done.6 = f32[26,8,1,128]{3,2,1,0:T(1,128)S(1)} collective-permute-done((f32[26,8,1,128]{3,2,1,0:T(1,128)S(1)}, f32[26,8,1,128]{3,2,1,0:T(1,128)S(1)}, u32[]{:S(2)}, u32[]{:S(2)}) %collective-permute-start.6) | collective-permute-done | bytes 106528 | tf_op jit(solution)/shard_map/ppermute | solution.py:18
  39.0 1.8 %fusion.102 = (f32[26,8,10,1]{3,2,1,0:T(8,128)}, f32[26,8,10,1]{3,2,1,0:T(8,128)S(1)}) fusion(f32[26,8,10,128]{3,2,1,0:T(8,128)S(1)} %pad_maximum_fusion), kind=kLoop, calls=%fused_computation.213 | loop fusion | bytes 33280 | tf_op jit(solution)/shard_map/slice | solution.py:15
  40.8 2.2 %copy.146 = f32[26,8,10,1]{0,1,3,2:T(8,128)S(1)} copy(f32[26,8,10,1]{3,2,1,0:T(8,128)} %get-tuple-element.36) | data formatting | bytes 16640 | tf_op jit(solution)/shard_map/slice | solution.py:15
  45.2 4.5 %collective-permute-start.7 = (f32[26,8,10,1]{0,1,3,2:T(8,128)S(1)}, f32[26,8,10,1]{0,1,3,2:T(8,128)S(1)}, u32[]{:S(2)}, u32[]{:S(2)}) collective-permute-start(f32[26,8,10,1]{0,1,3,2:T(8,128)S(1)} %copy.146), channel_id=1, source_target_pairs={{0,2},{1,3},{4,6},{5,7},{8,10},{9,11},{12,14},{13,15},{16,18},{17,... | collective-permute-start | bytes 24968 | tf_op jit(solution)/shard_map/ppermute | solution.py:17
  53.0 2.6 %copy.149 = f32[26,8,10,1]{3,2,1,0:T(8,128)} copy(f32[26,8,10,1]{0,1,3,2:T(8,128)S(1)} %collective-permute-done.8) | data formatting | bytes 16640 | tf_op jit(solution)/shard_map/ppermute | solution.py:18
  59.8 3.6 %all-to-all-start.1 = ((f32[8,8,128]{2,1,0:T(8,128)}), f32[8,8,128]{2,1,0:T(8,128)S(1)}, u32[]{:S(2)}, u32[]{:S(2)}) async-start(f32[8,8,128]{2,1,0:T(8,128)} %get-tuple-element.67), calls=%async_computation.1 | async-start | bytes 65536 | tf_op jit(solution)/shard_map/all_to_all | solution.py:150
  64.6 2.8 %all-to-all-done.1 = f32[8,8,128]{2,1,0:T(8,128)S(1)} async-done(((f32[8,8,128]{2,1,0:T(8,128)}), f32[8,8,128]{2,1,0:T(8,128)S(1)}, u32[]{:S(2)}, u32[]{:S(2)}) %all-to-all-start.1) | async-done | bytes 32800 | tf_op jit(solution)/shard_map/all_to_all | solution.py:150
  70.8 3.3 %all-to-all-start.2 = ((f32[2,1,8192]{2,1,0:T(1,128)}), f32[2,1,8192]{2,1,0:T(1,128)S(1)}, u32[]{:S(2)}, u32[]{:S(2)}) async-start(f32[2,1,8192]{2,1,0:T(1,128)} %reshape.58), calls=%async_computation.2 | async-start | bytes 131072 | tf_op jit(solution)/shard_map/all_to_all | solution.py:142
  75.1 3.4 %all-to-all-done.2 = f32[2,1,8192]{2,1,0:T(1,128)S(1)} async-done(((f32[2,1,8192]{2,1,0:T(1,128)}), f32[2,1,8192]{2,1,0:T(1,128)S(1)}, u32[]{:S(2)}, u32[]{:S(2)}) %all-to-all-start.2) | async-done | bytes 65568 | tf_op jit(solution)/shard_map/all_to_all | solution.py:142
  81.1 2.0 %collective-permute-start.9 = (f32[26,8,1,128]{3,2,1,0:T(1,128)S(1)}, f32[26,8,1,128]{3,2,1,0:T(1,128)S(1)}, u32[]{:S(2)}, u32[]{:S(2)}) collective-permute-start(f32[26,8,1,128]{3,2,1,0:T(1,128)S(1)} %get-tuple-element.38), channel_id=1, source_target_pairs={{0,1},{1,4},{4,5},{5,8},{8,9},{9,12},{12,13},{2,3},{3,6},{6,7},{7,... | collective-permute-start | bytes 319496 | tf_op jit(solution)/shard_map/ppermute | solution.py:17
  84.5 4.2 %collective-permute-done.10 = f32[26,8,1,128]{3,2,1,0:T(1,128)S(1)} collective-permute-done((f32[26,8,1,128]{3,2,1,0:T(1,128)S(1)}, f32[26,8,1,128]{3,2,1,0:T(1,128)S(1)}, u32[]{:S(2)}, u32[]{:S(2)}) %collective-permute-start.10) | collective-permute-done | bytes 106528 | tf_op jit(solution)/shard_map/ppermute | solution.py:18
  89.0 1.8 %fusion.101 = (f32[26,8,10,1]{3,2,1,0:T(8,128)}, f32[26,8,10,1]{3,2,1,0:T(8,128)S(1)}) fusion(f32[26,8,10,128]{3,2,1,0:T(8,128)S(1)} %pad_maximum_fusion.1), kind=kLoop, calls=%fused_computation.212 | loop fusion | bytes 33280 | tf_op jit(solution)/shard_map/slice | solution.py:15
  90.8 2.2 %copy.157 = f32[26,8,10,1]{0,1,3,2:T(8,128)S(1)} copy(f32[26,8,10,1]{3,2,1,0:T(8,128)} %get-tuple-element.34) | data formatting | bytes 16640 | tf_op jit(solution)/shard_map/slice | solution.py:15
  93.0 1.9 %collective-permute-start.11 = (f32[26,8,10,1]{0,1,3,2:T(8,128)S(1)}, f32[26,8,10,1]{0,1,3,2:T(8,128)S(1)}, u32[]{:S(2)}, u32[]{:S(2)}) collective-permute-start(f32[26,8,10,1]{0,1,3,2:T(8,128)S(1)} %copy.157), channel_id=1, source_target_pairs={{0,2},{1,3},{4,6},{5,7},{8,10},{9,11},{12,14},{13,15},{16,18},{17,... | collective-permute-start | bytes 24968 | tf_op jit(solution)/shard_map/ppermute | solution.py:17
  101.8 2.6 %copy.160 = f32[26,8,10,1]{3,2,1,0:T(8,128)} copy(f32[26,8,10,1]{0,1,3,2:T(8,128)S(1)} %collective-permute-done.12) | data formatting | bytes 16640 | tf_op jit(solution)/shard_map/ppermute | solution.py:18
  109.7 3.3 %all-to-all-start.3 = ((f32[8,8,128]{2,1,0:T(8,128)}), f32[8,8,128]{2,1,0:T(8,128)S(1)}, u32[]{:S(2)}, u32[]{:S(2)}) async-start(f32[8,8,128]{2,1,0:T(8,128)} %get-tuple-element.65), calls=%async_computation.3 | async-start | bytes 65536 | tf_op jit(solution)/shard_map/all_to_all | solution.py:150
  114.1 2.8 %all-to-all-done.3 = f32[8,8,128]{2,1,0:T(8,128)S(1)} async-done(((f32[8,8,128]{2,1,0:T(8,128)}), f32[8,8,128]{2,1,0:T(8,128)S(1)}, u32[]{:S(2)}, u32[]{:S(2)}) %all-to-all-start.3) | async-done | bytes 32800 | tf_op jit(solution)/shard_map/all_to_all | solution.py:150
  (114 shorter events, 46.4 us)
Async XLA Ops:
  0.6 62.7 %copy-start = (f32[24,24]{1,0:T(8,128)S(1)}, f32[24,24]{1,0:T(8,128)}, u32[]{:S(2)}) copy-start(f32[24,24]{1,0:T(8,128)} %param.13) | copy-start | bytes 6916
  0.6 11.6 %copy-start.12 = (f32[4,8,256]{2,1,0:T(8,128)S(1)}, f32[4,8,256]{2,1,0:T(8,128)}, u32[]{:S(2)}) copy-start(f32[4,8,256]{2,1,0:T(8,128)} %param.10) | copy-start | bytes 98308
  1.4 6.5 %collective-permute-start = (s32[1,256]{1,0:T(1,128)S(1)}, s32[1,256]{1,0:T(1,128)S(1)}, u32[]{:S(2)}, u32[]{:S(2)}) collective-permute-start(s32[1,256]{1,0:T(1,128)S(1)} %slice.289), channel_id=1, source_target_pairs={{1,0},{4,1},{5,4},{8,5},{9,8},{12,9},{13,12},{3,2},{6,3},{7,6},{10... | collective-permute-start | bytes 3080 | tf_op jit(solution)/shard_map/ppermute | solution.py:26
  3.5 6.1 %collective-permute-start.1 = (f32[3,4,1,256]{3,1,2,0:T(4,128)S(1)}, f32[3,4,1,256]{3,1,2,0:T(4,128)S(1)}, u32[]{:S(2)}, u32[]{:S(2)}) collective-permute-start(f32[3,4,1,256]{3,1,2,0:T(4,128)S(1)} %get-tuple-element.62), channel_id=1, source_target_pairs={{0,1},{1,4},{4,5},{5,8},{8,9},{9,12},{12,13},{2,3},{3,6},{6,7},{7,... | collective-permute-start | bytes 36872 | tf_op jit(solution)/shard_map/ppermute | solution.py:17
  6.5 5.2 %collective-permute-start.2 = (f32[3,4,1,256]{3,1,2,0:T(4,128)S(1)}, f32[3,4,1,256]{3,1,2,0:T(4,128)S(1)}, u32[]{:S(2)}, u32[]{:S(2)}) collective-permute-start(f32[3,4,1,256]{3,1,2,0:T(4,128)S(1)} %get-tuple-element.63), channel_id=1, source_target_pairs={{1,0},{4,1},{5,4},{8,5},{9,8},{12,9},{13,12},{3,2},{6,3},{7,6},{10... | collective-permute-start | bytes 36872 | tf_op jit(solution)/shard_map/ppermute | solution.py:18
  12.5 11.4 %collective-permute-start.3 = (f32[3,4,1,256]{3,1,2,0:T(4,128)S(1)}, f32[3,4,1,256]{3,1,2,0:T(4,128)S(1)}, u32[]{:S(2)}, u32[]{:S(2)}) collective-permute-start(f32[3,4,1,256]{3,1,2,0:T(4,128)S(1)} %get-tuple-element.60), channel_id=1, source_target_pairs={{0,1},{1,4},{4,5},{5,8},{8,9},{9,12},{12,13},{2,3},{3,6},{6,7},{7,... | collective-permute-start | bytes 36872 | tf_op jit(solution)/shard_map/ppermute | solution.py:17
  16.8 7.1 %collective-permute-start.4 = (f32[3,4,1,256]{3,1,2,0:T(4,128)S(1)}, f32[3,4,1,256]{3,1,2,0:T(4,128)S(1)}, u32[]{:S(2)}, u32[]{:S(2)}) collective-permute-start(f32[3,4,1,256]{3,1,2,0:T(4,128)S(1)} %get-tuple-element.61), channel_id=1, source_target_pairs={{1,0},{4,1},{5,4},{8,5},{9,8},{12,9},{13,12},{3,2},{6,3},{7,6},{10... | collective-permute-start | bytes 36872 | tf_op jit(solution)/shard_map/ppermute | solution.py:18
  20.5 10.8 %copy-start.1 = (f32[24,8,8,128]{3,2,1,0:T(8,128)S(1)}, f32[24,8,8,128]{3,2,1,0:T(8,128)}, u32[]{:S(2)}) copy-start(f32[24,8,8,128]{3,2,1,0:T(8,128)} %param.11) | copy-start | bytes 2359300
  20.5 7.7 %all-to-all-start = ((f32[2,1,8192]{2,1,0:T(1,128)}), f32[2,1,8192]{2,1,0:T(1,128)S(1)}, u32[]{:S(2)}, u32[]{:S(2)}) async-start(f32[2,1,8192]{2,1,0:T(1,128)} %reshape.56), calls=%async_computation | async-start | bytes 131072 | tf_op jit(solution)/shard_map/all_to_all | solution.py:142
  31.4 3.4 %collective-permute-start.5 = (f32[26,8,1,128]{3,2,1,0:T(1,128)S(1)}, f32[26,8,1,128]{3,2,1,0:T(1,128)S(1)}, u32[]{:S(2)}, u32[]{:S(2)}) collective-permute-start(f32[26,8,1,128]{3,2,1,0:T(1,128)S(1)} %get-tuple-element.40), channel_id=1, source_target_pairs={{0,1},{1,4},{4,5},{5,8},{8,9},{9,12},{12,13},{2,3},{3,6},{6,7},{7,... | collective-permute-start | bytes 319496 | tf_op jit(solution)/shard_map/ppermute | solution.py:17
  33.4 5.2 %collective-permute-start.6 = (f32[26,8,1,128]{3,2,1,0:T(1,128)S(1)}, f32[26,8,1,128]{3,2,1,0:T(1,128)S(1)}, u32[]{:S(2)}, u32[]{:S(2)}) collective-permute-start(f32[26,8,1,128]{3,2,1,0:T(1,128)S(1)} %get-tuple-element.41), channel_id=1, source_target_pairs={{1,0},{4,1},{5,4},{8,5},{9,8},{12,9},{13,12},{3,2},{6,3},{7,6},{10... | collective-permute-start | bytes 319496 | tf_op jit(solution)/shard_map/ppermute | solution.py:18
  34.8 15.0 %copy-start.4 = (f32[4,10,258]{2,0,1:T(4,128)}, f32[4,10,258]{2,0,1:T(4,128)S(1)}, u32[]{:S(2)}) copy-start(f32[4,10,258]{2,0,1:T(4,128)S(1)} %get-tuple-element.43) | copy-start | bytes 123844
  43.9 9.1 %collective-permute-start.8 = (f32[26,8,10,1]{0,1,3,2:T(8,128)S(1)}, f32[26,8,10,1]{0,1,3,2:T(8,128)S(1)}, u32[]{:S(2)}, u32[]{:S(2)}) collective-permute-start(f32[26,8,10,1]{0,1,3,2:T(8,128)S(1)} %copy.147), channel_id=1, source_target_pairs={{2,0},{3,1},{6,4},{7,5},{10,8},{11,9},{14,12},{15,13},{18,16},{19,... | collective-permute-start | bytes 24968 | tf_op jit(solution)/shard_map/ppermute | solution.py:18
  45.2 6.2 %collective-permute-start.7 = (f32[26,8,10,1]{0,1,3,2:T(8,128)S(1)}, f32[26,8,10,1]{0,1,3,2:T(8,128)S(1)}, u32[]{:S(2)}, u32[]{:S(2)}) collective-permute-start(f32[26,8,10,1]{0,1,3,2:T(8,128)S(1)} %copy.146), channel_id=1, source_target_pairs={{0,2},{1,3},{4,6},{5,7},{8,10},{9,11},{12,14},{13,15},{16,18},{17,... | collective-permute-start | bytes 24968 | tf_op jit(solution)/shard_map/ppermute | solution.py:17
  59.1 8.5 %copy-start.5 = (f32[4,10,258]{2,0,1:T(4,128)S(1)}, f32[4,10,258]{2,0,1:T(4,128)}, u32[]{:S(2)}) copy-start(f32[4,10,258]{2,0,1:T(4,128)} %copy-done.4) | copy-start | bytes 123844
  59.1 9.3 %copy-start.9 = (f32[4,8,256]{2,0,1:T(4,128)S(1)}, f32[4,8,256]{2,0,1:T(4,128)}, u32[]{:S(2)}) copy-start(f32[4,8,256]{2,0,1:T(4,128)} %fusion.59) | copy-start | bytes 98308
  59.8 7.7 %all-to-all-start.1 = ((f32[8,8,128]{2,1,0:T(8,128)}), f32[8,8,128]{2,1,0:T(8,128)S(1)}, u32[]{:S(2)}, u32[]{:S(2)}) async-start(f32[8,8,128]{2,1,0:T(8,128)} %get-tuple-element.67), calls=%async_computation.1 | async-start | bytes 65536 | tf_op jit(solution)/shard_map/all_to_all | solution.py:150
  70.8 7.7 %all-to-all-start.2 = ((f32[2,1,8192]{2,1,0:T(1,128)}), f32[2,1,8192]{2,1,0:T(1,128)S(1)}, u32[]{:S(2)}, u32[]{:S(2)}) async-start(f32[2,1,8192]{2,1,0:T(1,128)} %reshape.58), calls=%async_computation.2 | async-start | bytes 131072 | tf_op jit(solution)/shard_map/all_to_all | solution.py:142
  81.1 3.3 %collective-permute-start.9 = (f32[26,8,1,128]{3,2,1,0:T(1,128)S(1)}, f32[26,8,1,128]{3,2,1,0:T(1,128)S(1)}, u32[]{:S(2)}, u32[]{:S(2)}) collective-permute-start(f32[26,8,1,128]{3,2,1,0:T(1,128)S(1)} %get-tuple-element.38), channel_id=1, source_target_pairs={{0,1},{1,4},{4,5},{5,8},{8,9},{9,12},{12,13},{2,3},{3,6},{6,7},{7,... | collective-permute-start | bytes 319496 | tf_op jit(solution)/shard_map/ppermute | solution.py:17
  83.2 5.5 %collective-permute-start.10 = (f32[26,8,1,128]{3,2,1,0:T(1,128)S(1)}, f32[26,8,1,128]{3,2,1,0:T(1,128)S(1)}, u32[]{:S(2)}, u32[]{:S(2)}) collective-permute-start(f32[26,8,1,128]{3,2,1,0:T(1,128)S(1)} %get-tuple-element.39), channel_id=1, source_target_pairs={{1,0},{4,1},{5,4},{8,5},{9,8},{12,9},{13,12},{3,2},{6,3},{7,6},{10... | collective-permute-start | bytes 319496 | tf_op jit(solution)/shard_map/ppermute | solution.py:18
  90.8 7.8 %copy-start.11 = (f32[4,8,256]{2,0,1:T(4,128)S(1)}, f32[4,8,256]{2,0,1:T(4,128)}, u32[]{:S(2)}) copy-start(f32[4,8,256]{2,0,1:T(4,128)} %get-tuple-element.56) | copy-start | bytes 98308
  93.0 6.3 %collective-permute-start.11 = (f32[26,8,10,1]{0,1,3,2:T(8,128)S(1)}, f32[26,8,10,1]{0,1,3,2:T(8,128)S(1)}, u32[]{:S(2)}, u32[]{:S(2)}) collective-permute-start(f32[26,8,10,1]{0,1,3,2:T(8,128)S(1)} %copy.157), channel_id=1, source_target_pairs={{0,2},{1,3},{4,6},{5,7},{8,10},{9,11},{12,14},{13,15},{16,18},{17,... | collective-permute-start | bytes 24968 | tf_op jit(solution)/shard_map/ppermute | solution.py:17
  95.9 5.9 %collective-permute-start.12 = (f32[26,8,10,1]{0,1,3,2:T(8,128)S(1)}, f32[26,8,10,1]{0,1,3,2:T(8,128)S(1)}, u32[]{:S(2)}, u32[]{:S(2)}) collective-permute-start(f32[26,8,10,1]{0,1,3,2:T(8,128)S(1)} %copy.158), channel_id=1, source_target_pairs={{2,0},{3,1},{6,4},{7,5},{10,8},{11,9},{14,12},{15,13},{18,16},{19,... | collective-permute-start | bytes 24968 | tf_op jit(solution)/shard_map/ppermute | solution.py:18
  109.7 7.2 %all-to-all-start.3 = ((f32[8,8,128]{2,1,0:T(8,128)}), f32[8,8,128]{2,1,0:T(8,128)S(1)}, u32[]{:S(2)}, u32[]{:S(2)}) async-start(f32[8,8,128]{2,1,0:T(8,128)} %get-tuple-element.65), calls=%async_computation.3 | async-start | bytes 65536 | tf_op jit(solution)/shard_map/all_to_all | solution.py:150
  (6 other events, 27.7 us)
where the time goes:
time: 120 us; the launch traced here: 118 us
  starting transfers between devices  40.7 us (34%)
  local copies, waits for them, and re-layouts  30.7 us (26%)
  waiting for transfers between devices  25.1 us (21%)
  other arithmetic  17.3 us (14%)
  matrix products  2.5 us (2%)
  between operations  1.25 us (1%)
    ppermute x6, starting transfers between devices, padded(): before = lax.ppermute(last, axis, up)  17.9 us
    ppermute x6, waiting for transfers between devices, padded(): after = lax.ppermute(leading, axis, down)  11.1 us
    unnamed x33, local copies, waits for them, and re-layouts  8.39 us
    slice x5, local copies, waits for them, and re-layouts, padded(): last = lax.slice_in_dim(shard, length - width, length, axis=dim)  8.04 us
    ppermute x6, starting transfers between devices, padded(): after = lax.ppermute(leading, axis, down)  7.96 us
    all_to_all x2, waiting for transfers between devices, shards(): lax.all_to_all(jnp.stack([eastward_current, poleward_current]), 'lon', sp...  7.52 us
    all_to_all x2, starting transfers between devices, shards(): lax.all_to_all(heat_tile, 'lon', split_axis=0, concat_axis=2, tiled=True)  6.85 us
    all_to_all x2, starting transfers between devices, shards(): lax.all_to_all(jnp.stack([eastward_current, poleward_current]), 'lon', sp...  6.73 us
  transfers between devices with their start and end apart: 17, of which 9 were waited for; matrix products, arithmetic and copies ran while one was open for 13% of the time, Pallas kernels for 0%

commit v1 on v0

v1 whole, which is shorter than its diff:
```python
import functools

import jax
import jax.numpy as jnp
from jax import lax
from jax.experimental import pallas as pl
from jax.experimental.pallas import tpu as pltpu
from jax.sharding import PartitionSpec as P

STEPS = 2
ROWS = 8
LANES = 128
LEVELS = 8
CORES = 2

FIELDS = 4
DYN = FIELDS * LEVELS
CHL = DYN
SUM = CHL + LEVELS
EDGE = SUM + LEVELS
X_TILES = EDGE + LEVELS
DYN2 = DYN // 2
MIX2 = DYN2 + LEVELS
XZ_TILES = MIX2 + 1


def iota(shape, dim):
    return lax.broadcasted_iota(jnp.int32, shape, dim)


def roll(q, shift, axis):
    return pltpu.roll(q, shift % q.shape[axis], axis)


def pack_kernel(n, pos, rates, u, v, t, h, count, c, x_out, z_out, r_out, xz_out):
    tracers = c.shape[0]
    share = u.shape[0]
    upper = pos[2] == 1
    sub = iota((ROWS, LANES), 0)
    lane = iota((ROWS, LANES), 1)
    to_z = (sub >= ROWS // 2) == upper

    def halves(a, b):
        moved = roll(b, ROWS // 2, 0)
        return jnp.where(to_z, a, moved), jnp.where(to_z, moved, a)

    fields = (u, v, t, h)
    for level in range(share):
        for block in range(n):
            cols = slice(block * LANES, (block + 1) * LANES)
            tiles = [f[level, :, cols] for f in fields]
            place = level * n + block
            for f in range(FIELDS):
                x_out[f * LEVELS + place] = tiles[f]
            for pair in range(2):
                forth, across = halves(tiles[2 * pair], tiles[2 * pair + 1])
                z_out[pair * LEVELS + place] = forth
                xz_out[pair * LEVELS + place] = forth
                r_out[pair * LEVELS + place] = across
    for block in range(n):
        depth = count[:, block * LANES : (block + 1) * LANES].astype(jnp.float32)
        z_out[DYN2 + block] = depth
        r_out[DYN2 + block] = depth

    def one_level(k, carry):
        total = jnp.zeros((ROWS, LANES), jnp.float32)
        edge = jnp.zeros((ROWS, LANES), jnp.float32)
        for b in range(tracers):
            q = c[b, k]
            total = total + rates[0, b] * q
            edge = jnp.where(lane // 4 == b, roll(q, 4 * b + 2, 1), edge)
        x_out[CHL + k] = c[0, k]
        x_out[SUM + k] = total
        x_out[EDGE + k] = edge
        forth, _ = halves(c[0, k], total)
        xz_out[DYN2 + k] = forth
        return carry

    lax.fori_loop(0, LEVELS, one_level, 0)
    edges = [x_out[EDGE : EDGE + LEVELS, row, :] for row in (0, ROWS - 1)]
    xz_out[MIX2] = jnp.where(upper, edges[1], edges[0])
    base = DYN2 + n
    for b in range(tracers + 1):
        for far in range(2):
            low, high = far, ROWS - 1 - far
            if b < tracers:
                bottom, top = c[b, :, low, :], c[b, :, high, :]
            else:
                bottom, top = x_out[SUM : SUM + LEVELS, low, :], x_out[SUM : SUM + LEVELS, high, :]
            z_out[base + 2 * b + far] = jnp.where(upper, top, bottom)
            r_out[base + 2 * b + far] = jnp.where(upper, bottom, top)


def split(q):
    high = q.astype(jnp.bfloat16)
    return high, (q - high.astype(jnp.float32)).astype(jnp.bfloat16)


def spread_kernel(rates, m_high, m_low, e_high, e_low):
    tracers = rates.shape[0]
    exact = functools.partial(jnp.dot, precision=lax.Precision.HIGHEST, preferred_element_type=jnp.float32)
    for group, transposed, high, low in ((ROWS, False, m_high, m_low), (4, True, e_high, e_low)):
        size = high.shape[0]
        rows = (iota((size, tracers), 0) // group == iota((size, tracers), 1)).astype(jnp.float32)
        cols = (iota((tracers, size), 1) // group == iota((tracers, size), 0)).astype(jnp.float32)
        wide = exact(exact(rows, rates[...].T if transposed else rates[...]), cols)
        same = iota((size, size), 0) % group == iota((size, size), 1) % group
        high[...], low[...] = split(jnp.where(same, wide, 0.0))


def exact_product(left, right):
    dot = functools.partial(jnp.dot, preferred_element_type=jnp.float32)
    return dot(left[0], right[0]) + (dot(left[0], right[1]) + dot(left[1], right[0]))


def step_kernel(n, strips, *refs):
    pos, u, v, t, h, count, c, own, m_high, m_low, e_high, e_low, z, r = refs[:14]
    others = n - 1
    xs, r2s, xzs = (refs[14 + i * others : 14 + (i + 1) * others] for i in range(3))
    u_out, v_out, t_out, h_out, c_out = refs[14 + 3 * others : 19 + 3 * others]
    dyn, mix, depth, coef, row0, row1, edge0, corner, edge1, adv, mid, out4 = refs[19 + 3 * others :]
    tracers = c.shape[0]
    share = u.shape[0]
    width = n * LANES
    strip, lon, role = pos[0], pos[1], pos[2]
    upper = role == 1
    base = DYN2 + n

    sub = iota((ROWS, LANES), 0)
    lane = iota((ROWS, LANES), 1)
    from_r = (sub >= ROWS // 2) == upper
    no_south, no_north = strip == 0, strip == strips - 1
    lost = jnp.logical_or(no_south, no_north)
    lost_z = jnp.logical_or(
        jnp.logical_and(no_south, jnp.logical_not(upper)), jnp.logical_and(no_north, upper)
    )
    keep_z = jnp.where(lost_z, 0.0, 1.0)
    del lost

    def halo(near, far):
        return jnp.where(from_r, near, jnp.where(lost_z, 0.0, far))

    def block_of(m):
        return pl.ds(pl.multiple_of(m * LANES, LANES), LANES)

    fields = (u, v, t, h)
    for level in range(share):
        for block in range(n):
            cols = slice(block * LANES, (block + 1) * LANES)
            place = level * n + block
            for pair in range(2):
                near, far = r[pair * LEVELS + place], z[pair * LEVELS + place]
                for second in range(2):
                    f = 2 * pair + second
                    if second:
                        near, far = roll(near, ROWS // 2, 0), roll(far, ROWS // 2, 0)
                    dyn[f, lon * share + level, :ROWS, cols] = fields[f][level, :, cols]
                    dyn[f, lon * share + level, ROWS:, cols] = halo(near, far)
    for block in range(n):
        cols = slice(block * LANES, (block + 1) * LANES)
        depth[:ROWS, cols] = count[:, cols].astype(jnp.float32)
        depth[ROWS:, cols] = halo(r[DYN2 + block], z[DYN2 + block])

    def near_rows(b, far):
        a, d = r[base + 2 * b + far], z[base + 2 * b + far] * keep_z
        return jnp.where(upper, a, d), jnp.where(upper, d, a)

    here = block_of(lon)
    mix[0, :, :ROWS, here] = c[0]
    mix[1, :, :ROWS, here] = own[SUM : SUM + LEVELS]
    for i, b in enumerate((0, tracers)):
        for far in range(2):
            south, north = near_rows(b, far)
            mix[i, :, ROWS + far, here] = north
            mix[i, :, 2 * ROWS - 1 - far, here] = south

    for s, (x, r2, xz) in enumerate(zip(xs, r2s, xzs)):
        m = lax.rem(lon + (n - 1 - s), n)
        there = block_of(m)
        for level in range(share):
            for block in range(n):
                cols = slice(block * LANES, (block + 1) * LANES)
                place = level * n + block
                for pair in range(2):
                    far = xz[pair * LEVELS + place]
                    for second in range(2):
                        f = 2 * pair + second
                        if second:
                            far = roll(far, ROWS // 2, 0)
                        dyn[f, m * share + level, :ROWS, cols] = x[f * LEVELS + place]
                        dyn[f, m * share + level, ROWS:, cols] = halo(r2[f * LEVELS + place], far)
        for k in range(LEVELS):
            far = xz[DYN2 + k]
            mix[0, k, :ROWS, there] = x[CHL + k]
            mix[1, k, :ROWS, there] = x[SUM + k]
            mix[0, k, ROWS:, there] = halo(r2[CHL + k], far)
            mix[1, k, ROWS:, there] = halo(r2[SUM + k], roll(far, ROWS // 2, 0))
        edge0[m] = x[EDGE : EDGE + LEVELS]
        a, d = xz[MIX2] * keep_z, [r2[EDGE : EDGE + LEVELS, row, :] for row in (0, ROWS - 1)]
        corner[m, 0] = jnp.where(upper, d[1], a)
        corner[m, 1] = jnp.where(upper, a, d[0])

    wide = (2 * ROWS, width)
    col = iota(wide, 1)
    ring = iota(wide, 0)
    row = strip * ROWS + jnp.where(ring < ROWS + ROWS // 2, ring, ring - 2 * ROWS)
    fcor = 2.0 * (row.astype(jnp.float32) + 0.5) / (strips * ROWS) - 1.0
    not_last = col < width - 1
    not_first = col > 0

    def east(q):
        return jnp.where(not_last, roll(q, -1, 1), 0.0)

    def west(q):
        return jnp.where(not_first, roll(q, 1, 1), 0.0)

    def north(q):
        return roll(q, -1, 0)

    def south(q):
        return roll(q, 1, 0)

    def lap(q, e, nn):
        return e + west(q) + nn + south(q) - 4.0 * q

    def one_level(k, carry):
        uu, vv, tt, heat = dyn[0, k], dyn[1, k], dyn[2, k], dyn[3, k]
        chl, total = mix[0, k], mix[1, k]
        wet = (depth[...] > k.astype(jnp.float32)).astype(jnp.float32)
        wet_u, wet_v = wet * east(wet), wet * north(wet)
        new = []
        for step in range(STEPS):
            tau, top = carry[2 * step], carry[2 * step + 1]
            te, tn = east(tt), north(tt)
            u_new = wet_u * (
                uu + 0.1 * lap(uu, east(uu), north(uu)) + 0.3 * fcor * vv - 0.2 * (te - tt)
            )
            v_new = wet_v * (
                vv + 0.1 * lap(vv, east(vv), north(vv)) - 0.3 * fcor * uu - 0.2 * (tn - tt)
            )
            tt = wet * (tt + 0.1 * lap(tt, te, tn) + 0.5 * heat)
            uu, vv = u_new, v_new
            uw, vs = west(uu), south(vv)
            a0 = 1.0 - 0.5 * (
                (jnp.maximum(uu, 0.0) - jnp.minimum(uw, 0.0)) + (jnp.maximum(vv, 0.0) - jnp.minimum(vs, 0.0))
            )
            ae, aw = -0.5 * jnp.minimum(uu, 0.0), 0.5 * jnp.maximum(uw, 0.0)
            an, a_s = -0.5 * jnp.minimum(vv, 0.0), 0.5 * jnp.maximum(vs, 0.0)

            def advect(q):
                return a0 * q + (ae * east(q) + aw * west(q)) + (an * north(q) + a_s * south(q))

            moved = advect(chl)
            tau = tau + (0.1 + 0.3 * jnp.maximum(moved, 0.0))
            below = jnp.exp(-tau)
            heat = 2.0 * wet * (top - below)
            share_of_light = 0.5 * wet * top
            for i, q in enumerate((a0, ae, aw, an, a_s, wet, share_of_light)):
                coef[step, i, k] = q
            if step + 1 < STEPS:
                chl = wet * moved + share_of_light * advect(total)
            new += [tau, below]
        out4[0, k], out4[1, k], out4[2, k], out4[3, k] = uu[:ROWS], vv[:ROWS], tt[:ROWS], heat[:ROWS]
        return tuple(new)

    zero, one = jnp.zeros(wide, jnp.float32), jnp.ones(wide, jnp.float32)
    lax.fori_loop(0, LEVELS, one_level, (zero, one) * STEPS)
    mine = pl.ds(lon * share, share)
    for i, ref in enumerate((u_out, v_out, t_out, h_out)):
        ref[...] = out4[i, mine]

    kind = lane % 4
    lon_e, lon_w = jnp.minimum(lon + 1, n - 1), jnp.maximum(lon - 1, 0)
    to_east = jnp.where(lon < n - 1, 1.0, 0.0)
    to_west = jnp.where(lon > 0, 1.0, 0.0)
    exists = jnp.where(kind >= 2, to_east, to_west)
    easterly = kind >= 2

    def swapped(q):
        return jnp.where(kind == 1, roll(q, -1, 1), roll(q, 1, 1))

    def beside(edge, q, b):
        cols = roll(edge, LANES - 2 - 4 * b, 1)
        return (
            jnp.where(lane == LANES - 1, cols, roll(q, -1, 1)),
            jnp.where(lane == 0, cols, roll(q, 1, 1)),
        )

    def tile_coef(step, i, k):
        return coef[step, i, k, :ROWS, here]

    corners = []
    for side in range(2):
        q = jnp.where(easterly, corner[lon_e, side], corner[lon_w, side]) * exists
        corners.append(q)
    east_block, west_block = block_of(lon_e), block_of(lon_w)
    ends = []
    ends_raw = []
    for k in range(LEVELS):
        q = jnp.where(easterly, edge0[lon_e, k], edge0[lon_w, k]) * exists
        ends_raw.append(q)
        mid[0, k] = swapped(q)
    row_n, row_s = corners[1], corners[0]
    edge1[1, :, ROWS - 1, :] = row_n
    edge1[1, :, 0, :] = row_s
    for k in range(LEVELS):
        q = ends_raw[k]
        mine_edge = own[EDGE + k]
        outer = jnp.where(easterly, roll(q, -1, 1), roll(q, 1, 1))
        inner = jnp.where(easterly, roll(mine_edge, 1, 1), roll(mine_edge, -1, 1))
        rim = edge1[1, k]
        up = jnp.where(sub == ROWS - 1, rim, roll(q, -1, 0))
        down = jnp.where(sub == 0, rim, roll(q, 1, 0))

        def at_edge(i):
            e = jnp.broadcast_to(coef[0, i, k, :ROWS, east_block][:, :1], (ROWS, LANES))
            w = jnp.broadcast_to(coef[0, i, k, :ROWS, west_block][:, LANES - 1 :], (ROWS, LANES))
            return e, w

        a0, ae, aw, an, a_s, wet, light = (at_edge(i) for i in range(7))

        def pick(pair):
            return jnp.where(easterly, pair[0], pair[1])

        out_c = jnp.where(easterly, ae[0], aw[1])
        in_c = jnp.where(easterly, aw[0], ae[1])
        ends.append(
            (pick(a0) * q + (out_c * outer + in_c * inner) + (pick(an) * up + pick(a_s) * down), pick(wet), pick(light))
        )
    moved = jnp.concatenate([e[0] for e in ends], axis=0)
    react = exact_product(split(moved), (e_high[...], e_low[...]))
    for k in range(LEVELS):
        q, wet, light = ends[k]
        mid[1, k] = swapped((wet * q + light * react[k * ROWS : (k + 1) * ROWS]) * exists)

    m_pair = (m_high[...], m_low[...])
    for side, (at, ring_row) in enumerate(((0, 2 * ROWS - 1), (ROWS - 1, ROWS))):
        a0, ae, aw, an, a_s, wet, light = (coef[0, i, :, ring_row, here] for i in range(7))
        rim = swapped(corners[side])
        for b in range(tracers):
            q, q2 = near_rows(b, 0)[side], near_rows(b, 1)[side]
            row0[b, :, at, :] = q
            inner = c[b, :, at, :]
            e, w = beside(rim, q, b)
            up, down = (inner, q2) if side == 0 else (q2, inner)
            adv[b * ROWS : (b + 1) * ROWS, side * LANES : (side + 1) * LANES] = (
                a0 * q + (ae * e + aw * w) + (an * up + a_s * down)
            )
    react = exact_product(m_pair, split(adv[...]))
    for side, (at, ring_row) in enumerate(((0, 2 * ROWS - 1), (ROWS - 1, ROWS))):
        wet, light = (coef[0, i, :, ring_row, here] for i in (5, 6))
        for b in range(tracers):
            part = (slice(b * ROWS, (b + 1) * ROWS), slice(side * LANES, (side + 1) * LANES))
            row1[b, :, at, :] = wet * adv[part] + light * react[part]

    for step, (source, rows_ref, target) in enumerate(((c, row0, c_out), (c_out, row1, c_out))):

        def two_levels(i, carry, step=step, source=source, rows_ref=rows_ref, target=target):
            for half in range(2):
                k = 2 * i + half
                a0, ae, aw, an, a_s = (tile_coef(step, j, k) for j in range(5))
                edge = mid[step, k]
                for b in range(tracers):
                    q, rim = source[b, k], rows_ref[b, k]
                    e, w = beside(edge, q, b)
                    up = jnp.where(sub == ROWS - 1, rim, roll(q, -1, 0))
                    down = jnp.where(sub == 0, rim, roll(q, 1, 0))
                    adv[b * ROWS : (b + 1) * ROWS, half * LANES : (half + 1) * LANES] = (
                        a0 * q + (ae * e + aw * w) + (an * up + a_s * down)
                    )
            react = exact_product(m_pair, split(adv[...]))
            for half in range(2):
                k = 2 * i + half
                wet, light = tile_coef(step, 5, k), tile_coef(step, 6, k)
                for b in range(tracers):
                    part = (slice(b * ROWS, (b + 1) * ROWS), slice(half * LANES, (half + 1) * LANES))
                    target[b, k] = wet * adv[part] + light * react[part]
            return carry

        lax.fori_loop(0, LEVELS // 2, two_levels, 0)


def shards(n, lats, u, v, t, h, c, count, rates):
    tracers = c.shape[0]
    share, width = u.shape[0], u.shape[2]
    strips = lats * CORES
    lat, lon, role = lax.axis_index("lat"), lax.axis_index("lon"), lax.axis_index("role")
    pos = jnp.stack([lat * CORES + role, lon, role]).astype(jnp.int32)
    vmem = pl.BlockSpec(memory_space=pltpu.VMEM)
    smem = pl.BlockSpec(memory_space=pltpu.SMEM)
    params = pltpu.CompilerParams(vmem_limit_bytes=48 * 1024 * 1024)
    f32 = jnp.float32

    def tiles(count):
        return jax.ShapeDtypeStruct((count, ROWS, LANES), f32)

    z_tiles = DYN2 + n + 2 * (tracers + 1)
    x_pay, z_pay, r_pay, xz_pay = pl.pallas_call(
        functools.partial(pack_kernel, n),
        out_shape=(tiles(X_TILES), tiles(z_tiles), tiles(z_tiles), tiles(XZ_TILES)),
        in_specs=[smem, smem] + [vmem] * 6,
        out_specs=(vmem,) * 4,
        compiler_params=params,
        name="pack",
    )(pos, rates, u, v, t, h, count, c)

    def permute(q, target):
        pairs = []
        for a in range(lats):
            for o in range(n):
                for i in range(CORES):
                    a2, o2, i2 = target(a, o, i)
                    pairs.append(((a * n + o) * CORES + i, (a2 * n + o2) * CORES + i2))
        return lax.ppermute(q, ("lat", "lon", "role"), pairs)

    def over_lat(a, i):
        s = a * CORES + i + (1 if i else -1)
        return (s // CORES, s % CORES) if 0 <= s < strips else None

    def z_target(a, o, i):
        to = over_lat(a, i)
        return (to[0], o, to[1]) if to else (a, o ^ 1 if o ^ 1 < n else o, i)

    def shifted(shift):
        def x_target(a, o, i):
            return a, (o + shift) % n, i

        def xz_target(a, o, i):
            to = over_lat(a, i) or (a, i)
            return to[0], (o + shift) % n, to[1]

        return x_target, xz_target

    def across(a, o, i):
        return a, o, 1 - i

    z_in = permute(z_pay, z_target)
    xs, xzs = [], []
    for shift in range(1, n):
        x_target, xz_target = shifted(shift)
        xs.append(permute(x_pay, x_target))
        xzs.append(permute(xz_pay, xz_target))
    r_in = permute(r_pay, across)
    r2s = [permute(x, across) for x in xs]

    m_size, e_size = tracers * ROWS, LANES
    spread = pl.pallas_call(
        spread_kernel,
        out_shape=tuple(jax.ShapeDtypeStruct((s, s), jnp.bfloat16) for s in (m_size, m_size, e_size, e_size)),
        in_specs=[vmem],
        out_specs=(vmem,) * 4,
        compiler_params=params,
        name="spread",
    )(rates)

    whole = jax.ShapeDtypeStruct(u.shape, f32)
    args = (pos, u, v, t, h, count, c, x_pay, *spread, z_in, r_in, *xs, *r2s, *xzs)
    u, v, t, h, c = pl.pallas_call(
        functools.partial(step_kernel, n, strips),
        out_shape=(whole,) * 4 + (jax.ShapeDtypeStruct(c.shape, f32),),
        in_specs=[smem] + [vmem] * (len(args) - 1),
        out_specs=(vmem,) * 5,
        scratch_shapes=[
            pltpu.VMEM((FIELDS, LEVELS, 2 * ROWS, width), f32),
            pltpu.VMEM((2, LEVELS, 2 * ROWS, width), f32),
            pltpu.VMEM((2 * ROWS, width), f32),
            pltpu.VMEM((STEPS, 7, LEVELS, 2 * ROWS, width), f32),
            pltpu.VMEM((tracers, LEVELS, ROWS, LANES), f32),
            pltpu.VMEM((tracers, LEVELS, ROWS, LANES), f32),
            pltpu.VMEM((n, LEVELS, ROWS, LANES), f32),
            pltpu.VMEM((n, 2, LEVELS, LANES), f32),
            pltpu.VMEM((2, LEVELS, ROWS, LANES), f32),
            pltpu.VMEM((tracers * ROWS, 2 * LANES), f32),
            pltpu.VMEM((2, LEVELS, ROWS, LANES), f32),
            pltpu.VMEM((FIELDS, LEVELS, ROWS, width), f32),
        ],
        compiler_params=params,
        name="steps",
    )(*args)
    return u, v, t, h, c


def solution(mesh):
    level = P("lon", ("grp", "lat", "role"), None)
    tracer = P(None, None, ("grp", "lat", "role"), "lon")
    return jax.shard_map(
        functools.partial(shards, mesh.shape["lon"], mesh.shape["lat"]),
        mesh=mesh,
        in_specs=(level, level, level, level, tracer, P(("grp", "lat", "role"), None), P()),
        out_specs=(level, level, level, level, tracer),
        check_vma=False,
    )
```

time: 120 us -> 29.9 us (0.25)
  the two profiles are of different devices: /device:TPU:0 before, /device:TPU:31 now
where the time goes in v1:
time: 29.9 us; the launch traced here: 29.4 us
  Pallas kernels  10.6 us (35%)
  waiting for transfers between devices  8.73 us (29%)
  local copies, waits for them, and re-layouts  4.8 us (16%)
  starting transfers between devices  4.48 us (15%)
  between operations  0.73 us (2%)
    ppermute x5, waiting for transfers between devices, permute(): return lax.ppermute(q, ('lat', 'lon', 'role'), pairs)  8.73 us
    pallas_call x1, Pallas kernels, shards(): pl.pallas_call(functools.partial(step_kernel, n, strips), out_shape=(whol...  8.1 us
    unnamed x24, local copies, waits for them, and re-layouts  4.8 us
    ppermute x5, starting transfers between devices, permute(): return lax.ppermute(q, ('lat', 'lon', 'role'), pairs)  4.48 us
    pallas_call x1, Pallas kernels, shards(): pl.pallas_call(functools.partial(pack_kernel, n), out_shape=(tiles(X_TILE...  1.81 us
    pallas_call x1, Pallas kernels, shards(): pl.pallas_call(spread_kernel, out_shape=tuple((jax.ShapeDtypeStruct((s, s...  0.66 us
  transfers between devices with their start and end apart: 5, of which 2 were waited for; matrix products, arithmetic and copies ran while one was open for 0% of the time, Pallas kernels for 2%

profile of v1, /device:TPU:31, one launch (start us, length us, event | category | flops | bytes accessed | tf_op | source)
XLA Modules:
  0.0 29.4 jit_solution(3744614303694050471)
XLA Ops:
  0.6 0.0 copy-start.10
  0.6 0.0 copy-start.11
  0.7 0.1 pad_add_fusion.pos.refs_0_
  0.7 0.6 %copy-done.10 = f32[24,24]{1,0:T(8,128)S(1)} copy-done((f32[24,24]{1,0:T(8,128)S(1)}, f32[24,24]{1,0:T(8,128)}, u32[]{:S(2)}) %copy-start.10) | copy-done | bytes 2328
  1.3 0.0 copy-done.11
  1.4 1.1 %copy-done = f32[24,8,8,128]{3,2,1,0:T(8,128)S(1)} copy-done((f32[24,8,8,128]{3,2,1,0:T(8,128)S(1)}, f32[24,8,8,128]{3,2,1,0:T(8,128)}, u32[]{:S(2)}) %copy-start) | copy-done | bytes 786456
  2.5 0.8 %copy-done.2 = f32[4,8,256]{2,1,0:T(8,128)S(1)} copy-done((f32[4,8,256]{2,1,0:T(8,128)S(1)}, f32[4,8,256]{2,1,0:T(8,128)}, u32[]{:S(2)}) %copy-start.2) | copy-done | bytes 32792
  3.2 0.8 %copy-done.4 = f32[4,8,256]{2,1,0:T(8,128)S(1)} copy-done((f32[4,8,256]{2,1,0:T(8,128)S(1)}, f32[4,8,256]{2,1,0:T(8,128)}, u32[]{:S(2)}) %copy-start.4) | copy-done | bytes 32792
  4.0 0.8 %copy-done.6 = f32[4,8,256]{2,1,0:T(8,128)S(1)} copy-done((f32[4,8,256]{2,1,0:T(8,128)S(1)}, f32[4,8,256]{2,1,0:T(8,128)}, u32[]{:S(2)}) %copy-start.6) | copy-done | bytes 32792
  4.8 0.8 %copy-done.8 = f32[4,8,256]{2,1,0:T(8,128)S(1)} copy-done((f32[4,8,256]{2,1,0:T(8,128)S(1)}, f32[4,8,256]{2,1,0:T(8,128)}, u32[]{:S(2)}) %copy-start.8) | copy-done | bytes 32792
  5.5 0.0 copy-start.9
  5.5 1.8 %pack.1 = (f32[56,8,128]{2,1,0:T(8,128)S(1)}, f32[68,8,128]{2,1,0:T(8,128)S(1)}, f32[68,8,128]{2,1,0:T(8,128)S(1)}, f32[25,8,128]{2,1,0:T(8,128)S(1)}) custom-call(s32[3]{0:T(128)S(1)} %pad_add_fusion.pos.refs_0_, f32[24,24]{1,0:T(8,128)S(1)} %copy-done.10, f32[4,8,256]{2,1,0:T(8,128)S(1)} %copy-done.2, f32[4,8,256]{2,1,0:T(8,128)S(1)} %copy-done.4, ...), custom_call_target="tpu_custom_call" | custom-call | tf_op jit(solution)/shard_map/pack/pallas_call | solution.py:398
  7.4 0.3 %collective-permute-start.2 = (f32[56,8,128]{2,1,0:T(8,128)S(1)}, f32[56,8,128]{2,1,0:T(8,128)S(1)}, u32[]{:S(2)}, u32[]{:S(2)}) collective-permute-start(f32[56,8,128]{2,1,0:T(8,128)S(1)} %get-tuple-element.13.refs_7_), channel_id=1, source_target_pairs={{0,2},{1,3},{2,0},{3,1},{4,6},{5,7},{6,4},{7,5},{8,10},{9,11},{10,... | collective-permute-start | bytes 688136 | tf_op jit(solution)/shard_map/ppermute | solution.py:414
  7.7 1.2 %collective-permute-start = (f32[68,8,128]{2,1,0:T(8,128)S(1)}, f32[68,8,128]{2,1,0:T(8,128)S(1)}, u32[]{:S(2)}, u32[]{:S(2)}) collective-permute-start(f32[68,8,128]{2,1,0:T(8,128)S(1)} %get-tuple-element.18), channel_id=1, source_target_pairs={{0,2},{1,4},{2,0},{3,6},{4,1},{5,8},{6,3},{7,10},{8,5},{9,12},{10,... | collective-permute-start | bytes 835592 | tf_op jit(solution)/shard_map/ppermute | solution.py:414
  8.9 0.0 collective-permute-start.1
  8.9 5.0 %collective-permute-done.2.refs_14_ = f32[56,8,128]{2,1,0:T(8,128)S(1)} collective-permute-done((f32[56,8,128]{2,1,0:T(8,128)S(1)}, f32[56,8,128]{2,1,0:T(8,128)S(1)}, u32[]{:S(2)}, u32[]{:S(2)}) %collective-permute-start.2) | collective-permute-done | bytes 229408 | tf_op jit(solution)/shard_map/ppermute | solution.py:414
  13.9 2.7 %collective-permute-start.3 = (f32[56,8,128]{2,1,0:T(8,128)S(1)}, f32[56,8,128]{2,1,0:T(8,128)S(1)}, u32[]{:S(2)}, u32[]{:S(2)}) collective-permute-start(f32[56,8,128]{2,1,0:T(8,128)S(1)} %collective-permute-done.2.refs_14_), channel_id=1, source_target_pairs={{0,1},{1,0},{2,3},{3,2},{4,5},{5,4},{6,7},{7,6},{8,9},{9,8},{10,11... | collective-permute-start | bytes 688136 | tf_op jit(solution)/shard_map/ppermute | solution.py:414
  16.6 0.3 collective-permute-start.4
  16.8 0.7 %spread.1 = (bf16[192,192]{1,0:T(8,128)(2,1)S(1)}, bf16[192,192]{1,0:T(8,128)(2,1)S(1)}, bf16[128,128]{1,0:T(8,128)(2,1)S(1)}, bf16[128,128]{1,0:T(8,128)(2,1)S(1)}) custom-call(f32[24,24]{1,0:T(8,128)S(1)} %copy-done.10), custom_call_target="tpu_custom_call" | custom-call | tf_op jit(solution)/shard_map/spread/pallas_call | solution.py:447
  17.5 3.7 %collective-permute-done.4.refs_16_ = f32[25,8,128]{2,1,0:T(8,128)S(1)} collective-permute-done((f32[25,8,128]{2,1,0:T(8,128)S(1)}, f32[25,8,128]{2,1,0:T(8,128)S(1)}, u32[]{:S(2)}, u32[]{:S(2)}) %collective-permute-start.4) | collective-permute-done | bytes 102432 | tf_op jit(solution)/shard_map/ppermute | solution.py:414
  21.2 0.0 collective-permute-done.refs_12_
  21.2 0.0 collective-permute-done.1.refs_13_
  21.2 0.0 collective-permute-done.3.refs_15_
  21.3 8.1 %steps.1 = (f32[4,8,256]{2,1,0:T(8,128)}, f32[4,8,256]{2,1,0:T(8,128)}, f32[4,8,256]{2,1,0:T(8,128)}, f32[4,8,256]{2,1,0:T(8,128)}, f32[24,8,8,128]{3,2,1,0:T(8,128)}) custom-call(s32[3]{0:T(128)S(1)} %pad_add_fusion.pos.refs_0_, f32[4,8,256]{2,1,0:T(8,128)S(1)} %copy-done.3, f32[4,8,256]{2,1,0:T(8,128)S(1)} %copy-done.5, f32[4,8,256]{2,1,0:T(8,128)S(1)} %copy-done.7, ...), custom_call_target="tpu_custom_call" | custom-call | tf_op jit(solution)/shard_map/steps/pallas_call | solution.py:458
  (14 shorter events, 0.0 us)
Async XLA Ops:
  0.6 0.7 %copy-start.10 = (f32[24,24]{1,0:T(8,128)S(1)}, f32[24,24]{1,0:T(8,128)}, u32[]{:S(2)}) copy-start(f32[24,24]{1,0:T(8,128)} %rates.3) | copy-start | bytes 6916
  0.6 0.7 %copy-start.11 = (s32[8,256]{1,0:T(8,128)S(1)}, s32[8,256]{1,0:T(8,128)}, u32[]{:S(2)}) copy-start(s32[8,256]{1,0:T(8,128)} %refs_5_.1) | copy-start | bytes 24580
  1.3 1.1 %copy-start = (f32[24,8,8,128]{3,2,1,0:T(8,128)S(1)}, f32[24,8,8,128]{3,2,1,0:T(8,128)}, u32[]{:S(2)}) copy-start(f32[24,8,8,128]{3,2,1,0:T(8,128)} %refs_6_.1) | copy-start | bytes 2359300
  2.5 0.8 %copy-start.2 = (f32[4,8,256]{2,1,0:T(8,128)S(1)}, f32[4,8,256]{2,1,0:T(8,128)}, u32[]{:S(2)}) copy-start(f32[4,8,256]{2,1,0:T(8,128)} %refs_1_.1) | copy-start | bytes 98308
  3.2 0.8 %copy-start.4 = (f32[4,8,256]{2,1,0:T(8,128)S(1)}, f32[4,8,256]{2,1,0:T(8,128)}, u32[]{:S(2)}) copy-start(f32[4,8,256]{2,1,0:T(8,128)} %refs_2_.1) | copy-start | bytes 98308
  4.0 0.8 %copy-start.6 = (f32[4,8,256]{2,1,0:T(8,128)S(1)}, f32[4,8,256]{2,1,0:T(8,128)}, u32[]{:S(2)}) copy-start(f32[4,8,256]{2,1,0:T(8,128)} %refs_3_.1) | copy-start | bytes 98308
  4.8 0.8 %copy-start.8 = (f32[4,8,256]{2,1,0:T(8,128)S(1)}, f32[4,8,256]{2,1,0:T(8,128)}, u32[]{:S(2)}) copy-start(f32[4,8,256]{2,1,0:T(8,128)} %refs_4_.1) | copy-start | bytes 98308
  5.5 15.7 %copy-start.1 = (f32[24,8,8,128]{3,2,1,0:T(8,128)S(1)}, f32[24,8,8,128]{3,2,1,0:T(8,128)}, u32[]{:S(2)}) copy-start(f32[24,8,8,128]{3,2,1,0:T(8,128)} %refs_6_.1) | copy-start | bytes 2359300
  5.5 15.7 %copy-start.3 = (f32[4,8,256]{2,1,0:T(8,128)S(1)}, f32[4,8,256]{2,1,0:T(8,128)}, u32[]{:S(2)}) copy-start(f32[4,8,256]{2,1,0:T(8,128)} %refs_1_.1) | copy-start | bytes 98308
  5.5 15.7 %copy-start.5 = (f32[4,8,256]{2,1,0:T(8,128)S(1)}, f32[4,8,256]{2,1,0:T(8,128)}, u32[]{:S(2)}) copy-start(f32[4,8,256]{2,1,0:T(8,128)} %refs_2_.1) | copy-start | bytes 98308
  5.5 15.7 %copy-start.7 = (f32[4,8,256]{2,1,0:T(8,128)S(1)}, f32[4,8,256]{2,1,0:T(8,128)}, u32[]{:S(2)}) copy-start(f32[4,8,256]{2,1,0:T(8,128)} %refs_3_.1) | copy-start | bytes 98308
  5.5 15.8 %copy-start.9 = (f32[4,8,256]{2,1,0:T(8,128)S(1)}, f32[4,8,256]{2,1,0:T(8,128)}, u32[]{:S(2)}) copy-start(f32[4,8,256]{2,1,0:T(8,128)} %refs_4_.1) | copy-start | bytes 98308
  7.4 6.5 %collective-permute-start.2 = (f32[56,8,128]{2,1,0:T(8,128)S(1)}, f32[56,8,128]{2,1,0:T(8,128)S(1)}, u32[]{:S(2)}, u32[]{:S(2)}) collective-permute-start(f32[56,8,128]{2,1,0:T(8,128)S(1)} %get-tuple-element.13.refs_7_), channel_id=1, source_target_pairs={{0,2},{1,3},{2,0},{3,1},{4,6},{5,7},{6,4},{7,5},{8,10},{9,11},{10,... | collective-permute-start | bytes 688136 | tf_op jit(solution)/shard_map/ppermute | solution.py:414
  7.7 13.6 %collective-permute-start = (f32[68,8,128]{2,1,0:T(8,128)S(1)}, f32[68,8,128]{2,1,0:T(8,128)S(1)}, u32[]{:S(2)}, u32[]{:S(2)}) collective-permute-start(f32[68,8,128]{2,1,0:T(8,128)S(1)} %get-tuple-element.18), channel_id=1, source_target_pairs={{0,2},{1,4},{2,0},{3,6},{4,1},{5,8},{6,3},{7,10},{8,5},{9,12},{10,... | collective-permute-start | bytes 835592 | tf_op jit(solution)/shard_map/ppermute | solution.py:414
  8.9 12.3 %collective-permute-start.1 = (f32[68,8,128]{2,1,0:T(8,128)S(1)}, f32[68,8,128]{2,1,0:T(8,128)S(1)}, u32[]{:S(2)}, u32[]{:S(2)}) collective-permute-start(f32[68,8,128]{2,1,0:T(8,128)S(1)} %get-tuple-element.19), channel_id=1, source_target_pairs={{0,1},{1,0},{2,3},{3,2},{4,5},{5,4},{6,7},{7,6},{8,9},{9,8},{10,11... | collective-permute-start | bytes 835592 | tf_op jit(solution)/shard_map/ppermute | solution.py:414
  13.9 7.3 %collective-permute-start.3 = (f32[56,8,128]{2,1,0:T(8,128)S(1)}, f32[56,8,128]{2,1,0:T(8,128)S(1)}, u32[]{:S(2)}, u32[]{:S(2)}) collective-permute-start(f32[56,8,128]{2,1,0:T(8,128)S(1)} %collective-permute-done.2.refs_14_), channel_id=1, source_target_pairs={{0,1},{1,0},{2,3},{3,2},{4,5},{5,4},{6,7},{7,6},{8,9},{9,8},{10,11... | collective-permute-start | bytes 688136 | tf_op jit(solution)/shard_map/ppermute | solution.py:414
  16.6 4.6 %collective-permute-start.4 = (f32[25,8,128]{2,1,0:T(8,128)S(1)}, f32[25,8,128]{2,1,0:T(8,128)S(1)}, u32[]{:S(2)}, u32[]{:S(2)}) collective-permute-start(f32[25,8,128]{2,1,0:T(8,128)S(1)} %get-tuple-element.20), channel_id=1, source_target_pairs={{0,2},{1,6},{2,0},{3,4},{4,3},{5,10},{6,1},{7,8},{8,7},{9,14},{10,... | collective-permute-start | bytes 307208 | tf_op jit(solution)/shard_map/ppermute | solution.py:414

commit v2 on v0

v2 whole, which is shorter than its diff:
```python
import functools

import jax
import jax.numpy as jnp
from jax import lax
from jax.experimental import pallas as pl
from jax.experimental.pallas import tpu as pltpu
from jax.sharding import PartitionSpec as P

ROWS = 8
LANES = 128
LEVELS = 8
CORES = 2
FIELDS = 4
NEAR = 4

RING_ROWS = 2 * ROWS
RING_COLS = 2 * LANES


def iota(shape, dim):
    return lax.broadcasted_iota(jnp.int32, shape, dim)


def roll(q, shift, axis):
    return pltpu.roll(q, shift % q.shape[axis], axis)


def block_of(m):
    return pl.ds(pl.multiple_of(m * LANES, LANES), LANES)


def load_kernel(n, pos, u, v, t, h, count, c, f_out, c_out, d_out, z_out, r_out, f_sem, c_sem):
    tracers = c.shape[0]
    share = f_out.shape[1]
    copies = [pltpu.make_async_copy(ref, f_out.at[i], f_sem.at[i]) for i, ref in enumerate((u, v, t, h))]
    copies.append(pltpu.make_async_copy(count, d_out, f_sem.at[FIELDS]))
    batch = tracers // c_sem.shape[0]
    c_copies = []
    for i in range(c_sem.shape[0]):
        part = pl.ds(i * batch, batch)
        c_copies.append(pltpu.make_async_copy(c.at[part], c_out.at[part], c_sem.at[i]))
    for copy in copies + c_copies:
        copy.start()
    upper = pos[2] == 1
    to_z = (iota((ROWS, LANES), 0) >= ROWS // 2) == upper
    for copy in copies:
        copy.wait()
    for level in range(share):
        for block in range(n):
            cols = slice(block * LANES, (block + 1) * LANES)
            place = level * n + block
            for pair in range(2):
                a = f_out[2 * pair, level, :, cols]
                b = roll(f_out[2 * pair + 1, level, :, cols], ROWS // 2, 0)
                z_out[pair * LEVELS + place] = jnp.where(to_z, a, b)
                r_out[pair * LEVELS + place] = jnp.where(to_z, b, a)
    base = 2 * LEVELS
    for block in range(n):
        depth = d_out[:, block * LANES : (block + 1) * LANES].astype(jnp.float32)
        z_out[base + block] = depth
        r_out[base + block] = depth
    base += n
    for i, copy in enumerate(c_copies):
        copy.wait()
        for b in range(i * batch, (i + 1) * batch):
            for far in range(2):
                bottom, top = c_out[b, :, far, :], c_out[b, :, ROWS - 1 - far, :]
                z_out[base + 2 * b + far] = jnp.where(upper, top, bottom)
                r_out[base + 2 * b + far] = jnp.where(upper, bottom, top)


def pack_kernel(n, pos, rates, f, c, r, *outs):
    sums, edges = outs[:2]
    x_outs, xz_outs = outs[2 : 1 + n], outs[1 + n :]
    tracers, share = c.shape[0], f.shape[1]
    lon, upper = pos[1], pos[2] == 1
    to_z = (iota((ROWS, LANES), 0) >= ROWS // 2) == upper
    lane = iota((ROWS, LANES), 1)

    def packed(get):
        total = jnp.zeros((ROWS, LANES), jnp.float32)
        edge = jnp.zeros((ROWS, LANES), jnp.float32)
        for b in range(tracers):
            q = get(b)
            total = total + rates[0, b] * q
            edge = jnp.where(lane // 4 == b, roll(q, 4 * b + 2, 1), edge)
        return total, jnp.where(lane // 4 == tracers, roll(total, 4 * tracers + 2, 1), edge)

    def one_level(k, carry):
        sums[k], edges[k] = packed(lambda b: c[b, k])
        return carry

    lax.fori_loop(0, LEVELS, one_level, 0)
    base = 2 * LEVELS + n
    _, corner = packed(lambda b: r[base + 2 * b])
    count = FIELDS * share
    for s, (x_out, xz_out) in enumerate(zip(x_outs, xz_outs)):
        m = lax.rem(lon + (s + 1), n)
        e, w = lax.rem(m + 1, n), lax.rem(m + n - 1, n)

        def sides_of(get, amount):
            sides = jnp.zeros((ROWS, LANES), jnp.float32)
            for i in range(amount):
                side = jnp.where(lane < LANES // 2, get(i, e), get(i, w))
                sides = jnp.where(lane // (2 * NEAR) == i, roll(side, 2 * NEAR * i + NEAR, 1), sides)
            return sides

        def whole(i, block):
            return f[i // share, i % share, :, block_of(block)]

        def outgoing(i, block):
            pair, level = i // share, i % share
            a, b = f[2 * pair, level, :, block_of(block)], f[2 * pair + 1, level, :, block_of(block)]
            return jnp.where(to_z, a, roll(b, ROWS // 2, 0))

        def beside(i, block):
            return r[(i // share) * LEVELS + (i % share) * n + block]

        x_out[count + 1 : count + 1 + LEVELS] = edges[...]
        end = count + 1 + LEVELS
        for i in range(count):
            x_out[i] = whole(i, m)
        for i in range(count // 2):
            x_out[end + i] = beside(i, m)
            xz_out[i] = outgoing(i, m)
        x_out[count] = sides_of(whole, count)
        x_out[end + count // 2] = sides_of(beside, count // 2)
        x_out[end + count // 2 + 1] = corner
        xz_out[count // 2] = sides_of(outgoing, count // 2)
        xz_out[count // 2 + 1] = jnp.where(upper, edges[:, ROWS - 1, :], edges[:, 0, :])


def split(q):
    high = q.astype(jnp.bfloat16)
    return high, (q - high.astype(jnp.float32)).astype(jnp.bfloat16)


def spread_kernel(rates, m_high, m_low, e_high, e_low):
    tracers = rates.shape[0]
    exact = functools.partial(jnp.dot, precision=lax.Precision.HIGHEST, preferred_element_type=jnp.float32)
    for group, transposed, high, low in ((ROWS, False, m_high, m_low), (4, True, e_high, e_low)):
        size = high.shape[0]
        rows = (iota((size, tracers), 0) // group == iota((size, tracers), 1)).astype(jnp.float32)
        cols = (iota((tracers, size), 1) // group == iota((tracers, size), 0)).astype(jnp.float32)
        wide = exact(exact(rows, rates[...].T if transposed else rates[...]), cols)
        same = iota((size, size), 0) % group == iota((size, size), 1) % group
        high[...], low[...] = split(jnp.where(same, wide, 0.0))


def exact_product(left, right):
    dot = functools.partial(jnp.dot, preferred_element_type=jnp.float32)
    return dot(left[0], right[0]) + (dot(left[0], right[1]) + dot(left[1], right[0]))


class Halo:
    def __init__(self, pos, strips):
        self.upper = pos[2] == 1
        end = jnp.logical_or(
            jnp.logical_and(pos[0] == 0, jnp.logical_not(self.upper)),
            jnp.logical_and(pos[0] == strips - 1, self.upper),
        )
        self.keep_z = jnp.where(end, 0.0, 1.0)
        self.from_r = (iota((ROWS, LANES), 0) >= ROWS // 2) == self.upper

    def rows(self, r, z):
        return jnp.where(self.from_r, r, z * self.keep_z)

    def sides(self, r, z):
        z = z * self.keep_z
        return jnp.where(self.upper, r, z), jnp.where(self.upper, z, r)


def flow_kernel(n, strips, *refs):
    pos, rates, f, count, c, sums, edges, z, r = refs[:9]
    others = n - 1
    xs, xzs = (refs[9 + i * others : 9 + (i + 1) * others] for i in range(2))
    coef1, coef2, ends, rims, f_out = refs[9 + 2 * others : 14 + 2 * others]
    heats = refs[14 + 2 * others : 14 + 3 * others]
    dyn, mix, depth, all_edges, all_rims, out, light_out = refs[14 + 3 * others :]
    tracers, share = c.shape[0], f.shape[1]
    strip, lon = pos[0], pos[1]
    halo = Halo(pos, strips)
    lane = iota((ROWS, LANES), 1)
    first, second = slice(0, LANES), slice(LANES, RING_COLS)
    own_rows, next_rows = slice(0, ROWS), slice(ROWS, RING_ROWS)
    base = 2 * LEVELS + n
    half = ROWS // 2

    def beside(m):
        return lax.rem(m + 1, n), lax.rem(m + n - 1, n)

    def window(main, near, m):
        east, west = beside(m)

        def side(g):
            return g(east) if n == 2 else jnp.where(lane < LANES // 2, g(east), g(west))

        return main(m), side(main), near(m), side(near)

    def put(ref, at, tiles):
        for tile, (rows, cols) in zip(
            tiles, ((own_rows, first), (own_rows, second), (next_rows, first), (next_rows, second))
        ):
            ref[(*at, rows, cols)] = tile

    def own_window(field, level, m):
        pair, odd = field // 2, field % 2

        def near(block):
            place = pair * LEVELS + level * n + block
            a, b = r[place], z[place]
            if odd:
                a, b = roll(a, half, 0), roll(b, half, 0)
            return halo.rows(a, b)

        return window(lambda block: f[field, level, :, block_of(block)], near, m)

    for field in range(FIELDS):
        for level in range(share):
            put(dyn, (field, lon * share + level), own_window(field, level, lon))

    def depth_window(m):
        return window(
            lambda block: count[:, block_of(block)].astype(jnp.float32),
            lambda block: halo.rows(r[2 * LEVELS + block], z[2 * LEVELS + block]),
            m,
        )

    put(depth, (), depth_window(lon))

    sides = FIELDS * share
    end = sides + 1 + LEVELS
    for s, (x, xz) in enumerate(zip(xs, xzs)):
        m = lax.rem(lon + (n - 1 - s), n)
        for field in range(FIELDS):
            for level in range(share):
                i, j = field * share + level, (field // 2) * share + level
                shift = -(2 * NEAR * j + NEAR)
                near = [x[end + j], xz[j], roll(x[end + sides // 2], shift, 1), roll(xz[sides // 2], shift, 1)]
                if field % 2:
                    near = [roll(q, half, 0) for q in near]
                side = roll(x[sides], -(2 * NEAR * i + NEAR), 1)
                put(
                    dyn,
                    (field, m * share + level),
                    (x[i], side, halo.rows(near[0], near[1]), halo.rows(near[2], near[3])),
                )
        all_edges[m] = x[sides + 1 : end]
        all_rims[m, 0], all_rims[m, 1] = halo.sides(x[end + sides // 2 + 1], xz[sides // 2 + 1])

    east, west = beside(lon)
    easterly = lane % 4 >= 2
    exists = jnp.where(easterly, jnp.where(lon < n - 1, 1.0, 0.0), jnp.where(lon > 0, 1.0, 0.0))
    for k in range(LEVELS):
        ends[k] = jnp.where(easterly, all_edges[east, k], all_edges[west, k]) * exists
    for side in range(2):
        rims[side] = jnp.where(easterly, all_rims[east, side], all_rims[west, side]) * exists

    mix[0, :, own_rows, first] = c[0]
    mix[1, :, own_rows, first] = sums[...]
    for i, b in enumerate((0, tracers)):
        for k in range(LEVELS):
            mix[i, k, own_rows, second] = roll(ends[k], -(4 * b + 2), 1)
        for side, place in enumerate((RING_ROWS - 1, ROWS)):
            mix[i, :, place, second] = roll(rims[side], -(4 * b + 2), 1)
    for far in range(2):
        total = [jnp.zeros((LEVELS, LANES), jnp.float32)] * 2
        for b in range(tracers):
            rows = halo.sides(r[base + 2 * b + far], z[base + 2 * b + far])
            if b == 0:
                chl = rows
            total = [a + rates[0, b] * q for a, q in zip(total, rows)]
        for i, rows in enumerate((chl, total)):
            mix[i, :, RING_ROWS - 1 - far, first] = rows[0]
            mix[i, :, ROWS + far, first] = rows[1]

    wide = (RING_ROWS, RING_COLS)
    ring_row, ring_col = iota(wide, 0), iota(wide, 1)
    row = strip * ROWS + jnp.where(ring_row < ROWS + half, ring_row, ring_row - RING_ROWS)
    fcor = 2.0 * (row.astype(jnp.float32) + 0.5) / (strips * ROWS) - 1.0

    def north(q):
        return roll(q, -1, 0)

    def south(q):
        return roll(q, 1, 0)

    def around(m):
        e, w = beside(m)
        block = jnp.where(ring_col < LANES, m, jnp.where(ring_col < LANES + LANES // 2, e, w))
        col = block * LANES + ring_col % LANES
        not_last, not_first = col < n * LANES - 1, col > 0
        return (
            lambda q: jnp.where(not_last, roll(q, -1, 1), 0.0),
            lambda q: jnp.where(not_first, roll(q, 1, 1), 0.0),
        )

    def masks(k, counts, east):
        wet = jnp.where(counts > k.astype(jnp.float32), 1.0, 0.0)
        return wet, wet * east(wet), wet * north(wet)

    def advance(uu, vv, tt, wets, east, west):
        wet, wet_u, wet_v = wets

        def lap(q, e, nn):
            return e + west(q) + nn + south(q) - 4.0 * q

        te, tn = east(tt), north(tt)
        u_new = wet_u * (uu + 0.1 * lap(uu, east(uu), north(uu)) + 0.3 * fcor * vv - 0.2 * (te - tt))
        v_new = wet_v * (vv + 0.1 * lap(vv, east(vv), north(vv)) - 0.3 * fcor * uu - 0.2 * (tn - tt))
        return u_new, v_new, wet * (tt + 0.1 * lap(tt, te, tn))

    def coefficients(uu, vv, uw, vs):
        a0 = 1.0 - 0.5 * (
            (jnp.maximum(uu, 0.0) - jnp.minimum(uw, 0.0)) + (jnp.maximum(vv, 0.0) - jnp.minimum(vs, 0.0))
        )
        return (
            a0,
            -0.5 * jnp.minimum(uu, 0.0),
            0.5 * jnp.maximum(uw, 0.0),
            -0.5 * jnp.minimum(vv, 0.0),
            0.5 * jnp.maximum(vs, 0.0),
        )

    east_of, west_of = around(lon)

    def one_level(k, carry):
        tau1, top1, tau2, top2 = carry
        wets = masks(k, depth[...], east_of)
        wet = wets[0]
        heat0 = dyn[3, k]
        uu, vv, tt = advance(dyn[0, k], dyn[1, k], dyn[2, k], wets, east_of, west_of)
        tt = tt + 0.5 * (wet * heat0)
        stencil = coefficients(uu, vv, west_of(uu), south(vv))

        def advect(q):
            a0, ae, aw, an, a_s = stencil
            return a0 * q + (ae * east_of(q) + aw * west_of(q)) + (an * north(q) + a_s * south(q))

        moved = advect(mix[0, k])
        tau1 = tau1 + (0.1 + 0.3 * jnp.maximum(moved, 0.0))
        below = jnp.exp(-tau1)
        half_wet = 0.5 * wet
        warm = half_wet * (2.0 * (top1 - below))
        light = half_wet * top1
        for i, q in enumerate((*stencil, wet, light)):
            coef1[i, k] = q
        chl = wet * moved + light * advect(mix[1, k])
        top1 = below

        uu, vv, tt = advance(uu, vv, tt, wets, east_of, west_of)
        inner = (own_rows, first)
        own = [q[inner] for q in coefficients(uu, vv, west_of(uu), south(vv))]
        moved = (
            own[0] * chl[inner]
            + (own[1] * east_of(chl)[inner] + own[2] * west_of(chl)[inner])
            + (own[3] * north(chl)[inner] + own[4] * south(chl)[inner])
        )
        tau2 = tau2 + (0.1 + 0.3 * jnp.maximum(moved, 0.0))
        below = jnp.exp(-tau2)
        for i, q in enumerate((*own, wet[inner], half_wet[inner] * top2)):
            coef2[i, k] = q
        light_out[0, k] = warm[inner]
        light_out[1, k] = 2.0 * wet[inner] * (top2 - below)
        out[0, k], out[1, k], out[2, k] = uu[own_rows], vv[own_rows], tt[own_rows]
        return tau1, top1, tau2, below

    big = jnp.zeros(wide, jnp.float32)
    small = jnp.zeros((ROWS, LANES), jnp.float32)
    lax.fori_loop(0, LEVELS, one_level, (big, big + 1.0, small, small + 1.0))

    here = block_of(lon)
    for level in range(share):
        k = lon * share + level
        for i in range(3):
            q = out[i, k, :, first]
            f_out[i, level, :, here] = q + light_out[0, k] if i == 2 else q
            if n == 2:
                f_out[i, level, :, block_of(1 - lon)] = out[i, k, :, second]
        f_out[3, level, :, here] = light_out[1, k]
    for s, heat in enumerate(heats):
        m = lax.rem(lon + (s + 1), n)
        for i in range(2):
            heat[i] = light_out[i, pl.ds(m * share, share)]

    if n > 2:

        def other_block(s, carry):
            m = lax.rem(lon + s, n)
            e, w = around(m)
            put(depth, (), depth_window(m))
            for level in range(share):
                k = lon * share + level
                wets = masks(k, depth[...], e)
                for field in range(FIELDS):
                    put(dyn, (field, k), own_window(field, level, m))
                uu, vv, tt = advance(dyn[0, k], dyn[1, k], dyn[2, k], wets, e, w)
                tt = tt + 0.5 * (wets[0] * dyn[3, k])
                for i, q in enumerate(advance(uu, vv, tt, wets, e, w)):
                    f_out[i, level, :, block_of(m)] = q[own_rows, first]
            return carry

        lax.fori_loop(1, n, other_block, 0)


def tile_stencil(q, rim, columns, stencil, sub, lane):
    a0, ae, aw, an, a_s = stencil
    e = jnp.where(lane == LANES - 1, columns, roll(q, -1, 1))
    w = jnp.where(lane == 0, columns, roll(q, 1, 1))
    up = jnp.where(sub == ROWS - 1, rim, roll(q, -1, 0))
    down = jnp.where(sub == 0, rim, roll(q, 1, 0))
    return a0 * q + (ae * e + aw * w) + (an * up + a_s * down)


def swapped(q):
    return jnp.where(iota(q.shape, 1) % 4 == 1, roll(q, -1, 1), roll(q, 1, 1))


def beside_columns(edge, b):
    return roll(edge, LANES - 2 - 4 * b, 1)


def part_of(b, half):
    return slice(b * ROWS, (b + 1) * ROWS), slice(half * LANES, (half + 1) * LANES)


def tile_loop(source, rims, edge, coef, m_pair, adv, store):
    tracers = source.shape[0]
    sub, lane = iota((ROWS, LANES), 0), iota((ROWS, LANES), 1)

    def two_levels(i, carry):
        for half in range(2):
            k = 2 * i + half
            stencil = [coef(j, k) for j in range(5)]
            columns = edge[k]
            for b in range(tracers):
                adv[part_of(b, half)] = tile_stencil(
                    source[b, k], rims[b, k], beside_columns(columns, b), stencil, sub, lane
                )
        react = exact_product(m_pair, split(adv[...]))
        for half in range(2):
            k = 2 * i + half
            wet, light = coef(5, k), coef(6, k)
            for b in range(tracers):
                store(b, k, wet * adv[part_of(b, half)] + light * react[part_of(b, half)])
        return carry

    return two_levels


def first_kernel(n, strips, pos, c, edges, ends, rims, coef, m_high, m_low, e_high, e_low, z, r, c_out, row1, edge1, row0, edge0, adv):
    tracers = c.shape[0]
    lon = pos[1]
    halo = Halo(pos, strips)
    sub, lane = iota((ROWS, LANES), 0), iota((ROWS, LANES), 1)
    easterly = lane % 4 >= 2
    base = 2 * LEVELS + n
    m_pair = (m_high[...], m_low[...])

    rim = row0.at[0]
    rim[:, 0, :] = rims[0]
    rim[:, ROWS - 1, :] = rims[1]
    parts = []
    for k in range(LEVELS):
        q, inside = ends[k], edges[k]
        outer = jnp.where(easterly, roll(q, -1, 1), roll(q, 1, 1))
        inner = jnp.where(easterly, roll(inside, 1, 1), roll(inside, -1, 1))
        up = jnp.where(sub == ROWS - 1, rim[k], roll(q, -1, 0))
        down = jnp.where(sub == 0, rim[k], roll(q, 1, 0))

        def at_edge(i):
            side = coef[i, k, :ROWS, LANES:]
            return (
                jnp.broadcast_to(side[:, :1], (ROWS, LANES)),
                jnp.broadcast_to(side[:, LANES - 1 :], (ROWS, LANES)),
            )

        def pick(pair):
            return jnp.where(easterly, pair[0], pair[1])

        a0, ae, aw, an, a_s, wet, light = (at_edge(i) for i in range(7))
        moved = (
            pick(a0) * q
            + (pick((ae[0], aw[1])) * outer + pick((aw[0], ae[1])) * inner)
            + (pick(an) * up + pick(a_s) * down)
        )
        parts.append((moved, pick(wet), pick(light)))
        edge0[k] = swapped(q)
    react = exact_product(split(jnp.concatenate([p[0] for p in parts], axis=0)), (e_high[...], e_low[...]))
    east_exists = jnp.where(lon < n - 1, 1.0, 0.0)
    west_exists = jnp.where(lon > 0, 1.0, 0.0)
    exists = jnp.where(easterly, east_exists, west_exists)
    for k, (q, wet, light) in enumerate(parts):
        edge1[k] = swapped((wet * q + light * react[k * ROWS : (k + 1) * ROWS]) * exists)

    places = ((0, RING_ROWS - 1), (ROWS - 1, ROWS))
    corners = [swapped(rims[side]) for side in range(2)]
    stencils = [[coef[i, :, place, :LANES] for i in range(7)] for _, place in places]
    for b in range(tracers):
        near = halo.sides(r[base + 2 * b], z[base + 2 * b])
        far = halo.sides(r[base + 2 * b + 1], z[base + 2 * b + 1])
        for side, (at, _) in enumerate(places):
            a0, ae, aw, an, a_s, _, _ = stencils[side]
            q = near[side]
            row0[b, :, at, :] = q
            columns = beside_columns(corners[side], b)
            e = jnp.where(lane == LANES - 1, columns, roll(q, -1, 1))
            w = jnp.where(lane == 0, columns, roll(q, 1, 1))
            inner = c[b, :, at, :]
            up, down = (inner, far[side]) if side == 0 else (far[side], inner)
            adv[part_of(b, side)] = a0 * q + (ae * e + aw * w) + (an * up + a_s * down)
    react = exact_product(m_pair, split(adv[...]))
    for b in range(tracers):
        for side, (at, _) in enumerate(places):
            wet, light = stencils[side][5:]
            row1[b, :, at, :] = wet * adv[part_of(b, side)] + light * react[part_of(b, side)]

    def store(b, k, q):
        c_out[b, k] = q

    lax.fori_loop(
        0,
        LEVELS // 2,
        tile_loop(c, row0, edge0, lambda i, k: coef[i, k, :ROWS, :LANES], m_pair, adv, store),
        0,
    )


def last_kernel(n, *refs):
    others = n - 1
    pos, c, row1, edge1, coef, m_high, m_low, f = refs[:8]
    heats = refs[8 : 8 + others]
    u_out, v_out, t_out, h_out, c_out = refs[8 + others : 13 + others]
    result, warm, adv, sem, c_sem = refs[13 + others :]
    share = f.shape[1]
    lon = pos[1]
    flows = [pltpu.make_async_copy(f.at[i], ref, sem.at[i]) for i, ref in enumerate((u_out, v_out))]
    for copy in flows:
        copy.start()
    here = block_of(lon)
    for level in range(share):
        warm[0, level, :, here] = f[2, level, :, here]
        warm[1, level, :, here] = f[3, level, :, here]
        for s, heat in enumerate(heats):
            there = block_of(lax.rem(lon + (n - 1 - s), n))
            warm[0, level, :, there] = f[2, level, :, there] + heat[0, level]
            warm[1, level, :, there] = heat[1, level]
    flows += [pltpu.make_async_copy(warm.at[i], ref, sem.at[2 + i]) for i, ref in enumerate((t_out, h_out))]
    for copy in flows[2:]:
        copy.start()

    def store(b, k, q):
        result[b, k] = q

    def copy_out(i):
        part = pl.ds(2 * i, 2)
        return pltpu.make_async_copy(result.at[:, part], c_out.at[:, part], c_sem.at[i])

    body = tile_loop(c, row1, edge1, lambda i, k: coef[i, k], (m_high[...], m_low[...]), adv, store)

    def one_pass(i, carry):
        body(i, carry)
        copy_out(i).start()
        return carry

    lax.fori_loop(0, LEVELS // 2, one_pass, 0)
    for copy in flows:
        copy.wait()
    for i in range(LEVELS // 2):
        copy_out(i).wait()


def shards(n, lats, u, v, t, h, c, count, rates):
    tracers = c.shape[0]
    share, width = u.shape[0], u.shape[2]
    strips = lats * CORES
    lat, lon, role = lax.axis_index("lat"), lax.axis_index("lon"), lax.axis_index("role")
    pos = jnp.stack([lat * CORES + role, lon, role]).astype(jnp.int32)
    vmem = pl.BlockSpec(memory_space=pltpu.VMEM)
    smem = pl.BlockSpec(memory_space=pltpu.SMEM)
    anywhere = pl.BlockSpec(memory_space=pl.ANY)
    hbm = pl.BlockSpec(memory_space=pltpu.HBM)
    params = pltpu.CompilerParams(vmem_limit_bytes=32 * 1024 * 1024)
    dma = pltpu.SemaphoreType.DMA

    def shape(*dims, dtype=jnp.float32):
        return jax.ShapeDtypeStruct(dims, dtype)

    def tiles(*dims):
        return shape(*dims, ROWS, LANES)

    def scratch(*dims):
        return pltpu.VMEM(dims, jnp.float32)

    def call(kernel, name, args, in_specs, out_shape, out_specs=None, scratch_shapes=()):
        return pl.pallas_call(
            kernel,
            out_shape=tuple(out_shape),
            in_specs=in_specs,
            out_specs=out_specs or (vmem,) * len(out_shape),
            scratch_shapes=scratch_shapes,
            compiler_params=params,
            name=name,
        )(*args)

    def permute(q, target):
        pairs = []
        for a in range(lats):
            for o in range(n):
                for i in range(CORES):
                    a2, o2, i2 = target(a, o, i)
                    pairs.append(((a * n + o) * CORES + i, (a2 * n + o2) * CORES + i2))
        return lax.ppermute(q, ("lat", "lon", "role"), pairs)

    def over_lat(a, i):
        s = a * CORES + i + (1 if i else -1)
        return (s // CORES, s % CORES) if 0 <= s < strips else None

    def z_target(a, o, i):
        to = over_lat(a, i)
        return (to[0], o, to[1]) if to else (a, o ^ 1 if o ^ 1 < n else o, i)

    def x_target(shift):
        return lambda a, o, i: (a, (o + shift) % n, i)

    def xz_target(shift):
        def target(a, o, i):
            to = over_lat(a, i) or (a, i)
            return to[0], (o + shift) % n, to[1]

        return target

    def r_target(a, o, i):
        return a, o, 1 - i

    shifts = range(1, n)
    z_tiles = 2 * LEVELS + n + 2 * tracers
    xz_tiles = FIELDS * share // 2 + 2
    x_tiles = FIELDS * share + 1 + LEVELS + xz_tiles
    f, c_here, depth, z_pay, r_pay = call(
        functools.partial(load_kernel, n),
        "load",
        (pos, *(pltpu.with_memory_space_constraint(q, pltpu.HBM) for q in (u, v, t, h, count, c))),
        [smem] + [hbm] * 6,
        [
            shape(FIELDS, *u.shape),
            shape(*c.shape),
            shape(*count.shape, dtype=jnp.int32),
            tiles(z_tiles),
            tiles(z_tiles),
        ],
        scratch_shapes=[dma((FIELDS + 1,)), dma((4,))],
    )
    r_in = permute(r_pay, r_target)
    z_in = permute(z_pay, z_target)
    sums, edges, *pays = call(
        functools.partial(pack_kernel, n),
        "pack",
        (pos, rates, f, c_here, r_in),
        [smem, smem] + [vmem] * 3,
        [tiles(LEVELS)] * 2 + [tiles(x_tiles)] * (n - 1) + [tiles(xz_tiles)] * (n - 1),
    )
    xs = [permute(q, x_target(s)) for s, q in zip(shifts, pays[: n - 1])]
    xzs = [permute(q, xz_target(s)) for s, q in zip(shifts, pays[n - 1 :])]

    m_size, e_size = tracers * ROWS, LANES
    bf16 = jnp.bfloat16
    m_high, m_low, e_high, e_low = call(
        spread_kernel,
        "spread",
        (rates,),
        [vmem],
        [shape(s, s, dtype=bf16) for s in (m_size, m_size, e_size, e_size)],
    )

    args = (pos, rates, f, depth, c_here, sums, edges, z_in, r_in, *xs, *xzs)
    coef1, coef2, ends, rims, f_new, *heats = call(
        functools.partial(flow_kernel, n, strips),
        "flow",
        args,
        [smem, smem] + [vmem] * (len(args) - 2),
        [
            shape(7, LEVELS, RING_ROWS, RING_COLS),
            tiles(7, LEVELS),
            tiles(LEVELS),
            shape(2, LEVELS, LANES),
            shape(FIELDS, *u.shape),
        ]
        + [tiles(2, share)] * (n - 1),
        scratch_shapes=[
            scratch(FIELDS, LEVELS, RING_ROWS, RING_COLS),
            scratch(2, LEVELS, RING_ROWS, RING_COLS),
            scratch(RING_ROWS, RING_COLS),
            scratch(n, LEVELS, ROWS, LANES),
            scratch(n, 2, LEVELS, LANES),
            scratch(3, LEVELS, ROWS, RING_COLS),
            scratch(2, LEVELS, ROWS, LANES),
        ],
    )
    heats = [permute(q, x_target(s)) for s, q in zip(shifts, heats)]
    args = (pos, c_here, edges, ends, rims, coef1, m_high, m_low, e_high, e_low, z_in, r_in)
    c_mid, row1, edge1 = call(
        functools.partial(first_kernel, n, strips),
        "first",
        args,
        [smem] + [vmem] * (len(args) - 1),
        [shape(*c.shape), tiles(tracers, LEVELS), tiles(LEVELS)],
        scratch_shapes=[
            scratch(tracers, LEVELS, ROWS, LANES),
            scratch(LEVELS, ROWS, LANES),
            scratch(tracers * ROWS, 2 * LANES),
        ],
    )
    args = (pos, c_mid, row1, edge1, coef2, m_high, m_low, f_new, *heats)
    return call(
        functools.partial(last_kernel, n),
        "last",
        args,
        [smem] + [vmem] * (len(args) - 1),
        [shape(*u.shape)] * FIELDS + [shape(*c.shape)],
        out_specs=(anywhere,) * 5,
        scratch_shapes=[
            scratch(*c.shape),
            scratch(2, *u.shape),
            scratch(tracers * ROWS, 2 * LANES),
            dma((FIELDS,)),
            dma((LEVELS // 2,)),
        ],
    )


def solution(mesh):
    level = P("lon", ("grp", "lat", "role"), None)
    tracer = P(None, None, ("grp", "lat", "role"), "lon")
    return jax.shard_map(
        functools.partial(shards, mesh.shape["lon"], mesh.shape["lat"]),
        mesh=mesh,
        in_specs=(level, level, level, level, tracer, P(("grp", "lat", "role"), None), P()),
        out_specs=(level, level, level, level, tracer),
        check_vma=False,
    )
```

time: 120 us -> 26.5 us (0.22); the launches traced: 118 us -> 26.3 us
  starting transfers between devices: 40.7 us -> 7.18 us
  local copies, waits for them, and re-layouts: 30.7 us -> 0.01 us
  waiting for transfers between devices: 25.1 us -> 4.72 us
  other arithmetic: 17.3 us -> 0.08 us
  Pallas kernels: 0 us -> 13.7 us
  matrix products: 2.5 us -> 0 us
    ppermute x13 -> x5, starting transfers between devices: 27.1 us -> 7.18 us  [permute(): return lax.ppermute(q, ('lat', 'lon', 'role'), pairs)]
    pallas_call x0 -> x6, Pallas kernels: none -> 13.7 us  [call(): pl.pallas_call(kernel, out_shape=tuple(out_shape), in_specs=in_specs, out...]
    all_to_all x4 -> x0, starting transfers between devices: 13.6 us -> none  [the longest x2 6.85 us: shards(): lax.all_to_all(heat_tile, 'lon', split_axis=0, concat_axis=2, tiled=True)]
    all_to_all x4 -> x0, waiting for transfers between devices: 13.2 us -> none  [the longest x2 7.52 us: shards(): lax.all_to_all(jnp.stack([eastward_current, poleward_current]), 'lon', sp...]
    slice x11 -> x0, local copies, waits for them, and re-layouts: 10.7 us -> none  [the longest x5 8.04 us: padded(): last = lax.slice_in_dim(shard, length - width, length, axis=dim)]
    ppermute x4 -> x0, local copies, waits for them, and re-layouts: 8.4 us -> none  [the longest x2 5.2 us: padded(): after = lax.ppermute(leading, axis, down)]
    unnamed x33 -> x2, local copies, waits for them, and re-layouts: 8.39 us -> 0.01 us
    ppermute x13 -> x5, waiting for transfers between devices: 11.9 us -> 4.72 us  [permute(): return lax.ppermute(q, ('lat', 'lon', 'role'), pairs)]
  transfers between devices with their start and end apart: 17 -> 5, of which waited for: 9 -> 2; matrix products, arithmetic and copies ran while one was open for 13% -> 0% of each run, Pallas kernels for 0% -> 21%
where the time goes in v2:
time: 26.5 us; the launch traced here: 26.3 us
  Pallas kernels  13.7 us (52%)
  starting transfers between devices  7.18 us (27%)
  waiting for transfers between devices  4.72 us (18%)
  between operations  0.69 us (3%)
    pallas_call x6, Pallas kernels, call(): pl.pallas_call(kernel, out_shape=tuple(out_shape), in_specs=in_specs, out...  13.7 us
    ppermute x5, starting transfers between devices, permute(): return lax.ppermute(q, ('lat', 'lon', 'role'), pairs)  7.18 us
    ppermute x5, waiting for transfers between devices, permute(): return lax.ppermute(q, ('lat', 'lon', 'role'), pairs)  4.72 us
  transfers between devices with their start and end apart: 5, of which 2 were waited for; matrix products, arithmetic and copies ran while one was open for 0% of the time, Pallas kernels for 21%

profile of v2, /device:TPU:0, one launch (start us, length us, event | category | flops | bytes accessed | tf_op | source)
XLA Modules:
  0.0 26.3 jit_solution(16111050437564561015)
XLA Ops:
  0.6 0.1 pad_add_fusion.pos.refs_0_
  0.7 0.0 copy-start
  0.7 2.0 %load.1 = (f32[4,4,8,256]{3,2,1,0:T(8,128)S(1)}, f32[24,8,8,128]{3,2,1,0:T(8,128)S(1)}, s32[8,256]{1,0:T(8,128)S(1)}, f32[66,8,128]{2,1,0:T(8,128)S(1)}, f32[66,8,128]{2,1,0:T(8,128)S(1)}) custom-call(s32[3]{0:T(128)S(1)} %pad_add_fusion.pos.refs_0_, f32[4,8,256]{2,1,0:T(8,128)} %u.1, f32[4,8,256]{2,1,0:T(8,128)} %v.1, f32[4,8,256]{2,1,0:T(8,128)} %t.1, ...), custom_call_target="tpu_custom_call" | custom-call | tf_op jit(solution)/shard_map/load/pallas_call | solution.py:597
  2.7 0.5 %collective-permute-start = (f32[66,8,128]{2,1,0:T(8,128)S(1)}, f32[66,8,128]{2,1,0:T(8,128)S(1)}, u32[]{:S(2)}, u32[]{:S(2)}) collective-permute-start(f32[66,8,128]{2,1,0:T(8,128)S(1)} %get-tuple-element.29), channel_id=1, source_target_pairs={{0,1},{1,0},{2,3},{3,2},{4,5},{5,4},{6,7},{7,6},{8,9},{9,8},{10,11... | collective-permute-start | bytes 811016 | tf_op jit(solution)/shard_map/ppermute | solution.py:614
  3.2 2.6 %collective-permute-start.1 = (f32[66,8,128]{2,1,0:T(8,128)S(1)}, f32[66,8,128]{2,1,0:T(8,128)S(1)}, u32[]{:S(2)}, u32[]{:S(2)}) collective-permute-start(f32[66,8,128]{2,1,0:T(8,128)S(1)} %get-tuple-element.33), channel_id=1, source_target_pairs={{0,2},{1,4},{2,0},{3,6},{4,1},{5,8},{6,3},{7,10},{8,5},{9,12},{10,... | collective-permute-start | bytes 811016 | tf_op jit(solution)/shard_map/ppermute | solution.py:614
  5.8 0.0 collective-permute-done.r.refs_8_
  5.8 0.0 copy-done
  5.8 1.6 %pack.1 = (f32[8,8,128]{2,1,0:T(8,128)S(1)}, f32[8,8,128]{2,1,0:T(8,128)S(1)}, f32[35,8,128]{2,1,0:T(8,128)S(1)}, f32[10,8,128]{2,1,0:T(8,128)S(1)}) custom-call(s32[3]{0:T(128)S(1)} %pad_add_fusion.pos.refs_0_, f32[24,24]{1,0:T(8,128)S(1)} %copy-done, f32[4,4,8,256]{3,2,1,0:T(8,128)S(1)} %get-tuple-element.28.f.refs_2_, ...), custom_call_target="tpu_custom_call" | custom-call | tf_op jit(solution)/shard_map/pack/pallas_call | solution.py:597
  7.4 1.5 %collective-permute-start.2 = (f32[35,8,128]{2,1,0:T(8,128)S(1)}, f32[35,8,128]{2,1,0:T(8,128)S(1)}, u32[]{:S(2)}, u32[]{:S(2)}) collective-permute-start(f32[35,8,128]{2,1,0:T(8,128)S(1)} %get-tuple-element.34), channel_id=1, source_target_pairs={{0,2},{1,3},{2,0},{3,1},{4,6},{5,7},{6,4},{7,5},{8,10},{9,11},{10,... | collective-permute-start | bytes 430088 | tf_op jit(solution)/shard_map/ppermute | solution.py:614
  9.0 0.6 %collective-permute-start.3 = (f32[10,8,128]{2,1,0:T(8,128)S(1)}, f32[10,8,128]{2,1,0:T(8,128)S(1)}, u32[]{:S(2)}, u32[]{:S(2)}) collective-permute-start(f32[10,8,128]{2,1,0:T(8,128)S(1)} %get-tuple-element.35), channel_id=1, source_target_pairs={{0,2},{1,6},{2,0},{3,4},{4,3},{5,10},{6,1},{7,8},{8,7},{9,14},{10,... | collective-permute-start | bytes 122888 | tf_op jit(solution)/shard_map/ppermute | solution.py:614
  9.5 0.7 %collective-permute-done.1.refs_7_.z = f32[66,8,128]{2,1,0:T(8,128)S(1)} collective-permute-done((f32[66,8,128]{2,1,0:T(8,128)S(1)}, f32[66,8,128]{2,1,0:T(8,128)S(1)}, u32[]{:S(2)}, u32[]{:S(2)}) %collective-permute-start.1) | collective-permute-done | bytes 270368 | tf_op jit(solution)/shard_map/ppermute | solution.py:614
  10.2 4.0 %collective-permute-done.3.refs_10_ = f32[10,8,128]{2,1,0:T(8,128)S(1)} collective-permute-done((f32[10,8,128]{2,1,0:T(8,128)S(1)}, f32[10,8,128]{2,1,0:T(8,128)S(1)}, u32[]{:S(2)}, u32[]{:S(2)}) %collective-permute-start.3) | collective-permute-done | bytes 40992 | tf_op jit(solution)/shard_map/ppermute | solution.py:614
  14.2 0.0 collective-permute-done.2.refs_9_
  14.2 3.1 %flow.1 = (f32[7,8,16,256]{3,2,1,0:T(8,128)S(1)}, f32[7,8,8,128]{3,2,1,0:T(8,128)S(1)}, f32[8,8,128]{2,1,0:T(8,128)S(1)}, f32[2,8,128]{2,1,0:T(8,128)S(1)}, f32[...) custom-call(s32[3]{0:T(128)S(1)} %pad_add_fusion.pos.refs_0_, f32[24,24]{1,0:T(8,128)S(1)} %copy-done, ...), custom_call_target="tpu_custom_call" | custom-call | tf_op jit(solution)/shard_map/flow/pallas_call | solution.py:597
  17.4 2.0 %collective-permute-start.4 = (f32[2,4,8,128]{3,2,1,0:T(8,128)S(1)}, f32[2,4,8,128]{3,2,1,0:T(8,128)S(1)}, u32[]{:S(2)}, u32[]{:S(2)}) collective-permute-start(f32[2,4,8,128]{3,2,1,0:T(8,128)S(1)} %get-tuple-element.48), channel_id=1, source_target_pairs={{0,2},{1,3},{2,0},{3,1},{4,6},{5,7},{6,4},{7,5},{8,10},{9,11},{10,... | collective-permute-start | bytes 98312 | tf_op jit(solution)/shard_map/ppermute | solution.py:614
  19.4 0.7 %spread.1 = (bf16[192,192]{1,0:T(8,128)(2,1)S(1)}, bf16[192,192]{1,0:T(8,128)(2,1)S(1)}, bf16[128,128]{1,0:T(8,128)(2,1)S(1)}, bf16[128,128]{1,0:T(8,128)(2,1)S(1)}) custom-call(f32[24,24]{1,0:T(8,128)S(1)} %copy-done), custom_call_target="tpu_custom_call" | custom-call | tf_op jit(solution)/shard_map/spread/pallas_call | solution.py:597
  20.1 3.2 %first.1 = (f32[24,8,8,128]{3,2,1,0:T(8,128)S(1)}, f32[24,8,8,128]{3,2,1,0:T(8,128)S(1)}, f32[8,8,128]{2,1,0:T(8,128)S(1)}) custom-call(s32[3]{0:T(128)S(1)} %pad_add_fusion.pos.refs_0_, f32[24,8,8,128]{3,2,1,0:T(8,128)S(1)} %get-tuple-element.27.c.refs_4_, f32[8,8,128]{2,1,0:T(8,128)S(1)} %get-tuple-element.30.refs_6_.edges, ...), custom_call_target="tpu_custom_call" | custom-call | tf_op jit(solution)/shard_map/first/pallas_call | solution.py:597
  23.3 0.0 collective-permute-done.4.refs_8_
  23.3 3.1 %last.1 = (f32[4,8,256]{2,1,0:T(8,128)}, f32[4,8,256]{2,1,0:T(8,128)}, f32[4,8,256]{2,1,0:T(8,128)}, f32[4,8,256]{2,1,0:T(8,128)}, f32[24,8,8,128]{3,2,1,0:T(8,128)}) custom-call(s32[3]{0:T(128)S(1)} %pad_add_fusion.pos.refs_0_, f32[24,8,8,128]{3,2,1,0:T(8,128)S(1)} %get-tuple-element.43.refs_1_, f32[24,8,8,128]{3,2,1,0:T(8,128)S(1)} %get-tuple-element.44.refs_2_, ...), custom_call_target="tpu_custom_call" | custom-call | tf_op jit(solution)/shard_map/last/pallas_call | solution.py:597
Async XLA Ops:
  0.7 5.1 %copy-start = (f32[24,24]{1,0:T(8,128)S(1)}, f32[24,24]{1,0:T(8,128)}, u32[]{:S(2)}) copy-start(f32[24,24]{1,0:T(8,128)} %rates.3) | copy-start | bytes 6916
  2.7 3.1 %collective-permute-start = (f32[66,8,128]{2,1,0:T(8,128)S(1)}, f32[66,8,128]{2,1,0:T(8,128)S(1)}, u32[]{:S(2)}, u32[]{:S(2)}) collective-permute-start(f32[66,8,128]{2,1,0:T(8,128)S(1)} %get-tuple-element.29), channel_id=1, source_target_pairs={{0,1},{1,0},{2,3},{3,2},{4,5},{5,4},{6,7},{7,6},{8,9},{9,8},{10,11... | collective-permute-start | bytes 811016 | tf_op jit(solution)/shard_map/ppermute | solution.py:614
  3.2 7.0 %collective-permute-start.1 = (f32[66,8,128]{2,1,0:T(8,128)S(1)}, f32[66,8,128]{2,1,0:T(8,128)S(1)}, u32[]{:S(2)}, u32[]{:S(2)}) collective-permute-start(f32[66,8,128]{2,1,0:T(8,128)S(1)} %get-tuple-element.33), channel_id=1, source_target_pairs={{0,2},{1,4},{2,0},{3,6},{4,1},{5,8},{6,3},{7,10},{8,5},{9,12},{10,... | collective-permute-start | bytes 811016 | tf_op jit(solution)/shard_map/ppermute | solution.py:614
  7.4 6.8 %collective-permute-start.2 = (f32[35,8,128]{2,1,0:T(8,128)S(1)}, f32[35,8,128]{2,1,0:T(8,128)S(1)}, u32[]{:S(2)}, u32[]{:S(2)}) collective-permute-start(f32[35,8,128]{2,1,0:T(8,128)S(1)} %get-tuple-element.34), channel_id=1, source_target_pairs={{0,2},{1,3},{2,0},{3,1},{4,6},{5,7},{6,4},{7,5},{8,10},{9,11},{10,... | collective-permute-start | bytes 430088 | tf_op jit(solution)/shard_map/ppermute | solution.py:614
  9.0 5.3 %collective-permute-start.3 = (f32[10,8,128]{2,1,0:T(8,128)S(1)}, f32[10,8,128]{2,1,0:T(8,128)S(1)}, u32[]{:S(2)}, u32[]{:S(2)}) collective-permute-start(f32[10,8,128]{2,1,0:T(8,128)S(1)} %get-tuple-element.35), channel_id=1, source_target_pairs={{0,2},{1,6},{2,0},{3,4},{4,3},{5,10},{6,1},{7,8},{8,7},{9,14},{10,... | collective-permute-start | bytes 122888 | tf_op jit(solution)/shard_map/ppermute | solution.py:614
  17.4 5.9 %collective-permute-start.4 = (f32[2,4,8,128]{3,2,1,0:T(8,128)S(1)}, f32[2,4,8,128]{3,2,1,0:T(8,128)S(1)}, u32[]{:S(2)}, u32[]{:S(2)}) collective-permute-start(f32[2,4,8,128]{3,2,1,0:T(8,128)S(1)} %get-tuple-element.48), channel_id=1, source_target_pairs={{0,2},{1,3},{2,0},{3,1},{4,6},{5,7},{6,4},{7,5},{8,10},{9,11},{10,... | collective-permute-start | bytes 98312 | tf_op jit(solution)/shard_map/ppermute | solution.py:614

commit v3 on v2

v3 whole, which is shorter than its diff:
```python
import functools

import jax
import jax.numpy as jnp
from jax import lax
from jax.experimental import pallas as pl
from jax.experimental.pallas import tpu as pltpu
from jax.sharding import PartitionSpec as P

ROWS = 8
LANES = 128
LEVELS = 8
CORES = 2
FIELDS = 4
NEAR = 4

RING_ROWS = 2 * ROWS
RING_COLS = 2 * LANES


def iota(shape, dim):
    return lax.broadcasted_iota(jnp.int32, shape, dim)


def roll(q, shift, axis):
    return pltpu.roll(q, shift % q.shape[axis], axis)


def position():
    lat, lon, role = lax.axis_index("lat"), lax.axis_index("lon"), lax.axis_index("role")
    return lat * CORES + role, lon, role


def block_of(m):
    return pl.ds(pl.multiple_of(m * LANES, LANES), LANES)


def packed(tracers, rates, tiles):
    lane = iota((ROWS, LANES), 1)
    zero = jnp.zeros((ROWS, LANES), jnp.float32)
    total, edge = [zero] * len(tiles), [zero] * len(tiles)
    for b in range(tracers):
        rate = jnp.broadcast_to(rates[:1, b : b + 1], (ROWS, LANES))
        mine = lane // 4 == b
        for i, get in enumerate(tiles):
            q = get(b)
            total[i] = total[i] + rate * q
            edge[i] = jnp.where(mine, roll(q, 4 * b + 2, 1), edge[i])
    mine = lane // 4 == tracers
    return total, [jnp.where(mine, roll(t, 4 * tracers + 2, 1), e) for t, e in zip(total, edge)]


def last_rows(tiles):
    u, v, t, h = tiles
    sub = iota((ROWS, LANES), 0)
    low = jnp.where(sub >= 1, roll(t, -5, 0), roll(h, 1, 0))
    return jnp.where(sub >= 5, v, jnp.where(sub >= 3, roll(u, -3, 0), low))


def first_rows(tiles):
    u, v, t, h = tiles
    sub = iota((ROWS, LANES), 0)
    high = jnp.where(sub <= 6, roll(t, 5, 0), roll(h, -1, 0))
    return jnp.where(sub <= 2, v, jnp.where(sub <= 4, roll(u, 3, 0), high))


def next_rows(south, north, field):
    shift = (3, 0, 5, -1)[field]
    if shift:
        south, north = roll(south, shift, 0), roll(north, -shift, 0)
    return jnp.where(iota((ROWS, LANES), 0) >= ROWS // 2, south, north)


def sides_of(get, amount, east, west):
    lane = iota((ROWS, LANES), 1)
    sides = jnp.zeros((ROWS, LANES), jnp.float32)
    for i in range(amount):
        side = jnp.where(lane < LANES // 2, get(i, east), get(i, west))
        sides = jnp.where(lane // (2 * NEAR) == i, roll(side, 2 * NEAR * i + NEAR, 1), sides)
    return sides


def load_kernel(n, u, v, t, h, count, rates, c, f_out, c_out, d_out, rates_out, z_out, r_out, *refs):
    x_outs, xz_outs = refs[: n - 1], refs[n - 1 : 2 * (n - 1)]
    f_sem, c_sem = refs[2 * (n - 1) :]
    tracers, share = c.shape[0], f_out.shape[1]
    _, lon, role = position()
    upper = role == 1
    copies = [pltpu.make_async_copy(ref, f_out.at[i], f_sem.at[i]) for i, ref in enumerate((u, v, t, h))]
    copies.append(pltpu.make_async_copy(count, d_out, f_sem.at[FIELDS]))
    copies.append(pltpu.make_async_copy(rates, rates_out, f_sem.at[FIELDS + 1]))
    batch = tracers // c_sem.shape[0]
    c_copies = []
    for i in range(c_sem.shape[0]):
        part = pl.ds(i * batch, batch)
        c_copies.append(pltpu.make_async_copy(c.at[part], c_out.at[part], c_sem.at[i]))
    for copy in copies + c_copies:
        copy.start()
    for copy in copies:
        copy.wait()

    def whole(i, block):
        return f_out[i // share, i % share, :, block_of(block)]

    def strips_of(level, block):
        tiles = [whole(field * share + level, block) for field in range(FIELDS)]
        top, bottom = last_rows(tiles), first_rows(tiles)
        return jnp.where(upper, top, bottom), jnp.where(upper, bottom, top)

    count_f = FIELDS * share
    for level in range(share):
        for block in range(n):
            z_out[level * n + block], r_out[level * n + block] = strips_of(level, block)
    base = LEVELS
    for block in range(n):
        depth = d_out[:, block * LANES : (block + 1) * LANES].astype(jnp.float32)
        z_out[base + block] = depth
        r_out[base + block] = depth
    base += n
    for s, (x_out, xz_out) in enumerate(zip(x_outs, xz_outs)):
        m = lax.rem(lon + (s + 1), n)
        e, w = lax.rem(m + 1, n), lax.rem(m + n - 1, n)

        for i in range(count_f):
            x_out[i] = whole(i, m)
        for level in range(share):
            xz_out[level] = z_out[level * n + m]
        x_out[count_f] = sides_of(whole, count_f, e, w)
        xz_out[share] = sides_of(lambda level, block: z_out[level * n + block], share, e, w)
    for i, copy in enumerate(c_copies):
        copy.wait()
        for b in range(i * batch, (i + 1) * batch):
            for far in range(2):
                bottom, top = c_out[b, :, far, :], c_out[b, :, ROWS - 1 - far, :]
                z_out[base + 2 * b + far] = jnp.where(upper, top, bottom)
                r_out[base + 2 * b + far] = jnp.where(upper, bottom, top)
    _, corner = packed(tracers, rates_out, [lambda b: z_out[base + 2 * b]])
    for xz_out in xz_outs:
        xz_out[share + 1] = corner[0]


def pack_kernel(n, rates, c, r, sums, edges, *outs):
    tracers = c.shape[0]
    _, lon, _ = position()
    base = LEVELS + n
    tiles = [lambda b, k=k: c[b, k] for k in range(LEVELS)] + [lambda b: r[base + 2 * b]]
    total, edge = packed(tracers, rates, tiles)
    for k in range(LEVELS):
        sums[k], edges[k] = total[k], edge[k]
    low = iota((ROWS, LANES), 1) % 4 < 2
    share = LEVELS // n

    for s, out in enumerate(outs):
        m = lax.rem(lon + (s + 1), n)
        to_east = m > lon
        for level in range(share):
            out[LEVELS // 2 + 1 + level] = r[level * n + m]
        e, w = lax.rem(m + 1, n), lax.rem(m + n - 1, n)
        out[LEVELS // 2 + 1 + share] = sides_of(lambda level, block: r[level * n + block], share, e, w)
        for i in range(LEVELS // 2):
            a, b = (jnp.where(to_east, q, roll(q, -2, 1)) for q in (edge[2 * i], edge[2 * i + 1]))
            out[i] = jnp.where(low, a, roll(b, 2, 1))
        out[LEVELS // 2] = edge[LEVELS]


def split(q):
    high = q.astype(jnp.bfloat16)
    return high, (q - high.astype(jnp.float32)).astype(jnp.bfloat16)


def spread_kernel(rates, m_all, e_all):
    tracers = rates.shape[0]
    exact = functools.partial(jnp.dot, precision=lax.Precision.HIGHEST, preferred_element_type=jnp.float32)
    for group, transposed, size, out in ((ROWS, False, m_all.shape[0], m_all), (4, True, e_all.shape[1], e_all)):
        rows = (iota((size, tracers), 0) // group == iota((size, tracers), 1)).astype(jnp.float32)
        cols = (iota((tracers, size), 1) // group == iota((tracers, size), 0)).astype(jnp.float32)
        wide = exact(exact(rows, rates[...].T if transposed else rates[...]), cols)
        same = iota((size, size), 0) % group == iota((size, size), 1) % group
        high, low = split(jnp.where(same, wide, 0.0))
        out[...] = jnp.concatenate([high, high, low], axis=0 if transposed else 1)


def stacked(q, axis):
    high, low = split(q)
    return jnp.concatenate([high, low, high], axis=axis)


def product(left, right):
    return jnp.dot(left, right, preferred_element_type=jnp.float32)


class Halo:
    def __init__(self, pos, strips):
        self.upper = pos[2] == 1
        end = jnp.logical_or(
            jnp.logical_and(pos[0] == 0, jnp.logical_not(self.upper)),
            jnp.logical_and(pos[0] == strips - 1, self.upper),
        )
        self.keep_z = jnp.where(end, 0.0, 1.0)
        self.from_r = (iota((ROWS, LANES), 0) >= ROWS // 2) == self.upper

    def rows(self, r, z):
        return jnp.where(self.from_r, r, z * self.keep_z)

    def sides(self, r, z):
        z = z * self.keep_z
        return jnp.where(self.upper, r, z), jnp.where(self.upper, z, r)


def flow_kernel(n, strips, *refs):
    rates, f, count, c, sums, m_all, e_all, z, r = refs[:9]
    del m_all, e_all
    pos = position()
    others = n - 1
    xs, xzs, x2s = (refs[9 + i * others : 9 + (i + 1) * others] for i in range(3))
    coef1, coef2, ends, rims, f_out = refs[9 + 3 * others : 14 + 3 * others]
    heats = refs[14 + 3 * others : 14 + 4 * others]
    dyn, mix, depth, all_edges, all_rims, out, light_out = refs[14 + 4 * others :]
    tracers, share = c.shape[0], f.shape[1]
    strip, lon = pos[0], pos[1]
    halo = Halo(pos, strips)
    lane = iota((ROWS, LANES), 1)
    first, second = slice(0, LANES), slice(LANES, RING_COLS)
    own_rows, far_rows = slice(0, ROWS), slice(ROWS, RING_ROWS)
    base = LEVELS + n
    half = ROWS // 2

    def beside(m):
        return lax.rem(m + 1, n), lax.rem(m + n - 1, n)

    def window(main, near, m):
        east, west = beside(m)

        def side(g):
            return g(east) if n == 2 else jnp.where(lane < LANES // 2, g(east), g(west))

        return main(m), side(main), near(m), side(near)

    def put(ref, at, tiles):
        for tile, (rows, cols) in zip(
            tiles, ((own_rows, first), (own_rows, second), (far_rows, first), (far_rows, second))
        ):
            ref[(*at, rows, cols)] = tile

    def own_window(field, level, m):
        def near(block):
            return next_rows(*halo.sides(r[level * n + block], z[level * n + block]), field)

        return window(lambda block: f[field, level, :, block_of(block)], near, m)

    for field in range(FIELDS):
        for level in range(share):
            put(dyn, (field, lon * share + level), own_window(field, level, lon))

    def depth_window(m):
        return window(
            lambda block: count[:, block_of(block)].astype(jnp.float32),
            lambda block: halo.rows(r[LEVELS + block], z[LEVELS + block]),
            m,
        )

    put(depth, (), depth_window(lon))

    sides = FIELDS * share
    low = LEVELS // 2 + 1
    for s, (x, xz, x2) in enumerate(zip(xs, xzs, x2s)):
        m = lax.rem(lon + (n - 1 - s), n)
        for level in range(share):
            shift = -(2 * NEAR * level + NEAR)
            near = halo.sides(x2[low + level], xz[level])
            corners = halo.sides(roll(x2[low + share], shift, 1), roll(xz[share], shift, 1))
            for field in range(FIELDS):
                i = field * share + level
                put(
                    dyn,
                    (field, m * share + level),
                    (
                        x[i],
                        roll(x[sides], -(2 * NEAR * i + NEAR), 1),
                        next_rows(*near, field),
                        next_rows(*corners, field),
                    ),
                )
        all_edges[m] = x2[: LEVELS // 2]
        all_rims[m, 0], all_rims[m, 1] = halo.sides(x2[low - 1], xz[share + 1])

    east, west = beside(lon)
    easterly = lane % 4 >= 2
    exists = jnp.where(easterly, jnp.where(lon < n - 1, 1.0, 0.0), jnp.where(lon > 0, 1.0, 0.0))
    for k in range(LEVELS):
        e, w = all_edges[east, k // 2], all_edges[west, k // 2]
        if k % 2:
            w = roll(w, -2, 1)
        else:
            e = roll(e, 2, 1)
        ends[k] = jnp.where(easterly, e, w) * exists
    for side in range(2):
        rims[side] = jnp.where(easterly, all_rims[east, side], all_rims[west, side]) * exists

    mix[0, :, own_rows, first] = c[0]
    mix[1, :, own_rows, first] = sums[...]
    for i, b in enumerate((0, tracers)):
        for k in range(LEVELS):
            mix[i, k, own_rows, second] = roll(ends[k], -(4 * b + 2), 1)
        for side, place in enumerate((RING_ROWS - 1, ROWS)):
            mix[i, :, place, second] = roll(rims[side], -(4 * b + 2), 1)
    for far in range(2):
        total = [jnp.zeros((LEVELS, LANES), jnp.float32)] * 2
        for b in range(tracers):
            rows = halo.sides(r[base + 2 * b + far], z[base + 2 * b + far])
            if b == 0:
                chl = rows
            rate = jnp.broadcast_to(rates[:1, b : b + 1], (ROWS, LANES))
            total = [a + rate * q for a, q in zip(total, rows)]
        for i, rows in enumerate((chl, total)):
            mix[i, :, RING_ROWS - 1 - far, first] = rows[0]
            mix[i, :, ROWS + far, first] = rows[1]

    wide = (RING_ROWS, RING_COLS)
    ring_row, ring_col = iota(wide, 0), iota(wide, 1)
    row = strip * ROWS + jnp.where(ring_row < ROWS + half, ring_row, ring_row - RING_ROWS)
    fcor = 2.0 * (row.astype(jnp.float32) + 0.5) / (strips * ROWS) - 1.0

    def north(q):
        return roll(q, -1, 0)

    def south(q):
        return roll(q, 1, 0)

    def around(m):
        e, w = beside(m)
        block = jnp.where(ring_col < LANES, m, jnp.where(ring_col < LANES + LANES // 2, e, w))
        col = block * LANES + ring_col % LANES
        not_last, not_first = col < n * LANES - 1, col > 0
        return (
            lambda q: jnp.where(not_last, roll(q, -1, 1), 0.0),
            lambda q: jnp.where(not_first, roll(q, 1, 1), 0.0),
        )

    def masks(k, counts, east):
        wet = jnp.where(counts > k.astype(jnp.float32), 1.0, 0.0)
        return wet, wet * east(wet), wet * north(wet)

    def advance(uu, vv, tt, wets, east, west):
        wet, wet_u, wet_v = wets

        def lap(q, e, nn):
            return e + west(q) + nn + south(q) - 4.0 * q

        te, tn = east(tt), north(tt)
        u_new = wet_u * (uu + 0.1 * lap(uu, east(uu), north(uu)) + 0.3 * fcor * vv - 0.2 * (te - tt))
        v_new = wet_v * (vv + 0.1 * lap(vv, east(vv), north(vv)) - 0.3 * fcor * uu - 0.2 * (tn - tt))
        return u_new, v_new, wet * (tt + 0.1 * lap(tt, te, tn))

    def coefficients(uu, vv, uw, vs):
        a0 = 1.0 - 0.5 * (
            (jnp.maximum(uu, 0.0) - jnp.minimum(uw, 0.0)) + (jnp.maximum(vv, 0.0) - jnp.minimum(vs, 0.0))
        )
        return (
            a0,
            -0.5 * jnp.minimum(uu, 0.0),
            0.5 * jnp.maximum(uw, 0.0),
            -0.5 * jnp.minimum(vv, 0.0),
            0.5 * jnp.maximum(vs, 0.0),
        )

    east_of, west_of = around(lon)

    def one_level(k, carry):
        tau1, top1, tau2, top2 = carry
        wets = masks(k, depth[...], east_of)
        wet = wets[0]
        heat0 = dyn[3, k]
        uu, vv, tt = advance(dyn[0, k], dyn[1, k], dyn[2, k], wets, east_of, west_of)
        tt = tt + 0.5 * (wet * heat0)
        stencil = coefficients(uu, vv, west_of(uu), south(vv))

        def advect(q):
            a0, ae, aw, an, a_s = stencil
            return a0 * q + (ae * east_of(q) + aw * west_of(q)) + (an * north(q) + a_s * south(q))

        moved = advect(mix[0, k])
        tau1 = tau1 + (0.1 + 0.3 * jnp.maximum(moved, 0.0))
        below = jnp.exp(-tau1)
        half_wet = 0.5 * wet
        warm = half_wet * (2.0 * (top1 - below))
        light = half_wet * top1
        for i, q in enumerate((*stencil, wet, light)):
            coef1[i, k] = q
        chl = wet * moved + light * advect(mix[1, k])
        top1 = below

        uu, vv, tt = advance(uu, vv, tt, wets, east_of, west_of)
        inner = (own_rows, first)
        own = [q[inner] for q in coefficients(uu, vv, west_of(uu), south(vv))]
        moved = (
            own[0] * chl[inner]
            + (own[1] * east_of(chl)[inner] + own[2] * west_of(chl)[inner])
            + (own[3] * north(chl)[inner] + own[4] * south(chl)[inner])
        )
        tau2 = tau2 + (0.1 + 0.3 * jnp.maximum(moved, 0.0))
        below = jnp.exp(-tau2)
        for i, q in enumerate((*own, wet[inner], half_wet[inner] * top2)):
            coef2[i, k] = q
        light_out[0, k] = warm[inner]
        light_out[1, k] = 2.0 * wet[inner] * (top2 - below)
        out[0, k], out[1, k], out[2, k] = uu[own_rows], vv[own_rows], tt[own_rows]
        return tau1, top1, tau2, below

    big = jnp.zeros(wide, jnp.float32)
    small = jnp.zeros((ROWS, LANES), jnp.float32)
    lax.fori_loop(0, LEVELS, one_level, (big, big + 1.0, small, small + 1.0), unroll=2)

    here = block_of(lon)
    for level in range(share):
        k = lon * share + level
        for i in range(3):
            q = out[i, k, :, first]
            f_out[i, level, :, here] = q + light_out[0, k] if i == 2 else q
            if n == 2:
                f_out[i, level, :, block_of(1 - lon)] = out[i, k, :, second]
        f_out[3, level, :, here] = light_out[1, k]
    for s, heat in enumerate(heats):
        m = lax.rem(lon + (s + 1), n)
        for i in range(2):
            heat[i] = light_out[i, pl.ds(m * share, share)]

    if n > 2:

        def other_block(s, carry):
            m = lax.rem(lon + s, n)
            e, w = around(m)
            put(depth, (), depth_window(m))
            for level in range(share):
                k = lon * share + level
                wets = masks(k, depth[...], e)
                for field in range(FIELDS):
                    put(dyn, (field, k), own_window(field, level, m))
                uu, vv, tt = advance(dyn[0, k], dyn[1, k], dyn[2, k], wets, e, w)
                tt = tt + 0.5 * (wets[0] * dyn[3, k])
                for i, q in enumerate(advance(uu, vv, tt, wets, e, w)):
                    f_out[i, level, :, block_of(m)] = q[own_rows, first]
            return carry

        lax.fori_loop(1, n, other_block, 0)


def tile_stencil(q, rim, columns, stencil, sub, lane):
    a0, ae, aw, an, a_s = stencil
    e = jnp.where(lane == LANES - 1, columns, roll(q, -1, 1))
    w = jnp.where(lane == 0, columns, roll(q, 1, 1))
    up = jnp.where(sub == ROWS - 1, rim, roll(q, -1, 0))
    down = jnp.where(sub == 0, rim, roll(q, 1, 0))
    return a0 * q + (ae * e + aw * w) + (an * up + a_s * down)


def swapped(q):
    return jnp.where(iota(q.shape, 1) % 4 == 1, roll(q, -1, 1), roll(q, 1, 1))


def beside_columns(edge, b):
    return roll(edge, LANES - 2 - 4 * b, 1)


def part_of(b, half):
    return slice(b * ROWS, (b + 1) * ROWS), slice(half * LANES, (half + 1) * LANES)


def tile_loop(pairs, source, rims, edge, coef, m_all, adv, store):
    tracers = source.shape[0]
    sub, lane = iota((ROWS, LANES), 0), iota((ROWS, LANES), 1)
    for i in pairs:
        for half in range(2):
            k = 2 * i + half
            stencil = [coef(j, k) for j in range(5)]
            columns = edge[k]
            for b in range(tracers):
                adv[(i, *part_of(b, half))] = tile_stencil(
                    source[b, k], rims[b, k], beside_columns(columns, b), stencil, sub, lane
                )
        react = product(m_all[...], stacked(adv[i], 0))
        for half in range(2):
            k = 2 * i + half
            wet, light = coef(5, k), coef(6, k)
            for b in range(tracers):
                store(b, k, wet * adv[(i, *part_of(b, half))] + light * react[part_of(b, half)])
        yield i


def tracer_kernel(
    n, strips, c, edges, ends, rims, coef, coef2, m_all, e_all, z, r, done, c_out, row1, edge1, row0, edge0, adv, adv2
):
    pos = position()
    tracers = c.shape[0]
    lon = pos[1]
    halo = Halo(pos, strips)
    sub, lane = iota((ROWS, LANES), 0), iota((ROWS, LANES), 1)
    easterly = lane % 4 >= 2
    base = LEVELS + n

    rim = row0.at[0]
    rim[:, 0, :] = rims[0]
    rim[:, ROWS - 1, :] = rims[1]
    parts = []
    for k in range(LEVELS):
        q, inside = ends[k], edges[k]
        outer = jnp.where(easterly, roll(q, -1, 1), roll(q, 1, 1))
        inner = jnp.where(easterly, roll(inside, 1, 1), roll(inside, -1, 1))
        up = jnp.where(sub == ROWS - 1, rim[k], roll(q, -1, 0))
        down = jnp.where(sub == 0, rim[k], roll(q, 1, 0))

        def at_edge(i):
            side = coef[i, k, :ROWS, LANES:]
            return (
                jnp.broadcast_to(side[:, :1], (ROWS, LANES)),
                jnp.broadcast_to(side[:, LANES - 1 :], (ROWS, LANES)),
            )

        def pick(pair):
            return jnp.where(easterly, pair[0], pair[1])

        a0, ae, aw, an, a_s, wet, light = (at_edge(i) for i in range(7))
        moved = (
            pick(a0) * q
            + (pick((ae[0], aw[1])) * outer + pick((aw[0], ae[1])) * inner)
            + (pick(an) * up + pick(a_s) * down)
        )
        parts.append((moved, pick(wet), pick(light)))
        edge0[k] = swapped(q)
    react = product(stacked(jnp.concatenate([p[0] for p in parts], axis=0), 1), e_all[...])
    east_exists = jnp.where(lon < n - 1, 1.0, 0.0)
    west_exists = jnp.where(lon > 0, 1.0, 0.0)
    exists = jnp.where(easterly, east_exists, west_exists)
    for k, (q, wet, light) in enumerate(parts):
        edge1[k] = swapped((wet * q + light * react[k * ROWS : (k + 1) * ROWS]) * exists)

    places = ((0, RING_ROWS - 1), (ROWS - 1, ROWS))
    corners = [swapped(rims[side]) for side in range(2)]
    stencils = [[coef[i, :, place, :LANES] for i in range(7)] for _, place in places]
    for b in range(tracers):
        near = halo.sides(r[base + 2 * b], z[base + 2 * b])
        far = halo.sides(r[base + 2 * b + 1], z[base + 2 * b + 1])
        for side, (at, _) in enumerate(places):
            a0, ae, aw, an, a_s, _, _ = stencils[side]
            q = near[side]
            row0[b, :, at, :] = q
            columns = beside_columns(corners[side], b)
            e = jnp.where(lane == LANES - 1, columns, roll(q, -1, 1))
            w = jnp.where(lane == 0, columns, roll(q, 1, 1))
            inner = c[b, :, at, :]
            up, down = (inner, far[side]) if side == 0 else (far[side], inner)
            adv[(LEVELS // 2, *part_of(b, side))] = a0 * q + (ae * e + aw * w) + (an * up + a_s * down)
    react = product(m_all[...], stacked(adv[LEVELS // 2], 0))
    for b in range(tracers):
        for side, (at, _) in enumerate(places):
            wet, light = stencils[side][5:]
            row1[b, :, at, :] = wet * adv[(LEVELS // 2, *part_of(b, side))] + light * react[part_of(b, side)]

    def store(b, k, q):
        c_out[b, k] = q

    def store_done(b, k, q):
        done[b, k] = q

    pairs = range(LEVELS // 2)
    for _ in tile_loop(pairs, c, row0, edge0, lambda i, k: coef[i, k, :ROWS, :LANES], m_all, adv, store):
        pass
    pairs = range(done.shape[1] // 2)
    for _ in tile_loop(pairs, c_out, row1, edge1, lambda i, k: coef2[i, k], m_all, adv2, store_done):
        pass


def last_kernel(n, *refs):
    others = n - 1
    c, f = refs[:2]
    heats = refs[2 : 2 + others]
    u_out, v_out, t_out, h_out, c_out = refs[2 + others : 7 + others]
    warm, sem, c_sem = refs[7 + others :]
    share = f.shape[1]
    _, lon, _ = position()
    batch = c.shape[0] // c_sem.shape[0]
    copies = []
    for i in range(c_sem.shape[0]):
        part = pl.ds(i * batch, batch)
        copies.append(pltpu.make_async_copy(c.at[part], c_out.at[part], c_sem.at[i]))
    copies += [pltpu.make_async_copy(f.at[i], ref, sem.at[i]) for i, ref in enumerate((u_out, v_out))]
    for copy in copies:
        copy.start()
    here = block_of(lon)
    for level in range(share):
        warm[0, level, :, here] = f[2, level, :, here]
        warm[1, level, :, here] = f[3, level, :, here]
        for s, heat in enumerate(heats):
            there = block_of(lax.rem(lon + (n - 1 - s), n))
            warm[0, level, :, there] = f[2, level, :, there] + heat[0, level]
            warm[1, level, :, there] = heat[1, level]
    copies += [pltpu.make_async_copy(warm.at[i], ref, sem.at[2 + i]) for i, ref in enumerate((t_out, h_out))]
    for copy in copies[-2:]:
        copy.start()
    for copy in copies:
        copy.wait()


def shards(groups, n, lats, u, v, t, h, c, count, rates):
    tracers = c.shape[0]
    share, width = u.shape[0], u.shape[2]
    strips = lats * CORES
    vmem = pl.BlockSpec(memory_space=pltpu.VMEM)
    anywhere = pl.BlockSpec(memory_space=pl.ANY)
    hbm = pl.BlockSpec(memory_space=pltpu.HBM)
    params = pltpu.CompilerParams(vmem_limit_bytes=32 * 1024 * 1024)
    dma = pltpu.SemaphoreType.DMA

    def shape(*dims, dtype=jnp.float32):
        return jax.ShapeDtypeStruct(dims, dtype)

    def tiles(*dims):
        return shape(*dims, ROWS, LANES)

    def scratch(*dims):
        return pltpu.VMEM(dims, jnp.float32)

    def call(kernel, name, args, in_specs, out_shape, out_specs=None, scratch_shapes=()):
        return pl.pallas_call(
            kernel,
            out_shape=tuple(out_shape),
            in_specs=in_specs,
            out_specs=out_specs or (vmem,) * len(out_shape),
            scratch_shapes=scratch_shapes,
            compiler_params=params,
            name=name,
        )(*args)

    def permute(q, target):
        pairs = []
        for g in range(groups):
            for a in range(lats):
                for o in range(n):
                    for i in range(CORES):
                        g2, a2, o2, i2 = target(g, a, o, i)
                        pairs.append(
                            (((g * lats + a) * n + o) * CORES + i, ((g2 * lats + a2) * n + o2) * CORES + i2)
                        )
        return lax.ppermute(q, ("grp", "lat", "lon", "role"), pairs)

    def z_target(shift):
        def target(g, a, o, i):
            s = a * CORES + i + (1 if i else -1)
            if 0 <= s < strips:
                return g, s // CORES, (o + shift) % n, s % CORES
            return (g ^ 1 if g ^ 1 < groups else g), a, o, i

        return target

    def x_target(shift):
        return lambda g, a, o, i: (g, a, (o + shift) % n, i)

    def r_target(g, a, o, i):
        return g, a, o, 1 - i

    shifts = range(1, n)
    z_tiles = LEVELS + n + 2 * tracers
    x_tiles = FIELDS * share + 1
    xz_tiles = share + 2
    f, c_here, depth, rates, z_pay, r_pay, *pays = call(
        functools.partial(load_kernel, n),
        "load",
        [pltpu.with_memory_space_constraint(q, pltpu.HBM) for q in (u, v, t, h, count, rates, c)],
        [hbm] * 7,
        [
            shape(FIELDS, *u.shape),
            shape(*c.shape),
            shape(*count.shape, dtype=jnp.int32),
            shape(*rates.shape),
            tiles(z_tiles),
            tiles(z_tiles),
        ]
        + [tiles(x_tiles)] * (n - 1)
        + [tiles(xz_tiles)] * (n - 1),
        scratch_shapes=[dma((FIELDS + 2,)), dma((4,))],
    )
    r_in = permute(r_pay, r_target)
    z_in = permute(z_pay, z_target(0))
    xs = [permute(q, x_target(s)) for s, q in zip(shifts, pays[: n - 1])]
    xzs = [permute(q, z_target(s)) for s, q in zip(shifts, pays[n - 1 :])]
    sums, edges, *pays = call(
        functools.partial(pack_kernel, n),
        "pack",
        (rates, c_here, r_in),
        [vmem] * 3,
        [tiles(LEVELS)] * 2 + [tiles(LEVELS // 2 + 2 + share)] * (n - 1),
    )
    x2s = [permute(q, x_target(s)) for s, q in zip(shifts, pays)]

    m_size, e_size = tracers * ROWS, LANES
    bf16 = jnp.bfloat16
    m_all, e_all = call(
        spread_kernel,
        "spread",
        (rates,),
        [vmem],
        [shape(m_size, 3 * m_size, dtype=bf16), shape(3 * e_size, e_size, dtype=bf16)],
    )

    args = (rates, f, depth, c_here, sums, m_all, e_all, z_in, r_in, *xs, *xzs, *x2s)
    coef1, coef2, ends, rims, f_new, *heats = call(
        functools.partial(flow_kernel, n, strips),
        "flow",
        args,
        [vmem] * len(args),
        [
            shape(7, LEVELS, RING_ROWS, RING_COLS),
            tiles(7, LEVELS),
            tiles(LEVELS),
            shape(2, LEVELS, LANES),
            shape(FIELDS, *u.shape),
        ]
        + [tiles(2, share)] * (n - 1),
        scratch_shapes=[
            scratch(FIELDS, LEVELS, RING_ROWS, RING_COLS),
            scratch(2, LEVELS, RING_ROWS, RING_COLS),
            scratch(RING_ROWS, RING_COLS),
            scratch(n, LEVELS // 2, ROWS, LANES),
            scratch(n, 2, LEVELS, LANES),
            scratch(3, LEVELS, ROWS, RING_COLS),
            scratch(2, LEVELS, ROWS, LANES),
        ],
    )
    heats = [permute(q, x_target(s)) for s, q in zip(shifts, heats)]
    args = (c_here, edges, ends, rims, coef1, coef2, m_all, e_all, z_in, r_in)
    (c_new,) = call(
        functools.partial(tracer_kernel, n, strips),
        "tracers",
        args,
        [vmem] * len(args),
        [shape(*c.shape)],
        scratch_shapes=[
            scratch(*c.shape),
            scratch(tracers, LEVELS, ROWS, LANES),
            scratch(LEVELS, ROWS, LANES),
            scratch(tracers, LEVELS, ROWS, LANES),
            scratch(LEVELS, ROWS, LANES),
            scratch(LEVELS // 2 + 1, tracers * ROWS, 2 * LANES),
            scratch(LEVELS // 2, tracers * ROWS, 2 * LANES),
        ],
    )
    args = (c_new, f_new, *heats)
    return call(
        functools.partial(last_kernel, n),
        "last",
        args,
        [vmem] * len(args),
        [shape(*u.shape)] * FIELDS + [shape(*c.shape)],
        out_specs=(anywhere,) * 5,
        scratch_shapes=[scratch(2, *u.shape), dma((FIELDS,)), dma((4,))],
    )


def solution(mesh):
    level = P("lon", ("grp", "lat", "role"), None)
    tracer = P(None, None, ("grp", "lat", "role"), "lon")
    return jax.shard_map(
        functools.partial(shards, mesh.shape["grp"], mesh.shape["lon"], mesh.shape["lat"]),
        mesh=mesh,
        in_specs=(level, level, level, level, tracer, P(("grp", "lat", "role"), None), P()),
        out_specs=(level, level, level, level, tracer),
        check_vma=False,
    )
```

time: 26.5 us -> 18.6 us (0.70)
  Pallas kernels: 13.7 us -> 7.93 us
  waiting for transfers between devices: 4.72 us -> 2.22 us
  starting transfers between devices: 7.18 us -> 7.63 us
    pallas_call x6, Pallas kernels: 13.7 us -> 7.93 us  [call(): pl.pallas_call(kernel, out_shape=tuple(out_shape), in_specs=in_specs, out...]
    ppermute x5 -> x6, waiting for transfers between devices: 4.72 us -> 2.22 us  [permute(): return lax.ppermute(q, ('grp', 'lat', 'lon', 'role'), pairs)]
    ppermute x5 -> x6, starting transfers between devices: 7.18 us -> 7.63 us  [permute(): return lax.ppermute(q, ('grp', 'lat', 'lon', 'role'), pairs)]
  transfers between devices with their start and end apart: 5 -> 6, of which waited for: 2 -> 1; matrix products, arithmetic and copies ran while one was open for 0% -> 0% of each run, Pallas kernels for 21% -> 20%
where the time goes in v3:
time: 18.6 us; the launch traced here: 18.5 us
  Pallas kernels  7.93 us (43%)
  starting transfers between devices  7.63 us (41%)
  waiting for transfers between devices  2.22 us (12%)
  between operations  0.68 us (4%)
    pallas_call x6, Pallas kernels, call(): pl.pallas_call(kernel, out_shape=tuple(out_shape), in_specs=in_specs, out...  7.93 us
    ppermute x6, starting transfers between devices, permute(): return lax.ppermute(q, ('grp', 'lat', 'lon', 'role'), pairs)  7.63 us
    ppermute x6, waiting for transfers between devices, permute(): return lax.ppermute(q, ('grp', 'lat', 'lon', 'role'), pairs)  2.22 us
  transfers between devices with their start and end apart: 6, of which 1 were waited for; matrix products, arithmetic and copies ran while one was open for 0% of the time, Pallas kernels for 20%

profile of v3, /device:TPU:0, one launch (start us, length us, event | category | flops | bytes accessed | tf_op | source)
XLA Modules:
  0.0 18.5 jit_solution(7835781458149176806)
XLA Ops:
  0.6 1.7 %load.1 = (f32[4,4,8,256]{3,2,1,0:T(8,128)S(1)}, f32[24,8,8,128]{3,2,1,0:T(8,128)S(1)}, s32[8,256]{1,0:T(8,128)S(1)}, f32[24,24]{1,0:T(8,128)S(1)}, f32[58,8,128...) custom-call(f32[4,8,256]{2,1,0:T(8,128)} %u.1, ...), custom_call_target="tpu_custom_call" | custom-call | tf_op jit(solution)/shard_map/load/pallas_call | solution.py:624
  2.3 0.5 %collective-permute-start = (f32[58,8,128]{2,1,0:T(8,128)S(1)}, f32[58,8,128]{2,1,0:T(8,128)S(1)}, u32[]{:S(2)}, u32[]{:S(2)}) collective-permute-start(f32[58,8,128]{2,1,0:T(8,128)S(1)} %get-tuple-element.26), channel_id=1, source_target_pairs={{0,1},{1,0},{2,3},{3,2},{4,5},{5,4},{6,7},{7,6},{8,9},{9,8},{10,11... | collective-permute-start | bytes 712712 | tf_op jit(solution)/shard_map/ppermute | solution.py:644
  2.8 2.6 %collective-permute-start.1 = (f32[58,8,128]{2,1,0:T(8,128)S(1)}, f32[58,8,128]{2,1,0:T(8,128)S(1)}, u32[]{:S(2)}, u32[]{:S(2)}) collective-permute-start(f32[58,8,128]{2,1,0:T(8,128)S(1)} %get-tuple-element.33), channel_id=1, source_target_pairs={{0,16},{1,4},{2,18},{3,6},{4,1},{5,8},{6,3},{7,10},{8,5},{9,12},{1... | collective-permute-start | bytes 712712 | tf_op jit(solution)/shard_map/ppermute | solution.py:644
  5.4 1.5 %collective-permute-start.2 = (f32[17,8,128]{2,1,0:T(8,128)S(1)}, f32[17,8,128]{2,1,0:T(8,128)S(1)}, u32[]{:S(2)}, u32[]{:S(2)}) collective-permute-start(f32[17,8,128]{2,1,0:T(8,128)S(1)} %get-tuple-element.34), channel_id=1, source_target_pairs={{0,2},{1,3},{2,0},{3,1},{4,6},{5,7},{6,4},{7,5},{8,10},{9,11},{10,... | collective-permute-start | bytes 208904 | tf_op jit(solution)/shard_map/ppermute | solution.py:644
  6.9 0.0 collective-permute-done.r.refs_8_
  6.9 0.5 %pack.1 = (f32[8,8,128]{2,1,0:T(8,128)S(1)}, f32[8,8,128]{2,1,0:T(8,128)S(1)}, f32[10,8,128]{2,1,0:T(8,128)S(1)}) custom-call(f32[24,24]{1,0:T(8,128)S(1)} %get-tuple-element.25.rates.refs_0_, f32[24,8,8,128]{3,2,1,0:T(8,128)S(1)} %get-tuple-element.24.c.refs_3_, f32[58,8,128]{2,1,0:T(8,128)S(1)} %collective-permute-done.r.refs_8_), custom_call_target="tpu_custom_call" | custom-call | tf_op jit(solution)/shard_map/pack/pallas_call | solution.py:624
  7.4 0.6 %collective-permute-start.4 = (f32[10,8,128]{2,1,0:T(8,128)S(1)}, f32[10,8,128]{2,1,0:T(8,128)S(1)}, u32[]{:S(2)}, u32[]{:S(2)}) collective-permute-start(f32[10,8,128]{2,1,0:T(8,128)S(1)} %get-tuple-element.36), channel_id=1, source_target_pairs={{0,2},{1,3},{2,0},{3,1},{4,6},{5,7},{6,4},{7,5},{8,10},{9,11},{10,... | collective-permute-start | bytes 122888 | tf_op jit(solution)/shard_map/ppermute | solution.py:644
  8.0 0.9 %collective-permute-start.3 = (f32[6,8,128]{2,1,0:T(8,128)S(1)}, f32[6,8,128]{2,1,0:T(8,128)S(1)}, u32[]{:S(2)}, u32[]{:S(2)}) collective-permute-start(f32[6,8,128]{2,1,0:T(8,128)S(1)} %get-tuple-element.35), channel_id=1, source_target_pairs={{0,16},{1,6},{2,18},{3,4},{4,3},{5,10},{6,1},{7,8},{8,7},{9,14},{1... | collective-permute-start | bytes 73736 | tf_op jit(solution)/shard_map/ppermute | solution.py:644
  8.9 0.7 %spread.1 = (bf16[192,576]{1,0:T(8,128)(2,1)S(1)}, bf16[384,128]{1,0:T(8,128)(2,1)S(1)}) custom-call(f32[24,24]{1,0:T(8,128)S(1)} %get-tuple-element.25.rates.refs_0_), custom_call_target="tpu_custom_call" | custom-call | tf_op jit(solution)/shard_map/spread/pallas_call | solution.py:624
  9.6 2.2 %collective-permute-done.3.refs_10_ = f32[6,8,128]{2,1,0:T(8,128)S(1)} collective-permute-done((f32[6,8,128]{2,1,0:T(8,128)S(1)}, f32[6,8,128]{2,1,0:T(8,128)S(1)}, u32[]{:S(2)}, u32[]{:S(2)}) %collective-permute-start.3) | collective-permute-done | bytes 24608 | tf_op jit(solution)/shard_map/ppermute | solution.py:644
  11.8 0.0 collective-permute-done.2.refs_9_
  11.8 0.0 collective-permute-done.1.refs_7_.z
  11.8 0.0 collective-permute-done.4.refs_11_
  11.8 1.5 %flow.1 = (f32[7,8,16,256]{3,2,1,0:T(8,128)S(1)}, f32[7,8,8,128]{3,2,1,0:T(8,128)S(1)}, f32[8,8,128]{2,1,0:T(8,128)S(1)}, f32[2,8,128]{2,1,0:T(8,128)S(1)}, f32[...) custom-call(f32[24,24]{1,0:T(8,128)S(1)} %get-tuple-element.25.rates.refs_0_, ...), custom_call_target="tpu_custom_call" | custom-call | tf_op jit(solution)/shard_map/flow/pallas_call | solution.py:624
  13.3 1.6 %collective-permute-start.5 = (f32[2,4,8,128]{3,2,1,0:T(8,128)S(1)}, f32[2,4,8,128]{3,2,1,0:T(8,128)S(1)}, u32[]{:S(2)}, u32[]{:S(2)}) collective-permute-start(f32[2,4,8,128]{3,2,1,0:T(8,128)S(1)} %get-tuple-element.42), channel_id=1, source_target_pairs={{0,2},{1,3},{2,0},{3,1},{4,6},{5,7},{6,4},{7,5},{8,10},{9,11},{10,... | collective-permute-start | bytes 98312 | tf_op jit(solution)/shard_map/ppermute | solution.py:644
  14.9 2.6 %tracers.1.refs_0_ = f32[24,8,8,128]{3,2,1,0:T(8,128)S(1)} custom-call(f32[24,8,8,128]{3,2,1,0:T(8,128)S(1)} %get-tuple-element.24.c.refs_3_, f32[8,8,128]{2,1,0:T(8,128)S(1)} %get-tuple-element.27.edges, f32[8,8,128]{2,1,0:T(8,128)S(1)} %get-tuple-element.37.ends, f32[2,8,128]{2,1,0:T(8,128)S(1)} %get-tuple-element.38.rims, ...), custom_call_target="tpu_custom_call" | custom-call | tf_op jit(solution)/shard_map/tracers/pallas_call | solution.py:624
  17.5 0.0 collective-permute-done.5.refs_2_
  17.5 1.0 %last.1 = (f32[4,8,256]{2,1,0:T(8,128)}, f32[4,8,256]{2,1,0:T(8,128)}, f32[4,8,256]{2,1,0:T(8,128)}, f32[4,8,256]{2,1,0:T(8,128)}, f32[24,8,8,128]{3,2,1,0:T(8,128)}) custom-call(f32[24,8,8,128]{3,2,1,0:T(8,128)S(1)} %tracers.1.refs_0_, f32[4,4,8,256]{3,2,1,0:T(8,128)S(1)} %get-tuple-element.41.refs_1_, f32[2,4,8,128]{3,2,1,0:T(8,128)S(1)} %collective-permute-done.5.refs_2_), custom_call_target="tpu_custom_call" | custom-call | tf_op jit(solution)/shard_map/last/pallas_call | solution.py:624
Async XLA Ops:
  2.3 4.6 %collective-permute-start = (f32[58,8,128]{2,1,0:T(8,128)S(1)}, f32[58,8,128]{2,1,0:T(8,128)S(1)}, u32[]{:S(2)}, u32[]{:S(2)}) collective-permute-start(f32[58,8,128]{2,1,0:T(8,128)S(1)} %get-tuple-element.26), channel_id=1, source_target_pairs={{0,1},{1,0},{2,3},{3,2},{4,5},{5,4},{6,7},{7,6},{8,9},{9,8},{10,11... | collective-permute-start | bytes 712712 | tf_op jit(solution)/shard_map/ppermute | solution.py:644
  2.8 9.0 %collective-permute-start.1 = (f32[58,8,128]{2,1,0:T(8,128)S(1)}, f32[58,8,128]{2,1,0:T(8,128)S(1)}, u32[]{:S(2)}, u32[]{:S(2)}) collective-permute-start(f32[58,8,128]{2,1,0:T(8,128)S(1)} %get-tuple-element.33), channel_id=1, source_target_pairs={{0,16},{1,4},{2,18},{3,6},{4,1},{5,8},{6,3},{7,10},{8,5},{9,12},{1... | collective-permute-start | bytes 712712 | tf_op jit(solution)/shard_map/ppermute | solution.py:644
  5.4 6.4 %collective-permute-start.2 = (f32[17,8,128]{2,1,0:T(8,128)S(1)}, f32[17,8,128]{2,1,0:T(8,128)S(1)}, u32[]{:S(2)}, u32[]{:S(2)}) collective-permute-start(f32[17,8,128]{2,1,0:T(8,128)S(1)} %get-tuple-element.34), channel_id=1, source_target_pairs={{0,2},{1,3},{2,0},{3,1},{4,6},{5,7},{6,4},{7,5},{8,10},{9,11},{10,... | collective-permute-start | bytes 208904 | tf_op jit(solution)/shard_map/ppermute | solution.py:644
  7.4 4.4 %collective-permute-start.4 = (f32[10,8,128]{2,1,0:T(8,128)S(1)}, f32[10,8,128]{2,1,0:T(8,128)S(1)}, u32[]{:S(2)}, u32[]{:S(2)}) collective-permute-start(f32[10,8,128]{2,1,0:T(8,128)S(1)} %get-tuple-element.36), channel_id=1, source_target_pairs={{0,2},{1,3},{2,0},{3,1},{4,6},{5,7},{6,4},{7,5},{8,10},{9,11},{10,... | collective-permute-start | bytes 122888 | tf_op jit(solution)/shard_map/ppermute | solution.py:644
  8.0 3.8 %collective-permute-start.3 = (f32[6,8,128]{2,1,0:T(8,128)S(1)}, f32[6,8,128]{2,1,0:T(8,128)S(1)}, u32[]{:S(2)}, u32[]{:S(2)}) collective-permute-start(f32[6,8,128]{2,1,0:T(8,128)S(1)} %get-tuple-element.35), channel_id=1, source_target_pairs={{0,16},{1,6},{2,18},{3,4},{4,3},{5,10},{6,1},{7,8},{8,7},{9,14},{1... | collective-permute-start | bytes 73736 | tf_op jit(solution)/shard_map/ppermute | solution.py:644
  13.3 4.2 %collective-permute-start.5 = (f32[2,4,8,128]{3,2,1,0:T(8,128)S(1)}, f32[2,4,8,128]{3,2,1,0:T(8,128)S(1)}, u32[]{:S(2)}, u32[]{:S(2)}) collective-permute-start(f32[2,4,8,128]{3,2,1,0:T(8,128)S(1)} %get-tuple-element.42), channel_id=1, source_target_pairs={{0,2},{1,3},{2,0},{3,1},{4,6},{5,7},{6,4},{7,5},{8,10},{9,11},{10,... | collective-permute-start | bytes 98312 | tf_op jit(solution)/shard_map/ppermute | solution.py:644

commit v4 on v3

v4 whole, which is shorter than its diff:
```python
import functools

import jax
import jax.numpy as jnp
from jax import lax
from jax.experimental import pallas as pl
from jax.experimental.pallas import tpu as pltpu
from jax.sharding import PartitionSpec as P

ROWS = 8
LANES = 128
LEVELS = 8
CORES = 2
FIELDS = 4
NEAR = 3

RING_ROWS = 2 * ROWS
RING_COLS = 2 * LANES


def iota(shape, dim):
    return lax.broadcasted_iota(jnp.int32, shape, dim)


def roll(q, shift, axis):
    return pltpu.roll(q, shift % q.shape[axis], axis)


def position():
    lat, lon, role = lax.axis_index("lat"), lax.axis_index("lon"), lax.axis_index("role")
    return lat * CORES + role, lon, role


def block_of(m):
    return pl.ds(pl.multiple_of(m * LANES, LANES), LANES)


def packed(tracers, rates, tiles):
    lane = iota((ROWS, LANES), 1)
    zero = jnp.zeros((ROWS, LANES), jnp.float32)
    total, edge = [zero] * len(tiles), [zero] * len(tiles)
    for b in range(tracers):
        rate = jnp.broadcast_to(rates[:1, b : b + 1], (ROWS, LANES))
        mine = lane // 4 == b
        for i, get in enumerate(tiles):
            q = get(b)
            total[i] = total[i] + rate * q
            edge[i] = jnp.where(mine, roll(q, 4 * b + 2, 1), edge[i])
    mine = lane // 4 == tracers
    return total, [jnp.where(mine, roll(t, 4 * tracers + 2, 1), e) for t, e in zip(total, edge)]


def last_rows(tiles):
    u, v, t, h = tiles
    sub = iota((ROWS, LANES), 0)
    low = jnp.where(sub >= 1, roll(t, -5, 0), roll(h, 1, 0))
    return jnp.where(sub >= 5, v, jnp.where(sub >= 3, roll(u, -3, 0), low))


def first_rows(tiles):
    u, v, t, h = tiles
    sub = iota((ROWS, LANES), 0)
    high = jnp.where(sub <= 6, roll(t, 5, 0), roll(h, -1, 0))
    return jnp.where(sub <= 2, v, jnp.where(sub <= 4, roll(u, 3, 0), high))


def next_rows(south, north, field):
    shift = (3, 0, 5, -1)[field]
    if shift:
        south, north = roll(south, shift, 0), roll(north, -shift, 0)
    return jnp.where(iota((ROWS, LANES), 0) >= ROWS // 2, south, north)


def sides_of(get, amount, east, west, into, start):
    lane = iota((ROWS, LANES), 1)
    for i in range(amount):
        first = start + 2 * NEAR * i
        side = jnp.where(lane < LANES // 2, get(i, east), get(i, west))
        into = jnp.where((lane >= first) & (lane < first + 2 * NEAR), roll(side, first + NEAR, 1), into)
    return into


def side_in(tile, i, start):
    return roll(tile, -(start + 2 * NEAR * i + NEAR), 1)


def load_kernel(n, u, v, t, h, count, rates, c, f_out, c_out, d_out, rates_out, z_out, r_out, f_sem, c_sem):
    tracers, share = c.shape[0], f_out.shape[1]
    _, _, role = position()
    upper = role == 1
    copies = [pltpu.make_async_copy(ref, f_out.at[i], f_sem.at[i]) for i, ref in enumerate((u, v, t, h))]
    copies.append(pltpu.make_async_copy(count, d_out, f_sem.at[FIELDS]))
    copies.append(pltpu.make_async_copy(rates, rates_out, f_sem.at[FIELDS + 1]))
    batch = tracers // c_sem.shape[0]
    c_copies = []
    for i in range(c_sem.shape[0]):
        part = pl.ds(i * batch, batch)
        c_copies.append(pltpu.make_async_copy(c.at[part], c_out.at[part], c_sem.at[i]))
    for copy in copies + c_copies:
        copy.start()
    for copy in copies:
        copy.wait()

    def whole(i, block):
        return f_out[i // share, i % share, :, block_of(block)]

    def strips_of(level, block):
        tiles = [whole(field * share + level, block) for field in range(FIELDS)]
        top, bottom = last_rows(tiles), first_rows(tiles)
        return jnp.where(upper, top, bottom), jnp.where(upper, bottom, top)

    count_f = FIELDS * share
    for level in range(share):
        for block in range(n):
            z_out[level * n + block], r_out[level * n + block] = strips_of(level, block)
    base = LEVELS
    for block in range(n):
        depth = d_out[:, block * LANES : (block + 1) * LANES].astype(jnp.float32)
        z_out[base + block] = depth
        r_out[base + block] = depth
    base += n
    for i, copy in enumerate(c_copies):
        copy.wait()
        for b in range(i * batch, (i + 1) * batch):
            for far in range(2):
                bottom, top = c_out[b, :, far, :], c_out[b, :, ROWS - 1 - far, :]
                z_out[base + 2 * b + far] = jnp.where(upper, top, bottom)
                r_out[base + 2 * b + far] = jnp.where(upper, bottom, top)


def edge_kernel(n, rates, c, sums, edges, *outs):
    _, lon, _ = position()
    total, edge = packed(c.shape[0], rates, [lambda b, k=k: c[b, k] for k in range(LEVELS)])
    for k in range(LEVELS):
        sums[k], edges[k] = total[k], edge[k]
    low = iota((ROWS, LANES), 1) % 4 < 2
    for s, out in enumerate(outs):
        to_east = lax.rem(lon + (s + 1), n) > lon
        for i in range(LEVELS // 2):
            a, b = (jnp.where(to_east, q, roll(q, -2, 1)) for q in (edge[2 * i], edge[2 * i + 1]))
            out[i] = jnp.where(low, a, roll(b, 2, 1))


def join_kernel(n, rates, f, z, r, *refs):
    pays, x_outs, xz_outs = (refs[i * (n - 1) : (i + 1) * (n - 1)] for i in range(3))
    _, lon, _ = position()
    tracers, share, base = rates.shape[0], LEVELS // n, LEVELS + n
    _, (rim_r, rim_z) = packed(tracers, rates, [lambda b: r[base + 2 * b], lambda b: z[base + 2 * b]])
    zero = jnp.zeros((ROWS, LANES), jnp.float32)
    count = FIELDS * share

    def whole(i, block):
        return f[i // share, i % share, :, block_of(block)]

    for s, (pay, x, xz) in enumerate(zip(pays, x_outs, xz_outs)):
        m = lax.rem(lon + (s + 1), n)
        e, w = lax.rem(m + 1, n), lax.rem(m + n - 1, n)
        for i in range(count):
            x[i] = whole(i, m)
        x[count : count + LEVELS // 2] = pay[...]
        end = count + LEVELS // 2
        for level in range(share):
            x[end + level] = r[level * n + m]
            xz[level] = z[level * n + m]
        x[end + share] = rim_r
        sides = sides_of(whole, count, e, w, zero, 0)
        x[end + share + 1] = sides_of(
            lambda level, block: r[level * n + block], share, e, w, sides, 2 * NEAR * count
        )
        xz[share] = sides_of(lambda level, block: z[level * n + block], share, e, w, rim_z, 4 * (tracers + 1))


def split(q):
    high = q.astype(jnp.bfloat16)
    return high, (q - high.astype(jnp.float32)).astype(jnp.bfloat16)


def spread_kernel(rates, m_all, e_all):
    tracers = rates.shape[0]
    for group, transposed, size, out in ((ROWS, False, m_all.shape[0], m_all), (4, True, e_all.shape[1], e_all)):
        rows = (iota((size, tracers), 0) // group == iota((size, tracers), 1)).astype(jnp.bfloat16)
        cols = (iota((tracers, size), 1) // group == iota((tracers, size), 0)).astype(jnp.bfloat16)
        same = iota((size, size), 0) % group == iota((size, size), 1) % group
        parts = []
        for q in split(rates[...].T if transposed else rates[...]):
            wide = product(product(rows, q).astype(jnp.bfloat16), cols)
            parts.append(jnp.where(same, wide, 0.0).astype(jnp.bfloat16))
        high, low = parts
        out[...] = jnp.concatenate([high, high, low], axis=0 if transposed else 1)


def stacked(q, axis):
    high, low = split(q)
    return jnp.concatenate([high, low, high], axis=axis)


def product(left, right):
    return jnp.dot(left, right, preferred_element_type=jnp.float32)


def advected(q, e, w, up, down, stencil):
    a0, mu, pw, mv, ps = stencil
    return (a0 * q + (pw * w - mu * e)) + (ps * down - mv * up)


class Halo:
    def __init__(self, pos, strips):
        self.upper = pos[2] == 1
        end = jnp.logical_or(
            jnp.logical_and(pos[0] == 0, jnp.logical_not(self.upper)),
            jnp.logical_and(pos[0] == strips - 1, self.upper),
        )
        self.keep_z = jnp.where(end, 0.0, 1.0)
        self.from_r = (iota((ROWS, LANES), 0) >= ROWS // 2) == self.upper

    def rows(self, r, z):
        return jnp.where(self.from_r, r, z * self.keep_z)

    def sides(self, r, z):
        z = z * self.keep_z
        return jnp.where(self.upper, r, z), jnp.where(self.upper, z, r)


FIRST, SECOND = slice(0, LANES), slice(LANES, RING_COLS)
OWN_ROWS, FAR_ROWS = slice(0, ROWS), slice(ROWS, RING_ROWS)
WIDE = (RING_ROWS, RING_COLS)


def put(ref, at, tiles):
    places = ((OWN_ROWS, FIRST), (OWN_ROWS, SECOND), (FAR_ROWS, FIRST), (FAR_ROWS, SECOND))
    for tile, (rows, cols) in zip(tiles, places):
        ref[(*at, rows, cols)] = tile


def beside(m, n):
    return lax.rem(m + 1, n), lax.rem(m + n - 1, n)


def north(q):
    return roll(q, -1, 0)


def south(q):
    return roll(q, 1, 0)


def east(q):
    return roll(q, -1, 1)


def west(q):
    return roll(q, 1, 1)


def around(m, n):
    e, w = beside(m, n)
    ring_col = iota(WIDE, 1)
    block = jnp.where(ring_col < LANES, m, jnp.where(ring_col < LANES + LANES // 2, e, w))
    col = block * LANES + ring_col % LANES
    not_last, not_first = col < n * LANES - 1, col > 0
    return lambda q: jnp.where(not_last, east(q), 0.0), lambda q: jnp.where(not_first, west(q), 0.0)


def coriolis(strip, strips):
    ring_row = iota(WIDE, 0)
    row = strip * ROWS + jnp.where(ring_row < ROWS + ROWS // 2, ring_row, ring_row - RING_ROWS)
    return 0.3 * (2.0 * (row.astype(jnp.float32) + 0.5) / (strips * ROWS) - 1.0)


def masks(k, counts, east_of):
    wet = jnp.where(counts > k, 1.0, 0.0)
    return wet, wet * east_of(wet), wet * north(wet)


def advance(uu, vv, tt, wet_u, wet_v, turn, east_of, west_of, again):
    def mixed(q, e, w, nn):
        return 0.6 * q + 0.1 * ((e + w) + (nn + south(q)))

    te, tn = east_of(tt), north(tt)
    u_west = west(uu) if again else west_of(uu)
    u_new = wet_u * (mixed(uu, east(uu), u_west, north(uu)) + (turn * vv - 0.2 * (te - tt)))
    v_new = wet_v * (mixed(vv, east_of(vv), west_of(vv), north(vv)) - (turn * uu + 0.2 * (tn - tt)))
    return u_new, v_new, mixed(tt, te, west_of(tt), tn)


def coefficients(uu, vv):
    uu, vv = 0.5 * uu, 0.5 * vv
    uw, vs = west(uu), south(vv)
    pw, ps = jnp.maximum(uw, 0.0), jnp.maximum(vs, 0.0)
    mu, mv = jnp.minimum(uu, 0.0), jnp.minimum(vv, 0.0)
    a0 = (1.0 - (jnp.maximum(uu, 0.0) - jnp.minimum(uw, 0.0))) - (jnp.maximum(vv, 0.0) - jnp.minimum(vs, 0.0))
    return a0, mu, pw, mv, ps


def two_steps(read, wets, turn, shifts):
    uu, vv, tt = advance(read(0), read(1), read(2), *wets[1:], turn, *shifts, False)
    tt = wets[0] * (tt + 0.5 * read(3))
    stencil = coefficients(uu, vv)
    uu, vv, tt = advance(uu, vv, tt, *wets[1:], turn, *shifts, True)
    return uu, vv, wets[0] * tt, stencil, [q[OWN_ROWS, FIRST] for q in coefficients(uu, vv)]


def own_kernel(n, strips, rates, f, count, c, sums, z, r, coef1, coef2, wets, mix, f_out, dyn, depth):
    tracers, share = c.shape[0], f.shape[1]
    strip, lon, _ = pos = position()
    halo = Halo(pos, strips)
    lane = iota((ROWS, LANES), 1)
    base = LEVELS + n

    def window(main, near, m):
        e, w = beside(m, n)

        def side(g):
            return g(e) if n == 2 else jnp.where(lane < LANES // 2, g(e), g(w))

        return main(m), side(main), near(m), side(near)

    def own_window(field, level, m):
        def near(block):
            return next_rows(*halo.sides(r[level * n + block], z[level * n + block]), field)

        return window(lambda block: f[field, level, :, block_of(block)], near, m)

    def depth_window(m):
        return window(
            lambda block: count[:, block_of(block)].astype(jnp.float32),
            lambda block: halo.rows(r[LEVELS + block], z[LEVELS + block]),
            m,
        )

    put(depth, (), depth_window(lon))
    for field in range(FIELDS):
        for level in range(share):
            put(dyn, (field, level), own_window(field, level, lon))
    turn = coriolis(strip, strips)
    shifts = around(lon, n)
    for k in range(LEVELS):
        for i, q in enumerate(masks(float(k), depth[...], shifts[0])):
            wets[i, k] = q

    def one_level(level, carry):
        wet = [wets[i, lon * share + level] for i in range(3)]
        uu, vv, tt, stencil, stencil2 = two_steps(lambda i: dyn[i, level], wet, turn, shifts)
        for i, q in enumerate(stencil):
            coef1[i, level] = q
        for i, q in enumerate(stencil2):
            coef2[i, level] = q
        for i, q in enumerate((uu, vv, tt)):
            f_out[i, level, :, block_of(lon)] = q[OWN_ROWS, FIRST]
            if n == 2:
                f_out[i, level, :, block_of(1 - lon)] = q[OWN_ROWS, SECOND]
        return carry

    lax.fori_loop(0, share, one_level, 0, unroll=min(2, share))

    mix[0, :, OWN_ROWS] = c[0]
    mix[1, :, OWN_ROWS] = sums[...]
    for far in range(2):
        total = [jnp.zeros((LEVELS, LANES), jnp.float32)] * 2
        for b in range(tracers):
            rows = halo.sides(r[base + 2 * b + far], z[base + 2 * b + far])
            if b == 0:
                chl = rows
            rate = jnp.broadcast_to(rates[:1, b : b + 1], (ROWS, LANES))
            total = [a + rate * q for a, q in zip(total, rows)]
        for i, rows in enumerate((chl, total)):
            mix[i, :, RING_ROWS - 1 - far] = rows[0]
            mix[i, :, ROWS + far] = rows[1]

    if n > 2:

        def other_block(s, carry):
            m = lax.rem(lon + s, n)
            around_m = around(m, n)
            put(depth, (), depth_window(m))
            for level in range(share):
                k = (lon * share + level).astype(jnp.float32)
                for field in range(FIELDS):
                    put(dyn, (field, level), own_window(field, level, m))
                wet = masks(k, depth[...], around_m[0])
                after = two_steps(lambda i, level=level: dyn[i, level], wet, turn, around_m)
                for i, q in enumerate(after[:3]):
                    f_out[i, level, :, block_of(m)] = q[OWN_ROWS, FIRST]
            return carry

        lax.fori_loop(1, n, other_block, 0)


def flow_kernel(n, strips, tracers, *refs):
    own1, own2, wets, mix = refs[:4]
    others = n - 1
    xs, xzs = (refs[6 + i * others : 6 + (i + 1) * others] for i in range(2))
    coef1, coef2, ends, rims, light_out = refs[6 + 2 * others : 11 + 2 * others]
    heats = refs[11 + 2 * others : 11 + 3 * others]
    dyn, side_mix, all_edges, all_rims, moved = refs[11 + 3 * others :]
    share = own1.shape[1]
    strip, lon, _ = pos = position()
    halo = Halo(pos, strips)
    lane = iota((ROWS, LANES), 1)
    turn = coriolis(strip, strips)
    shifts = around(lon, n)
    mine = pl.ds(lon * share, share)
    for i in range(5):
        coef1[i, mine] = own1[i]
        coef2[i, mine] = own2[i]

    fields = FIELDS * share
    end = fields + LEVELS // 2
    last_lane = 4 * (tracers + 1)
    for s, (x, xz) in enumerate(zip(xs, xzs)):
        m = lax.rem(lon + (n - 1 - s), n)
        sides, far_sides = x[end + share + 1], xz[share]
        for level in range(share):
            near = halo.sides(x[end + level], xz[level])
            corners = halo.sides(side_in(sides, level, 2 * NEAR * fields), side_in(far_sides, level, last_lane))
            for field in range(FIELDS):
                i = field * share + level
                put(
                    dyn,
                    (field, s * share + level),
                    (x[i], side_in(sides, i, 0), next_rows(*near, field), next_rows(*corners, field)),
                )
        all_edges[m] = x[fields:end]
        all_rims[m, 0], all_rims[m, 1] = halo.sides(x[end + share], far_sides)

    def other_level(i):
        s, level = i // share, i % share
        k = lax.rem(lon + (n - 1 - s), n) * share + level
        wet = [wets[j, k] for j in range(3)]
        _, _, _, stencil, stencil2 = two_steps(lambda j: dyn[j, i], wet, turn, shifts)
        for j, q in enumerate(stencil):
            coef1[j, k] = q
        for j, q in enumerate(stencil2):
            coef2[j, k] = q

    for i in range(others * share):
        other_level(i)

    east_m, west_m = beside(lon, n)
    easterly = lane % 4 >= 2
    exists = jnp.where(easterly, jnp.where(lon < n - 1, 1.0, 0.0), jnp.where(lon > 0, 1.0, 0.0))
    for k in range(LEVELS):
        e, w = all_edges[east_m, k // 2], all_edges[west_m, k // 2]
        if k % 2:
            w = roll(w, -2, 1)
        else:
            e = roll(e, 2, 1)
        ends[k] = jnp.where(easterly, e, w) * exists
    for side in range(2):
        rims[side] = jnp.where(easterly, all_rims[east_m, side], all_rims[west_m, side]) * exists

    for i, b in enumerate((0, tracers)):
        for k in range(LEVELS):
            side_mix[i, k, OWN_ROWS] = roll(ends[k], -(4 * b + 2), 1)
        for side, place in enumerate((RING_ROWS - 1, ROWS)):
            side_mix[i, :, place] = roll(rims[side], -(4 * b + 2), 1)

    levels = range(LEVELS)
    for k in levels:
        stencil = [coef1[i, k] for i in range(5)]
        for i in range(2):
            q = jnp.concatenate([mix[i, k], side_mix[i, k]], axis=1)
            moved[i, k] = advected(q, east(q), west(q), north(q), south(q), stencil)
    tau = jnp.zeros(WIDE, jnp.float32)
    top = tau + 1.0
    for k in levels:
        wet = wets[0, k]
        tau = tau + (0.1 + 0.3 * jnp.maximum(moved[0, k], 0.0))
        below = jnp.exp(-tau)
        light_out[0, k] = (wet * (top - below))[OWN_ROWS, FIRST]
        light = (0.5 * wet) * top
        coef1[5, k] = wet
        coef1[6, k] = light
        moved[0, k] = wet * moved[0, k] + light * moved[1, k]
        top = below
    inner = (OWN_ROWS, FIRST)
    tau = jnp.zeros((ROWS, LANES), jnp.float32)
    top = tau + 1.0
    for k in levels:
        chl = moved[0, k]
        stencil = [coef2[i, k] for i in range(5)]
        after = advected(*(q[inner] for q in (chl, east(chl), west(chl), north(chl), south(chl))), stencil)
        wet = wets[(0, k, *inner)]
        tau = tau + (0.1 + 0.3 * jnp.maximum(after, 0.0))
        below = jnp.exp(-tau)
        coef2[5, k] = wet
        coef2[6, k] = (0.5 * wet) * top
        light_out[1, k] = (2.0 * wet) * (top - below)
        top = below
    for s, heat in enumerate(heats):
        m = lax.rem(lon + (s + 1), n)
        for i in range(2):
            heat[i] = light_out[i, pl.ds(m * share, share)]


def tile_stencil(q, rim, columns, stencil, sub, lane):
    e = jnp.where(lane == LANES - 1, columns, roll(q, -1, 1))
    w = jnp.where(lane == 0, columns, roll(q, 1, 1))
    up = jnp.where(sub == ROWS - 1, rim, roll(q, -1, 0))
    down = jnp.where(sub == 0, rim, roll(q, 1, 0))
    return advected(q, e, w, up, down, stencil)


def swapped(q):
    return jnp.where(iota(q.shape, 1) % 4 == 1, roll(q, -1, 1), roll(q, 1, 1))


def beside_columns(edge, b):
    return roll(edge, LANES - 2 - 4 * b, 1)


def part_of(b, half):
    return slice(b * ROWS, (b + 1) * ROWS), slice(half * LANES, (half + 1) * LANES)


def tile_loop(pairs, source, rims, edge, coef, m_all, adv, store):
    tracers = source.shape[0]
    sub, lane = iota((ROWS, LANES), 0), iota((ROWS, LANES), 1)
    for i in pairs:
        for half in range(2):
            k = 2 * i + half
            stencil = [coef(j, k) for j in range(5)]
            columns = edge[k]
            for b in range(tracers):
                adv[(i, *part_of(b, half))] = tile_stencil(
                    source[b, k], rims[b, k], beside_columns(columns, b), stencil, sub, lane
                )
        react = product(m_all[...], stacked(adv[i], 0))
        for half in range(2):
            k = 2 * i + half
            wet, light = coef(5, k), coef(6, k)
            for b in range(tracers):
                store(b, k, wet * adv[(i, *part_of(b, half))] + light * react[part_of(b, half)])
        yield i


def tracer_kernel(
    n,
    strips,
    f,
    c,
    edges,
    ends,
    rims,
    coef,
    coef2,
    m_all,
    e_all,
    z,
    r,
    u_out,
    v_out,
    result,
    c_out,
    row1,
    edge1,
    row0,
    edge0,
    done,
    adv,
    adv2,
    sem,
    c_sem,
):
    pos = position()
    tracers = c.shape[0]
    lon = pos[1]
    halo = Halo(pos, strips)
    sub, lane = iota((ROWS, LANES), 0), iota((ROWS, LANES), 1)
    easterly = lane % 4 >= 2
    base = LEVELS + n

    rim = row0.at[0]
    rim[:, 0, :] = rims[0]
    rim[:, ROWS - 1, :] = rims[1]
    parts = []
    for k in range(LEVELS):
        q, inside = ends[k], edges[k]
        outer = jnp.where(easterly, roll(q, -1, 1), roll(q, 1, 1))
        inner = jnp.where(easterly, roll(inside, 1, 1), roll(inside, -1, 1))
        up = jnp.where(sub == ROWS - 1, rim[k], roll(q, -1, 0))
        down = jnp.where(sub == 0, rim[k], roll(q, 1, 0))

        def at_edge(i):
            side = coef[i, k, :ROWS, LANES:]
            return (
                jnp.broadcast_to(side[:, :1], (ROWS, LANES)),
                jnp.broadcast_to(side[:, LANES - 1 :], (ROWS, LANES)),
            )

        def pick(pair):
            return jnp.where(easterly, pair[0], pair[1])

        stencil = [pick(at_edge(i)) for i in range(5)]
        wet, light = at_edge(5), at_edge(6)
        moved = advected(
            q, jnp.where(easterly, outer, inner), jnp.where(easterly, inner, outer), up, down, stencil
        )
        parts.append((moved, pick(wet), pick(light)))
        edge0[k] = swapped(q)
    react = product(stacked(jnp.concatenate([p[0] for p in parts], axis=0), 1), e_all[...])
    east_exists = jnp.where(lon < n - 1, 1.0, 0.0)
    west_exists = jnp.where(lon > 0, 1.0, 0.0)
    exists = jnp.where(easterly, east_exists, west_exists)
    for k, (q, wet, light) in enumerate(parts):
        edge1[k] = swapped((wet * q + light * react[k * ROWS : (k + 1) * ROWS]) * exists)

    places = ((0, RING_ROWS - 1), (ROWS - 1, ROWS))
    corners = [swapped(rims[side]) for side in range(2)]
    stencils = [[coef[i, :, place, :LANES] for i in range(7)] for _, place in places]
    for b in range(tracers):
        near = halo.sides(r[base + 2 * b], z[base + 2 * b])
        far = halo.sides(r[base + 2 * b + 1], z[base + 2 * b + 1])
        for side, (at, _) in enumerate(places):
            q = near[side]
            row0[b, :, at, :] = q
            columns = beside_columns(corners[side], b)
            e = jnp.where(lane == LANES - 1, columns, roll(q, -1, 1))
            w = jnp.where(lane == 0, columns, roll(q, 1, 1))
            inner = c[b, :, at, :]
            up, down = (inner, far[side]) if side == 0 else (far[side], inner)
            adv[(LEVELS // 2, *part_of(b, side))] = advected(q, e, w, up, down, stencils[side][:5])
    react = product(m_all[...], stacked(adv[LEVELS // 2], 0))
    for b in range(tracers):
        for side, (at, _) in enumerate(places):
            wet, light = stencils[side][5:]
            row1[b, :, at, :] = wet * adv[(LEVELS // 2, *part_of(b, side))] + light * react[part_of(b, side)]

    def store(b, k, q):
        c_out[b, k] = q

    copies = [pltpu.make_async_copy(f.at[i], ref, sem.at[i]) for i, ref in enumerate((u_out, v_out))]
    for copy in copies:
        copy.start()

    def store_done(b, k, q):
        done[b, k] = q

    pairs = range(LEVELS // 2)
    for _ in tile_loop(pairs, c, row0, edge0, lambda i, k: coef[i, k, :ROWS, :LANES], m_all, adv, store):
        pass
    for i in tile_loop(pairs, c_out, row1, edge1, lambda i, k: coef2[i, k], m_all, adv2, store_done):
        part = pl.ds(2 * i, 2)
        copies.append(pltpu.make_async_copy(done.at[:, part], result.at[:, part], c_sem.at[i]))
        copies[-1].start()
    for copy in copies:
        copy.wait()


def last_kernel(n, *refs):
    others = n - 1
    f, light, heats = refs[0], refs[1], refs[2 : 2 + others]
    t_out, h_out, warm, sem = refs[2 + others :]
    share = f.shape[1]
    _, lon, _ = position()
    here = block_of(lon)
    for level in range(share):
        k = lon * share + level
        warm[0, level, :, here] = f[2, level, :, here] + light[0, k]
        warm[1, level, :, here] = light[1, k]
        for s, heat in enumerate(heats):
            there = block_of(lax.rem(lon + (n - 1 - s), n))
            warm[0, level, :, there] = f[2, level, :, there] + heat[0, level]
            warm[1, level, :, there] = heat[1, level]
    copies = [pltpu.make_async_copy(warm.at[i], ref, sem.at[i]) for i, ref in enumerate((t_out, h_out))]
    for copy in copies:
        copy.start()
    for copy in copies:
        copy.wait()


def shards(groups, n, lats, u, v, t, h, c, count, rates):
    tracers = c.shape[0]
    share, width = u.shape[0], u.shape[2]
    strips = lats * CORES
    vmem = pl.BlockSpec(memory_space=pltpu.VMEM)
    anywhere = pl.BlockSpec(memory_space=pl.ANY)
    hbm = pl.BlockSpec(memory_space=pltpu.HBM)
    params = pltpu.CompilerParams(vmem_limit_bytes=32 * 1024 * 1024)
    dma = pltpu.SemaphoreType.DMA

    def shape(*dims, dtype=jnp.float32):
        return jax.ShapeDtypeStruct(dims, dtype)

    def tiles(*dims):
        return shape(*dims, ROWS, LANES)

    def scratch(*dims):
        return pltpu.VMEM(dims, jnp.float32)

    def call(kernel, name, args, in_specs, out_shape, out_specs=None, scratch_shapes=()):
        return pl.pallas_call(
            kernel,
            out_shape=tuple(out_shape),
            in_specs=in_specs,
            out_specs=out_specs or (vmem,) * len(out_shape),
            scratch_shapes=scratch_shapes,
            compiler_params=params,
            name=name,
        )(*args)

    def permute(q, target):
        pairs = []
        for g in range(groups):
            for a in range(lats):
                for o in range(n):
                    for i in range(CORES):
                        g2, a2, o2, i2 = target(g, a, o, i)
                        pairs.append(
                            (((g * lats + a) * n + o) * CORES + i, ((g2 * lats + a2) * n + o2) * CORES + i2)
                        )
        return lax.ppermute(q, ("grp", "lat", "lon", "role"), pairs)

    def z_target(shift):
        def target(g, a, o, i):
            s = a * CORES + i + (1 if i else -1)
            if 0 <= s < strips:
                return g, s // CORES, (o + shift) % n, s % CORES
            return (g ^ 1 if g ^ 1 < groups else g), a, o, i

        return target

    def x_target(shift):
        return lambda g, a, o, i: (g, a, (o + shift) % n, i)

    def r_target(g, a, o, i):
        return g, a, o, 1 - i

    shifts = range(1, n)
    z_tiles = LEVELS + n + 2 * tracers
    f, c_here, depth, rates, z_pay, r_pay = call(
        functools.partial(load_kernel, n),
        "load",
        [pltpu.with_memory_space_constraint(q, pltpu.HBM) for q in (u, v, t, h, count, rates, c)],
        [hbm] * 7,
        [
            shape(FIELDS, *u.shape),
            shape(*c.shape),
            shape(*count.shape, dtype=jnp.int32),
            shape(*rates.shape),
            tiles(z_tiles),
            tiles(z_tiles),
        ],
        scratch_shapes=[dma((FIELDS + 2,)), dma((4,))],
    )
    r_in = permute(r_pay, r_target)
    z_in = permute(z_pay, z_target(0))
    sums, edges, *pays = call(
        functools.partial(edge_kernel, n),
        "edges",
        (rates, c_here),
        [vmem] * 2,
        [tiles(LEVELS)] * 2 + [tiles(LEVELS // 2)] * (n - 1),
    )
    pays = call(
        functools.partial(join_kernel, n),
        "join",
        (rates, f, z_pay, r_in, *pays),
        [vmem] * (n + 3),
        [tiles(FIELDS * share + LEVELS // 2 + share + 2)] * (n - 1) + [tiles(share + 1)] * (n - 1),
    )
    xs = [permute(q, x_target(s)) for s, q in zip(shifts, pays[: n - 1])]
    xzs = [permute(q, z_target(s)) for s, q in zip(shifts, pays[n - 1 :])]

    m_size, e_size = tracers * ROWS, LANES
    bf16 = jnp.bfloat16
    m_all, e_all = call(
        spread_kernel,
        "spread",
        (rates,),
        [vmem],
        [shape(m_size, 3 * m_size, dtype=bf16), shape(3 * e_size, e_size, dtype=bf16)],
    )

    args = (rates, f, depth, c_here, sums, z_in, r_in)
    own1, own2, wets, mix, f_new = call(
        functools.partial(own_kernel, n, strips),
        "own",
        args,
        [vmem] * len(args),
        [
            shape(5, share, RING_ROWS, RING_COLS),
            tiles(5, share),
            shape(3, LEVELS, RING_ROWS, RING_COLS),
            shape(2, LEVELS, RING_ROWS, LANES),
            shape(3, *u.shape),
        ],
        scratch_shapes=[scratch(FIELDS, share, RING_ROWS, RING_COLS), scratch(RING_ROWS, RING_COLS)],
    )
    args = (own1, own2, wets, mix, m_all, e_all, *xs, *xzs)
    coef1, coef2, ends, rims, light, *heats = call(
        functools.partial(flow_kernel, n, strips, tracers),
        "flow",
        args,
        [vmem] * len(args),
        [
            shape(7, LEVELS, RING_ROWS, RING_COLS),
            tiles(7, LEVELS),
            tiles(LEVELS),
            shape(2, LEVELS, LANES),
            tiles(2, LEVELS),
        ]
        + [tiles(2, share)] * (n - 1),
        scratch_shapes=[
            scratch(FIELDS, (n - 1) * share, RING_ROWS, RING_COLS),
            scratch(2, LEVELS, RING_ROWS, LANES),
            scratch(n, LEVELS // 2, ROWS, LANES),
            scratch(n, 2, LEVELS, LANES),
            scratch(2, LEVELS, RING_ROWS, RING_COLS),
        ],
    )
    heats = [permute(q, x_target(s)) for s, q in zip(shifts, heats)]
    args = (f_new, c_here, edges, ends, rims, coef1, coef2, m_all, e_all, z_in, r_in)
    u_new, v_new, c_new = call(
        functools.partial(tracer_kernel, n, strips),
        "tracers",
        args,
        [vmem] * len(args),
        [shape(*u.shape)] * 2 + [shape(*c.shape)],
        out_specs=(anywhere,) * 3,
        scratch_shapes=[
            scratch(*c.shape),
            scratch(tracers, LEVELS, ROWS, LANES),
            scratch(LEVELS, ROWS, LANES),
            scratch(tracers, LEVELS, ROWS, LANES),
            scratch(LEVELS, ROWS, LANES),
            scratch(*c.shape),
            scratch(LEVELS // 2 + 1, tracers * ROWS, 2 * LANES),
            scratch(LEVELS // 2, tracers * ROWS, 2 * LANES),
            dma((2,)),
            dma((LEVELS // 2,)),
        ],
    )
    args = (f_new, light, *heats)
    t_new, h_new = call(
        functools.partial(last_kernel, n),
        "last",
        args,
        [vmem] * len(args),
        [shape(*u.shape)] * 2,
        out_specs=(anywhere,) * 2,
        scratch_shapes=[scratch(2, *u.shape), dma((2,))],
    )
    return u_new, v_new, t_new, h_new, c_new


def solution(mesh):
    level = P("lon", ("grp", "lat", "role"), None)
    tracer = P(None, None, ("grp", "lat", "role"), "lon")
    return jax.shard_map(
        functools.partial(shards, mesh.shape["grp"], mesh.shape["lon"], mesh.shape["lat"]),
        mesh=mesh,
        in_specs=(level, level, level, level, tracer, P(("grp", "lat", "role"), None), P()),
        out_specs=(level, level, level, level, tracer),
        check_vma=False,
    )
```

time: 18.6 us -> 17.6 us (0.946)
  waiting for transfers between devices: 2.22 us -> 1.41 us
  starting transfers between devices: 7.63 us -> 7.18 us
  Pallas kernels: 7.93 us -> 8.17 us
    ppermute x6 -> x5, waiting for transfers between devices: 2.22 us -> 1.41 us  [permute(): return lax.ppermute(q, ('grp', 'lat', 'lon', 'role'), pairs)]
    ppermute x6 -> x5, starting transfers between devices: 7.63 us -> 7.18 us  [permute(): return lax.ppermute(q, ('grp', 'lat', 'lon', 'role'), pairs)]
    pallas_call x6 -> x8, Pallas kernels: 7.93 us -> 8.17 us  [call(): pl.pallas_call(kernel, out_shape=tuple(out_shape), in_specs=in_specs, out...]
  transfers between devices with their start and end apart: 6 -> 5, of which waited for: 1 -> 2; matrix products, arithmetic and copies ran while one was open for 0% -> 0% of each run, Pallas kernels for 20% -> 30%
where the time goes in v4:
time: 17.6 us; the launch traced here: 17.4 us
  Pallas kernels  8.17 us (46%)
  starting transfers between devices  7.18 us (41%)
  waiting for transfers between devices  1.41 us (8%)
  between operations  0.68 us (4%)
    pallas_call x8, Pallas kernels, call(): pl.pallas_call(kernel, out_shape=tuple(out_shape), in_specs=in_specs, out...  8.17 us
    ppermute x5, starting transfers between devices, permute(): return lax.ppermute(q, ('grp', 'lat', 'lon', 'role'), pairs)  7.18 us
    ppermute x5, waiting for transfers between devices, permute(): return lax.ppermute(q, ('grp', 'lat', 'lon', 'role'), pairs)  1.41 us
  transfers between devices with their start and end apart: 5, of which 2 were waited for; matrix products, arithmetic and copies ran while one was open for 0% of the time, Pallas kernels for 30%

profile of v4, /device:TPU:0, one launch (start us, length us, event | category | flops | bytes accessed | tf_op | source)
XLA Modules:
  0.0 17.4 jit_solution(5056493314674493049)
XLA Ops:
  0.6 1.4 %load.1 = (f32[4,4,8,256]{3,2,1,0:T(8,128)S(1)}, f32[24,8,8,128]{3,2,1,0:T(8,128)S(1)}, s32[8,256]{1,0:T(8,128)S(1)}, f32[24,24]{1,0:T(8,128)S(1)}, f32[58,8,128...) custom-call(f32[4,8,256]{2,1,0:T(8,128)} %u.1, f32[4,8,256]{2,1,0:T(8,128)} %v.1, f32[4,8,256]{2,1,0:T(8,128)} %t.1, ...), custom_call_target="tpu_custom_call" | custom-call | tf_op jit(solution)/shard_map/load/pallas_call | solution.py:692
  2.1 0.5 %collective-permute-start.1 = (f32[58,8,128]{2,1,0:T(8,128)S(1)}, f32[58,8,128]{2,1,0:T(8,128)S(1)}, u32[]{:S(2)}, u32[]{:S(2)}) collective-permute-start(f32[58,8,128]{2,1,0:T(8,128)S(1)} %get-tuple-element.40), channel_id=1, source_target_pairs={{0,1},{1,0},{2,3},{3,2},{4,5},{5,4},{6,7},{7,6},{8,9},{9,8},{10,11... | collective-permute-start | bytes 712712 | tf_op jit(solution)/shard_map/ppermute | solution.py:712
  2.6 2.6 %collective-permute-start = (f32[58,8,128]{2,1,0:T(8,128)S(1)}, f32[58,8,128]{2,1,0:T(8,128)S(1)}, u32[]{:S(2)}, u32[]{:S(2)}) collective-permute-start(f32[58,8,128]{2,1,0:T(8,128)S(1)} %get-tuple-element.39.z), channel_id=1, source_target_pairs={{0,16},{1,4},{2,18},{3,6},{4,1},{5,8},{6,3},{7,10},{8,5},{9,12},{1... | collective-permute-start | bytes 712712 | tf_op jit(solution)/shard_map/ppermute | solution.py:712
  5.2 0.4 %edges.1 = (f32[8,8,128]{2,1,0:T(8,128)S(1)}, f32[8,8,128]{2,1,0:T(8,128)S(1)}, f32[4,8,128]{2,1,0:T(8,128)S(1)}) custom-call(f32[24,24]{1,0:T(8,128)S(1)} %get-tuple-element.34.rates, f32[24,8,8,128]{3,2,1,0:T(8,128)S(1)} %get-tuple-element.37.c), custom_call_target="tpu_custom_call" | custom-call | tf_op jit(solution)/shard_map/edges/pallas_call | solution.py:692
  5.6 0.0 collective-permute-done.1.r
  5.6 0.2 %join.1 = (f32[26,8,128]{2,1,0:T(8,128)S(1)}, f32[5,8,128]{2,1,0:T(8,128)S(1)}) custom-call(f32[24,24]{1,0:T(8,128)S(1)} %get-tuple-element.34.rates, f32[4,4,8,256]{3,2,1,0:T(8,128)S(1)} %get-tuple-element.35.f, f32[58,8,128]{2,1,0:T(8,128)S(1)} %get-tuple-element.39.z, f32[58,8,128]{2,1,0:T(8,128)S(1)} %collective-permute-done.1.r, ...), custom_call_target="tpu_custom_call" | custom-call | tf_op jit(solution)/shard_map/join/pallas_call | solution.py:692
  5.8 1.5 %collective-permute-start.2 = (f32[26,8,128]{2,1,0:T(8,128)S(1)}, f32[26,8,128]{2,1,0:T(8,128)S(1)}, u32[]{:S(2)}, u32[]{:S(2)}) collective-permute-start(f32[26,8,128]{2,1,0:T(8,128)S(1)} %get-tuple-element.50), channel_id=1, source_target_pairs={{0,2},{1,3},{2,0},{3,1},{4,6},{5,7},{6,4},{7,5},{8,10},{9,11},{10,... | collective-permute-start | bytes 319496 | tf_op jit(solution)/shard_map/ppermute | solution.py:712
  7.4 1.0 %collective-permute-start.3 = (f32[5,8,128]{2,1,0:T(8,128)S(1)}, f32[5,8,128]{2,1,0:T(8,128)S(1)}, u32[]{:S(2)}, u32[]{:S(2)}) collective-permute-start(f32[5,8,128]{2,1,0:T(8,128)S(1)} %get-tuple-element.51), channel_id=1, source_target_pairs={{0,16},{1,6},{2,18},{3,4},{4,3},{5,10},{6,1},{7,8},{8,7},{9,14},{1... | collective-permute-start | bytes 61448 | tf_op jit(solution)/shard_map/ppermute | solution.py:712
  8.4 0.6 %spread.1 = (bf16[192,576]{1,0:T(8,128)(2,1)S(1)}, bf16[384,128]{1,0:T(8,128)(2,1)S(1)}) custom-call(f32[24,24]{1,0:T(8,128)S(1)} %get-tuple-element.34.rates), custom_call_target="tpu_custom_call" | custom-call | tf_op jit(solution)/shard_map/spread/pallas_call | solution.py:692
  8.9 0.3 %collective-permute-done.z = f32[58,8,128]{2,1,0:T(8,128)S(1)} collective-permute-done((f32[58,8,128]{2,1,0:T(8,128)S(1)}, f32[58,8,128]{2,1,0:T(8,128)S(1)}, u32[]{:S(2)}, u32[]{:S(2)}) %collective-permute-start) | collective-permute-done | bytes 237600 | tf_op jit(solution)/shard_map/ppermute | solution.py:712
  9.3 0.8 %own.1 = (f32[5,4,16,256]{3,2,1,0:T(8,128)S(1)}, f32[5,4,8,128]{3,2,1,0:T(8,128)S(1)}, f32[3,8,16,256]{3,2,1,0:T(8,128)S(1)}, f32[2,8,16,128]{3,2,1,0:T(8,128)S(1)}, f32[3,4,8,256]{3,2,1,0:T(8,128)S(1)}) custom-call(f32[24,24]{1,0:T(8,128)S(1)} %get-tuple-element.34.rates, f32[4,4,8,256]{3,2,1,0:T(8,128)S(1)} %get-tuple-element.35.f, ...), custom_call_target="tpu_custom_call" | custom-call | tf_op jit(solution)/shard_map/own/pallas_call | solution.py:692
  10.1 1.1 %collective-permute-done.3.refs_7_ = f32[5,8,128]{2,1,0:T(8,128)S(1)} collective-permute-done((f32[5,8,128]{2,1,0:T(8,128)S(1)}, f32[5,8,128]{2,1,0:T(8,128)S(1)}, u32[]{:S(2)}, u32[]{:S(2)}) %collective-permute-start.3) | collective-permute-done | bytes 20512 | tf_op jit(solution)/shard_map/ppermute | solution.py:712
  11.1 0.0 collective-permute-done.2.refs_6_
  11.1 0.8 %flow.1 = (f32[7,8,16,256]{3,2,1,0:T(8,128)S(1)}, f32[7,8,8,128]{3,2,1,0:T(8,128)S(1)}, f32[8,8,128]{2,1,0:T(8,128)S(1)}, f32[2,8,128]{2,1,0:T(8,128)S(1)}, f32[...) custom-call(f32[5,4,16,256]{3,2,1,0:T(8,128)S(1)} %get-tuple-element.43.refs_0_, ...), custom_call_target="tpu_custom_call" | custom-call | tf_op jit(solution)/shard_map/flow/pallas_call | solution.py:692
  12.0 1.5 %collective-permute-start.4 = (f32[2,4,8,128]{3,2,1,0:T(8,128)S(1)}, f32[2,4,8,128]{3,2,1,0:T(8,128)S(1)}, u32[]{:S(2)}, u32[]{:S(2)}) collective-permute-start(f32[2,4,8,128]{3,2,1,0:T(8,128)S(1)} %get-tuple-element.59), channel_id=1, source_target_pairs={{0,2},{1,3},{2,0},{3,1},{4,6},{5,7},{6,4},{7,5},{8,10},{9,11},{10,... | collective-permute-start | bytes 98312 | tf_op jit(solution)/shard_map/ppermute | solution.py:712
  13.5 3.3 %tracers.1 = (f32[4,8,256]{2,1,0:T(8,128)}, f32[4,8,256]{2,1,0:T(8,128)}, f32[24,8,8,128]{3,2,1,0:T(8,128)}) custom-call(f32[3,4,8,256]{3,2,1,0:T(8,128)S(1)} %get-tuple-element.41.f.refs_0_, f32[24,8,8,128]{3,2,1,0:T(8,128)S(1)} %get-tuple-element.37.c, f32[8,8,128]{2,1,0:T(8,128)S(1)} %get-tuple-element.42.edges, f32[8,8,128]{2,1,0:T(8,128)S(1)} %get-tuple-element.52.ends, ...), custom_call_target="tpu_custom_call" | custom-call | tf_op jit(solution)/shard_map/tracers/pallas_call | solution.py:692
  16.8 0.0 collective-permute-done.4.refs_2_
  16.8 0.7 %last.1 = (f32[4,8,256]{2,1,0:T(8,128)}, f32[4,8,256]{2,1,0:T(8,128)}) custom-call(f32[3,4,8,256]{3,2,1,0:T(8,128)S(1)} %get-tuple-element.41.f.refs_0_, f32[2,8,8,128]{3,2,1,0:T(8,128)S(1)} %get-tuple-element.58.refs_1_, f32[2,4,8,128]{3,2,1,0:T(8,128)S(1)} %collective-permute-done.4.refs_2_), custom_call_target="tpu_custom_call" | custom-call | tf_op jit(solution)/shard_map/last/pallas_call | solution.py:692
Async XLA Ops:
  2.1 3.5 %collective-permute-start.1 = (f32[58,8,128]{2,1,0:T(8,128)S(1)}, f32[58,8,128]{2,1,0:T(8,128)S(1)}, u32[]{:S(2)}, u32[]{:S(2)}) collective-permute-start(f32[58,8,128]{2,1,0:T(8,128)S(1)} %get-tuple-element.40), channel_id=1, source_target_pairs={{0,1},{1,0},{2,3},{3,2},{4,5},{5,4},{6,7},{7,6},{8,9},{9,8},{10,11... | collective-permute-start | bytes 712712 | tf_op jit(solution)/shard_map/ppermute | solution.py:712
  2.6 6.7 %collective-permute-start = (f32[58,8,128]{2,1,0:T(8,128)S(1)}, f32[58,8,128]{2,1,0:T(8,128)S(1)}, u32[]{:S(2)}, u32[]{:S(2)}) collective-permute-start(f32[58,8,128]{2,1,0:T(8,128)S(1)} %get-tuple-element.39.z), channel_id=1, source_target_pairs={{0,16},{1,4},{2,18},{3,6},{4,1},{5,8},{6,3},{7,10},{8,5},{9,12},{1... | collective-permute-start | bytes 712712 | tf_op jit(solution)/shard_map/ppermute | solution.py:712
  5.8 5.3 %collective-permute-start.2 = (f32[26,8,128]{2,1,0:T(8,128)S(1)}, f32[26,8,128]{2,1,0:T(8,128)S(1)}, u32[]{:S(2)}, u32[]{:S(2)}) collective-permute-start(f32[26,8,128]{2,1,0:T(8,128)S(1)} %get-tuple-element.50), channel_id=1, source_target_pairs={{0,2},{1,3},{2,0},{3,1},{4,6},{5,7},{6,4},{7,5},{8,10},{9,11},{10,... | collective-permute-start | bytes 319496 | tf_op jit(solution)/shard_map/ppermute | solution.py:712
  7.4 3.8 %collective-permute-start.3 = (f32[5,8,128]{2,1,0:T(8,128)S(1)}, f32[5,8,128]{2,1,0:T(8,128)S(1)}, u32[]{:S(2)}, u32[]{:S(2)}) collective-permute-start(f32[5,8,128]{2,1,0:T(8,128)S(1)} %get-tuple-element.51), channel_id=1, source_target_pairs={{0,16},{1,6},{2,18},{3,4},{4,3},{5,10},{6,1},{7,8},{8,7},{9,14},{1... | collective-permute-start | bytes 61448 | tf_op jit(solution)/shard_map/ppermute | solution.py:712
  12.0 4.8 %collective-permute-start.4 = (f32[2,4,8,128]{3,2,1,0:T(8,128)S(1)}, f32[2,4,8,128]{3,2,1,0:T(8,128)S(1)}, u32[]{:S(2)}, u32[]{:S(2)}) collective-permute-start(f32[2,4,8,128]{3,2,1,0:T(8,128)S(1)} %get-tuple-element.59), channel_id=1, source_target_pairs={{0,2},{1,3},{2,0},{3,1},{4,6},{5,7},{6,4},{7,5},{8,10},{9,11},{10,... | collective-permute-start | bytes 98312 | tf_op jit(solution)/shard_map/ppermute | solution.py:712

commit v5 on v4

--- a/solution.py
+++ b/solution.py
@@ -537,7 +537,6 @@
 def tracer_kernel(
     n,
     strips,
-    f,
     c,
     edges,
     ends,
@@ -548,19 +547,15 @@
     e_all,
     z,
     r,
-    u_out,
-    v_out,
-    result,
+    done,
     c_out,
     row1,
     edge1,
     row0,
     edge0,
-    done,
+    rim,
     adv,
     adv2,
-    sem,
-    c_sem,
 ):
     pos = position()
     tracers = c.shape[0]
@@ -570,7 +565,6 @@
     easterly = lane % 4 >= 2
     base = LEVELS + n
 
-    rim = row0.at[0]
     rim[:, 0, :] = rims[0]
     rim[:, ROWS - 1, :] = rims[1]
     parts = []
@@ -629,28 +623,27 @@
     def store(b, k, q):
         c_out[b, k] = q
 
-    copies = [pltpu.make_async_copy(f.at[i], ref, sem.at[i]) for i, ref in enumerate((u_out, v_out))]
-    for copy in copies:
-        copy.start()
-
     def store_done(b, k, q):
         done[b, k] = q
 
     pairs = range(LEVELS // 2)
     for _ in tile_loop(pairs, c, row0, edge0, lambda i, k: coef[i, k, :ROWS, :LANES], m_all, adv, store):
         pass
-    for i in tile_loop(pairs, c_out, row1, edge1, lambda i, k: coef2[i, k], m_all, adv2, store_done):
-        part = pl.ds(2 * i, 2)
-        copies.append(pltpu.make_async_copy(done.at[:, part], result.at[:, part], c_sem.at[i]))
-        copies[-1].start()
-    for copy in copies:
-        copy.wait()
+    for _ in tile_loop(pairs, c_out, row1, edge1, lambda i, k: coef2[i, k], m_all, adv2, store_done):
+        pass
 
 
 def last_kernel(n, *refs):
     others = n - 1
-    f, light, heats = refs[0], refs[1], refs[2 : 2 + others]
-    t_out, h_out, warm, sem = refs[2 + others :]
+    c, f, light, heats = *refs[:3], refs[3 : 3 + others]
+    c_out, u_out, v_out, t_out, h_out, warm, sem, c_sem = refs[3 + others :]
+    copies = [pltpu.make_async_copy(f.at[i], ref, sem.at[i]) for i, ref in enumerate((u_out, v_out))]
+    batch = c.shape[0] // c_sem.shape[0]
+    for i in range(c_sem.shape[0]):
+        part = pl.ds(i * batch, batch)
+        copies.append(pltpu.make_async_copy(c.at[part], c_out.at[part], c_sem.at[i]))
+    for copy in copies:
+        copy.start()
     share = f.shape[1]
     _, lon, _ = position()
     here = block_of(lon)
@@ -662,8 +655,8 @@
             there = block_of(lax.rem(lon + (n - 1 - s), n))
             warm[0, level, :, there] = f[2, level, :, there] + heat[0, level]
             warm[1, level, :, there] = heat[1, level]
-    copies = [pltpu.make_async_copy(warm.at[i], ref, sem.at[i]) for i, ref in enumerate((t_out, h_out))]
-    for copy in copies:
+    copies += [pltpu.make_async_copy(warm.at[i], ref, sem.at[2 + i]) for i, ref in enumerate((t_out, h_out))]
+    for copy in copies[-2:]:
         copy.start()
     for copy in copies:
         copy.wait()
@@ -810,36 +803,33 @@
         ],
     )
     heats = [permute(q, x_target(s)) for s, q in zip(shifts, heats)]
-    args = (f_new, c_here, edges, ends, rims, coef1, coef2, m_all, e_all, z_in, r_in)
-    u_new, v_new, c_new = call(
+    args = (c_here, edges, ends, rims, coef1, coef2, m_all, e_all, z_in, r_in)
+    (c_new,) = call(
         functools.partial(tracer_kernel, n, strips),
         "tracers",
         args,
         [vmem] * len(args),
-        [shape(*u.shape)] * 2 + [shape(*c.shape)],
-        out_specs=(anywhere,) * 3,
+        [shape(*c.shape)],
         scratch_shapes=[
             scratch(*c.shape),
             scratch(tracers, LEVELS, ROWS, LANES),
             scratch(LEVELS, ROWS, LANES),
             scratch(tracers, LEVELS, ROWS, LANES),
             scratch(LEVELS, ROWS, LANES),
-            scratch(*c.shape),
+            scratch(LEVELS, ROWS, LANES),
             scratch(LEVELS // 2 + 1, tracers * ROWS, 2 * LANES),
             scratch(LEVELS // 2, tracers * ROWS, 2 * LANES),
-            dma((2,)),
-            dma((LEVELS // 2,)),
         ],
     )
-    args = (f_new, light, *heats)
-    t_new, h_new = call(
+    args = (c_new, f_new, light, *heats)
+    c_new, u_new, v_new, t_new, h_new = call(
         functools.partial(last_kernel, n),
         "last",
         args,
         [vmem] * len(args),
-        [shape(*u.shape)] * 2,
-        out_specs=(anywhere,) * 2,
-        scratch_shapes=[scratch(2, *u.shape), dma((2,))],
+        [shape(*c.shape)] + [shape(*u.shape)] * FIELDS,
+        out_specs=(anywhere,) * 5,
+        scratch_shapes=[scratch(2, *u.shape), dma((FIELDS,)), dma((1,))],
     )
     return u_new, v_new, t_new, h_new, c_new
 

time: 17.6 us -> 17.2 us (0.977)
  Pallas kernels: 8.17 us -> 7.74 us
    pallas_call x8, Pallas kernels: 8.17 us -> 7.74 us  [call(): pl.pallas_call(kernel, out_shape=tuple(out_shape), in_specs=in_specs, out...]
  transfers between devices with their start and end apart: 5 -> 5, of which waited for: 2 -> 2; matrix products, arithmetic and copies ran while one was open for 0% -> 0% of each run, Pallas kernels for 30% -> 26%
where the time goes in v5:
time: 17.2 us; the launch traced here: 17 us
  Pallas kernels  7.74 us (45%)
  starting transfers between devices  7.18 us (42%)
  waiting for transfers between devices  1.41 us (8%)
  between operations  0.68 us (4%)
    pallas_call x8, Pallas kernels, call(): pl.pallas_call(kernel, out_shape=tuple(out_shape), in_specs=in_specs, out...  7.74 us
    ppermute x5, starting transfers between devices, permute(): return lax.ppermute(q, ('grp', 'lat', 'lon', 'role'), pairs)  7.18 us
    ppermute x5, waiting for transfers between devices, permute(): return lax.ppermute(q, ('grp', 'lat', 'lon', 'role'), pairs)  1.41 us
  transfers between devices with their start and end apart: 5, of which 2 were waited for; matrix products, arithmetic and copies ran while one was open for 0% of the time, Pallas kernels for 26%

profile of v5, /device:TPU:0, one launch (start us, length us, event | category | flops | bytes accessed | tf_op | source)
XLA Modules:
  0.0 17.0 jit_solution(8008396076735248419)
XLA Ops:
  0.6 1.4 %load.1 = (f32[4,4,8,256]{3,2,1,0:T(8,128)S(1)}, f32[24,8,8,128]{3,2,1,0:T(8,128)S(1)}, s32[8,256]{1,0:T(8,128)S(1)}, f32[24,24]{1,0:T(8,128)S(1)}, f32[58,8,128...) custom-call(f32[4,8,256]{2,1,0:T(8,128)} %u.1, f32[4,8,256]{2,1,0:T(8,128)} %v.1, f32[4,8,256]{2,1,0:T(8,128)} %t.1, ...), custom_call_target="tpu_custom_call" | custom-call | tf_op jit(solution)/shard_map/load/pallas_call | solution.py:685
  2.1 0.5 %collective-permute-start.1 = (f32[58,8,128]{2,1,0:T(8,128)S(1)}, f32[58,8,128]{2,1,0:T(8,128)S(1)}, u32[]{:S(2)}, u32[]{:S(2)}) collective-permute-start(f32[58,8,128]{2,1,0:T(8,128)S(1)} %get-tuple-element.41), channel_id=1, source_target_pairs={{0,1},{1,0},{2,3},{3,2},{4,5},{5,4},{6,7},{7,6},{8,9},{9,8},{10,11... | collective-permute-start | bytes 712712 | tf_op jit(solution)/shard_map/ppermute | solution.py:705
  2.6 2.6 %collective-permute-start = (f32[58,8,128]{2,1,0:T(8,128)S(1)}, f32[58,8,128]{2,1,0:T(8,128)S(1)}, u32[]{:S(2)}, u32[]{:S(2)}) collective-permute-start(f32[58,8,128]{2,1,0:T(8,128)S(1)} %get-tuple-element.40.z), channel_id=1, source_target_pairs={{0,16},{1,4},{2,18},{3,6},{4,1},{5,8},{6,3},{7,10},{8,5},{9,12},{1... | collective-permute-start | bytes 712712 | tf_op jit(solution)/shard_map/ppermute | solution.py:705
  5.2 0.4 %edges.1 = (f32[8,8,128]{2,1,0:T(8,128)S(1)}, f32[8,8,128]{2,1,0:T(8,128)S(1)}, f32[4,8,128]{2,1,0:T(8,128)S(1)}) custom-call(f32[24,24]{1,0:T(8,128)S(1)} %get-tuple-element.35.rates, f32[24,8,8,128]{3,2,1,0:T(8,128)S(1)} %get-tuple-element.34.c), custom_call_target="tpu_custom_call" | custom-call | tf_op jit(solution)/shard_map/edges/pallas_call | solution.py:685
  5.6 0.0 collective-permute-done.1.r
  5.6 0.2 %join.1 = (f32[26,8,128]{2,1,0:T(8,128)S(1)}, f32[5,8,128]{2,1,0:T(8,128)S(1)}) custom-call(f32[24,24]{1,0:T(8,128)S(1)} %get-tuple-element.35.rates, f32[4,4,8,256]{3,2,1,0:T(8,128)S(1)} %get-tuple-element.37.f, f32[58,8,128]{2,1,0:T(8,128)S(1)} %get-tuple-element.40.z, f32[58,8,128]{2,1,0:T(8,128)S(1)} %collective-permute-done.1.r, ...), custom_call_target="tpu_custom_call" | custom-call | tf_op jit(solution)/shard_map/join/pallas_call | solution.py:685
  5.8 1.5 %collective-permute-start.2 = (f32[26,8,128]{2,1,0:T(8,128)S(1)}, f32[26,8,128]{2,1,0:T(8,128)S(1)}, u32[]{:S(2)}, u32[]{:S(2)}) collective-permute-start(f32[26,8,128]{2,1,0:T(8,128)S(1)} %get-tuple-element.49), channel_id=1, source_target_pairs={{0,2},{1,3},{2,0},{3,1},{4,6},{5,7},{6,4},{7,5},{8,10},{9,11},{10,... | collective-permute-start | bytes 319496 | tf_op jit(solution)/shard_map/ppermute | solution.py:705
  7.4 1.0 %collective-permute-start.3 = (f32[5,8,128]{2,1,0:T(8,128)S(1)}, f32[5,8,128]{2,1,0:T(8,128)S(1)}, u32[]{:S(2)}, u32[]{:S(2)}) collective-permute-start(f32[5,8,128]{2,1,0:T(8,128)S(1)} %get-tuple-element.50), channel_id=1, source_target_pairs={{0,16},{1,6},{2,18},{3,4},{4,3},{5,10},{6,1},{7,8},{8,7},{9,14},{1... | collective-permute-start | bytes 61448 | tf_op jit(solution)/shard_map/ppermute | solution.py:705
  8.4 0.6 %spread.1 = (bf16[192,576]{1,0:T(8,128)(2,1)S(1)}, bf16[384,128]{1,0:T(8,128)(2,1)S(1)}) custom-call(f32[24,24]{1,0:T(8,128)S(1)} %get-tuple-element.35.rates), custom_call_target="tpu_custom_call" | custom-call | tf_op jit(solution)/shard_map/spread/pallas_call | solution.py:685
  8.9 0.3 %collective-permute-done.z = f32[58,8,128]{2,1,0:T(8,128)S(1)} collective-permute-done((f32[58,8,128]{2,1,0:T(8,128)S(1)}, f32[58,8,128]{2,1,0:T(8,128)S(1)}, u32[]{:S(2)}, u32[]{:S(2)}) %collective-permute-start) | collective-permute-done | bytes 237600 | tf_op jit(solution)/shard_map/ppermute | solution.py:705
  9.3 0.8 %own.1 = (f32[5,4,16,256]{3,2,1,0:T(8,128)S(1)}, f32[5,4,8,128]{3,2,1,0:T(8,128)S(1)}, f32[3,8,16,256]{3,2,1,0:T(8,128)S(1)}, f32[2,8,16,128]{3,2,1,0:T(8,128)S(1)}, f32[3,4,8,256]{3,2,1,0:T(8,128)S(1)}) custom-call(f32[24,24]{1,0:T(8,128)S(1)} %get-tuple-element.35.rates, f32[4,4,8,256]{3,2,1,0:T(8,128)S(1)} %get-tuple-element.37.f, ...), custom_call_target="tpu_custom_call" | custom-call | tf_op jit(solution)/shard_map/own/pallas_call | solution.py:685
  10.1 1.1 %collective-permute-done.3.refs_7_ = f32[5,8,128]{2,1,0:T(8,128)S(1)} collective-permute-done((f32[5,8,128]{2,1,0:T(8,128)S(1)}, f32[5,8,128]{2,1,0:T(8,128)S(1)}, u32[]{:S(2)}, u32[]{:S(2)}) %collective-permute-start.3) | collective-permute-done | bytes 20512 | tf_op jit(solution)/shard_map/ppermute | solution.py:705
  11.1 0.0 collective-permute-done.2.refs_6_
  11.1 0.8 %flow.1 = (f32[7,8,16,256]{3,2,1,0:T(8,128)S(1)}, f32[7,8,8,128]{3,2,1,0:T(8,128)S(1)}, f32[8,8,128]{2,1,0:T(8,128)S(1)}, f32[2,8,128]{2,1,0:T(8,128)S(1)}, f32[...) custom-call(f32[5,4,16,256]{3,2,1,0:T(8,128)S(1)} %get-tuple-element.42.refs_0_, ...), custom_call_target="tpu_custom_call" | custom-call | tf_op jit(solution)/shard_map/flow/pallas_call | solution.py:685
  12.0 1.5 %collective-permute-start.4 = (f32[2,4,8,128]{3,2,1,0:T(8,128)S(1)}, f32[2,4,8,128]{3,2,1,0:T(8,128)S(1)}, u32[]{:S(2)}, u32[]{:S(2)}) collective-permute-start(f32[2,4,8,128]{3,2,1,0:T(8,128)S(1)} %get-tuple-element.57), channel_id=1, source_target_pairs={{0,2},{1,3},{2,0},{3,1},{4,6},{5,7},{6,4},{7,5},{8,10},{9,11},{10,... | collective-permute-start | bytes 98312 | tf_op jit(solution)/shard_map/ppermute | solution.py:705
  13.5 2.5 %tracers.1.refs_0_ = f32[24,8,8,128]{3,2,1,0:T(8,128)S(1)} custom-call(f32[24,8,8,128]{3,2,1,0:T(8,128)S(1)} %get-tuple-element.34.c, f32[8,8,128]{2,1,0:T(8,128)S(1)} %get-tuple-element.36.edges, f32[8,8,128]{2,1,0:T(8,128)S(1)} %get-tuple-element.51.ends, f32[2,8,128]{2,1,0:T(8,128)S(1)} %get-tuple-element.52.rims, ...), custom_call_target="tpu_custom_call" | custom-call | tf_op jit(solution)/shard_map/tracers/pallas_call | solution.py:685
  16.0 0.0 collective-permute-done.4.refs_3_
  16.1 1.0 %last.1 = (f32[24,8,8,128]{3,2,1,0:T(8,128)}, f32[4,8,256]{2,1,0:T(8,128)}, f32[4,8,256]{2,1,0:T(8,128)}, f32[4,8,256]{2,1,0:T(8,128)}, f32[4,8,256]{2,1,0:T(8,128)}) custom-call(f32[24,8,8,128]{3,2,1,0:T(8,128)S(1)} %tracers.1.refs_0_, f32[3,4,8,256]{3,2,1,0:T(8,128)S(1)} %get-tuple-element.55.refs_1_, f32[2,8,8,128]{3,2,1,0:T(8,128)S(1)} %get-tuple-element.56.refs_2_, ...), custom_call_target="tpu_custom_call" | custom-call | tf_op jit(solution)/shard_map/last/pallas_call | solution.py:685
Async XLA Ops:
  2.1 3.5 %collective-permute-start.1 = (f32[58,8,128]{2,1,0:T(8,128)S(1)}, f32[58,8,128]{2,1,0:T(8,128)S(1)}, u32[]{:S(2)}, u32[]{:S(2)}) collective-permute-start(f32[58,8,128]{2,1,0:T(8,128)S(1)} %get-tuple-element.41), channel_id=1, source_target_pairs={{0,1},{1,0},{2,3},{3,2},{4,5},{5,4},{6,7},{7,6},{8,9},{9,8},{10,11... | collective-permute-start | bytes 712712 | tf_op jit(solution)/shard_map/ppermute | solution.py:705
  2.6 6.7 %collective-permute-start = (f32[58,8,128]{2,1,0:T(8,128)S(1)}, f32[58,8,128]{2,1,0:T(8,128)S(1)}, u32[]{:S(2)}, u32[]{:S(2)}) collective-permute-start(f32[58,8,128]{2,1,0:T(8,128)S(1)} %get-tuple-element.40.z), channel_id=1, source_target_pairs={{0,16},{1,4},{2,18},{3,6},{4,1},{5,8},{6,3},{7,10},{8,5},{9,12},{1... | collective-permute-start | bytes 712712 | tf_op jit(solution)/shard_map/ppermute | solution.py:705
  5.8 5.3 %collective-permute-start.2 = (f32[26,8,128]{2,1,0:T(8,128)S(1)}, f32[26,8,128]{2,1,0:T(8,128)S(1)}, u32[]{:S(2)}, u32[]{:S(2)}) collective-permute-start(f32[26,8,128]{2,1,0:T(8,128)S(1)} %get-tuple-element.49), channel_id=1, source_target_pairs={{0,2},{1,3},{2,0},{3,1},{4,6},{5,7},{6,4},{7,5},{8,10},{9,11},{10,... | collective-permute-start | bytes 319496 | tf_op jit(solution)/shard_map/ppermute | solution.py:705
  7.4 3.8 %collective-permute-start.3 = (f32[5,8,128]{2,1,0:T(8,128)S(1)}, f32[5,8,128]{2,1,0:T(8,128)S(1)}, u32[]{:S(2)}, u32[]{:S(2)}) collective-permute-start(f32[5,8,128]{2,1,0:T(8,128)S(1)} %get-tuple-element.50), channel_id=1, source_target_pairs={{0,16},{1,6},{2,18},{3,4},{4,3},{5,10},{6,1},{7,8},{8,7},{9,14},{1... | collective-permute-start | bytes 61448 | tf_op jit(solution)/shard_map/ppermute | solution.py:705
  12.0 4.1 %collective-permute-start.4 = (f32[2,4,8,128]{3,2,1,0:T(8,128)S(1)}, f32[2,4,8,128]{3,2,1,0:T(8,128)S(1)}, u32[]{:S(2)}, u32[]{:S(2)}) collective-permute-start(f32[2,4,8,128]{3,2,1,0:T(8,128)S(1)} %get-tuple-element.57), channel_id=1, source_target_pairs={{0,2},{1,3},{2,0},{3,1},{4,6},{5,7},{6,4},{7,5},{8,10},{9,11},{10,... | collective-permute-start | bytes 98312 | tf_op jit(solution)/shard_map/ppermute | solution.py:705

commit v6 on v5

--- a/solution.py
+++ b/solution.py
@@ -40,7 +40,7 @@
     zero = jnp.zeros((ROWS, LANES), jnp.float32)
     total, edge = [zero] * len(tiles), [zero] * len(tiles)
     for b in range(tracers):
-        rate = jnp.broadcast_to(rates[:1, b : b + 1], (ROWS, LANES))
+        rate = rates[b]
         mine = lane // 4 == b
         for i, get in enumerate(tiles):
             q = get(b)
@@ -84,9 +84,10 @@
     return roll(tile, -(start + 2 * NEAR * i + NEAR), 1)
 
 
-def load_kernel(n, u, v, t, h, count, rates, c, f_out, c_out, d_out, rates_out, z_out, r_out, f_sem, c_sem):
+def load_kernel(n, u, v, t, h, count, rates, c, f_out, c_out, d_out, rates_out, z_out, r_out, sums, edges, first_rates, *refs):
+    pays, (f_sem, c_sem) = refs[: n - 1], refs[n - 1 :]
     tracers, share = c.shape[0], f_out.shape[1]
-    _, _, role = position()
+    _, lon, role = position()
     upper = role == 1
     copies = [pltpu.make_async_copy(ref, f_out.at[i], f_sem.at[i]) for i, ref in enumerate((u, v, t, h))]
     copies.append(pltpu.make_async_copy(count, d_out, f_sem.at[FIELDS]))
@@ -119,6 +120,11 @@
         z_out[base + block] = depth
         r_out[base + block] = depth
     base += n
+    for b in range(tracers):
+        first_rates[b] = jnp.broadcast_to(rates_out[:1, b : b + 1], (ROWS, LANES))
+    lane = iota((ROWS, LANES), 1)
+    zero = jnp.zeros((ROWS, LANES), jnp.float32)
+    total, edge = [zero] * LEVELS, [zero] * LEVELS
     for i, copy in enumerate(c_copies):
         copy.wait()
         for b in range(i * batch, (i + 1) * batch):
@@ -126,15 +132,15 @@
                 bottom, top = c_out[b, :, far, :], c_out[b, :, ROWS - 1 - far, :]
                 z_out[base + 2 * b + far] = jnp.where(upper, top, bottom)
                 r_out[base + 2 * b + far] = jnp.where(upper, bottom, top)
-
-
-def edge_kernel(n, rates, c, sums, edges, *outs):
-    _, lon, _ = position()
-    total, edge = packed(c.shape[0], rates, [lambda b, k=k: c[b, k] for k in range(LEVELS)])
+            for k in range(LEVELS):
+                q = c_out[b, k]
+                total[k] = total[k] + first_rates[b] * q
+                edge[k] = jnp.where(lane // 4 == b, roll(q, 4 * b + 2, 1), edge[k])
     for k in range(LEVELS):
+        edge[k] = jnp.where(lane // 4 == tracers, roll(total[k], 4 * tracers + 2, 1), edge[k])
         sums[k], edges[k] = total[k], edge[k]
-    low = iota((ROWS, LANES), 1) % 4 < 2
-    for s, out in enumerate(outs):
+    low = lane % 4 < 2
+    for s, out in enumerate(pays):
         to_east = lax.rem(lon + (s + 1), n) > lon
         for i in range(LEVELS // 2):
             a, b = (jnp.where(to_east, q, roll(q, -2, 1)) for q in (edge[2 * i], edge[2 * i + 1]))
@@ -342,9 +348,9 @@
         wet = [wets[i, lon * share + level] for i in range(3)]
         uu, vv, tt, stencil, stencil2 = two_steps(lambda i: dyn[i, level], wet, turn, shifts)
         for i, q in enumerate(stencil):
-            coef1[i, level] = q
+            coef1[i, lon * share + level] = q
         for i, q in enumerate(stencil2):
-            coef2[i, level] = q
+            coef2[i, lon * share + level] = q
         for i, q in enumerate((uu, vv, tt)):
             f_out[i, level, :, block_of(lon)] = q[OWN_ROWS, FIRST]
             if n == 2:
@@ -361,8 +367,7 @@
             rows = halo.sides(r[base + 2 * b + far], z[base + 2 * b + far])
             if b == 0:
                 chl = rows
-            rate = jnp.broadcast_to(rates[:1, b : b + 1], (ROWS, LANES))
-            total = [a + rate * q for a, q in zip(total, rows)]
+            total = [a + rates[b] * q for a, q in zip(total, rows)]
         for i, rows in enumerate((chl, total)):
             mix[i, :, RING_ROWS - 1 - far] = rows[0]
             mix[i, :, ROWS + far] = rows[1]
@@ -387,22 +392,18 @@
 
 
 def flow_kernel(n, strips, tracers, *refs):
-    own1, own2, wets, mix = refs[:4]
+    wets, mix = refs[2:4]
     others = n - 1
     xs, xzs = (refs[6 + i * others : 6 + (i + 1) * others] for i in range(2))
     coef1, coef2, ends, rims, light_out = refs[6 + 2 * others : 11 + 2 * others]
     heats = refs[11 + 2 * others : 11 + 3 * others]
     dyn, side_mix, all_edges, all_rims, moved = refs[11 + 3 * others :]
-    share = own1.shape[1]
+    share = LEVELS // n
     strip, lon, _ = pos = position()
     halo = Halo(pos, strips)
     lane = iota((ROWS, LANES), 1)
     turn = coriolis(strip, strips)
     shifts = around(lon, n)
-    mine = pl.ds(lon * share, share)
-    for i in range(5):
-        coef1[i, mine] = own1[i]
-        coef2[i, mine] = own2[i]
 
     fields = FIELDS * share
     end = fields + LEVELS // 2
@@ -681,13 +682,13 @@
     def scratch(*dims):
         return pltpu.VMEM(dims, jnp.float32)
 
-    def call(kernel, name, args, in_specs, out_shape, out_specs=None, scratch_shapes=()):
+    def call(kernel, name, args, in_specs, out_shape, out_specs=None, **options):
         return pl.pallas_call(
             kernel,
             out_shape=tuple(out_shape),
             in_specs=in_specs,
             out_specs=out_specs or (vmem,) * len(out_shape),
-            scratch_shapes=scratch_shapes,
+            **options,
             compiler_params=params,
             name=name,
         )(*args)
@@ -721,7 +722,7 @@
 
     shifts = range(1, n)
     z_tiles = LEVELS + n + 2 * tracers
-    f, c_here, depth, rates, z_pay, r_pay = call(
+    f, c_here, depth, rates, z_pay, r_pay, sums, edges, first_rates, *pays = call(
         functools.partial(load_kernel, n),
         "load",
         [pltpu.with_memory_space_constraint(q, pltpu.HBM) for q in (u, v, t, h, count, rates, c)],
@@ -733,22 +734,19 @@
             shape(*rates.shape),
             tiles(z_tiles),
             tiles(z_tiles),
-        ],
-        scratch_shapes=[dma((FIELDS + 2,)), dma((4,))],
+            tiles(LEVELS),
+            tiles(LEVELS),
+            tiles(tracers),
+        ]
+        + [tiles(LEVELS // 2)] * (n - 1),
+        scratch_shapes=[dma((FIELDS + 2,)), dma((2,))],
     )
     r_in = permute(r_pay, r_target)
     z_in = permute(z_pay, z_target(0))
-    sums, edges, *pays = call(
-        functools.partial(edge_kernel, n),
-        "edges",
-        (rates, c_here),
-        [vmem] * 2,
-        [tiles(LEVELS)] * 2 + [tiles(LEVELS // 2)] * (n - 1),
-    )
     pays = call(
         functools.partial(join_kernel, n),
         "join",
-        (rates, f, z_pay, r_in, *pays),
+        (first_rates, f, z_pay, r_in, *pays),
         [vmem] * (n + 3),
         [tiles(FIELDS * share + LEVELS // 2 + share + 2)] * (n - 1) + [tiles(share + 1)] * (n - 1),
     )
@@ -765,15 +763,15 @@
         [shape(m_size, 3 * m_size, dtype=bf16), shape(3 * e_size, e_size, dtype=bf16)],
     )
 
-    args = (rates, f, depth, c_here, sums, z_in, r_in)
+    args = (first_rates, f, depth, c_here, sums, z_in, r_in)
     own1, own2, wets, mix, f_new = call(
         functools.partial(own_kernel, n, strips),
         "own",
         args,
         [vmem] * len(args),
         [
-            shape(5, share, RING_ROWS, RING_COLS),
-            tiles(5, share),
+            shape(7, LEVELS, RING_ROWS, RING_COLS),
+            tiles(7, LEVELS),
             shape(3, LEVELS, RING_ROWS, RING_COLS),
             shape(2, LEVELS, RING_ROWS, LANES),
             shape(3, *u.shape),
@@ -794,6 +792,7 @@
             tiles(2, LEVELS),
         ]
         + [tiles(2, share)] * (n - 1),
+        input_output_aliases={0: 0, 1: 1},
         scratch_shapes=[
             scratch(FIELDS, (n - 1) * share, RING_ROWS, RING_COLS),
             scratch(2, LEVELS, RING_ROWS, LANES),

time: 17.2 us -> 17 us (0.988)
  starting transfers between devices: 7.18 us -> 7.62 us
  Pallas kernels: 7.74 us -> 7.41 us
  waiting for transfers between devices: 1.41 us -> 1.11 us
    ppermute x5, starting transfers between devices: 7.18 us -> 7.62 us  [permute(): return lax.ppermute(q, ('grp', 'lat', 'lon', 'role'), pairs)]
    pallas_call x8 -> x7, Pallas kernels: 7.74 us -> 7.41 us  [call(): pl.pallas_call(kernel, out_shape=tuple(out_shape), in_specs=in_specs, out...]
    ppermute x5, waiting for transfers between devices: 1.41 us -> 1.11 us  [permute(): return lax.ppermute(q, ('grp', 'lat', 'lon', 'role'), pairs)]
  transfers between devices with their start and end apart: 5 -> 5, of which waited for: 2 -> 2; matrix products, arithmetic and copies ran while one was open for 0% -> 0% of each run, Pallas kernels for 26% -> 23%
where the time goes in v6:
time: 17 us; the launch traced here: 16.8 us
  starting transfers between devices  7.62 us (45%)
  Pallas kernels  7.41 us (44%)
  waiting for transfers between devices  1.11 us (7%)
  between operations  0.68 us (4%)
    ppermute x5, starting transfers between devices, permute(): return lax.ppermute(q, ('grp', 'lat', 'lon', 'role'), pairs)  7.62 us
    pallas_call x7, Pallas kernels, call(): pl.pallas_call(kernel, out_shape=tuple(out_shape), in_specs=in_specs, out...  7.41 us
    ppermute x5, waiting for transfers between devices, permute(): return lax.ppermute(q, ('grp', 'lat', 'lon', 'role'), pairs)  1.11 us
  transfers between devices with their start and end apart: 5, of which 2 were waited for; matrix products, arithmetic and copies ran while one was open for 0% of the time, Pallas kernels for 23%

profile of v6, /device:TPU:0, one launch (start us, length us, event | category | flops | bytes accessed | tf_op | source)
XLA Modules:
  0.0 16.8 jit_solution(11508621149187041251)
XLA Ops:
  0.6 1.7 %load.1 = (f32[4,4,8,256]{3,2,1,0:T(8,128)S(1)}, f32[24,8,8,128]{3,2,1,0:T(8,128)S(1)}, s32[8,256]{1,0:T(8,128)S(1)}, f32[24,24]{1,0:T(8,128)S(1)}, f32[58,8,128...) custom-call(f32[4,8,256]{2,1,0:T(8,128)} %u.1, ...), custom_call_target="tpu_custom_call" | custom-call | tf_op jit(solution)/shard_map/load/pallas_call | solution.py:686
  2.4 0.5 %collective-permute-start.1 = (f32[58,8,128]{2,1,0:T(8,128)S(1)}, f32[58,8,128]{2,1,0:T(8,128)S(1)}, u32[]{:S(2)}, u32[]{:S(2)}) collective-permute-start(f32[58,8,128]{2,1,0:T(8,128)S(1)} %get-tuple-element.42), channel_id=1, source_target_pairs={{0,1},{1,0},{2,3},{3,2},{4,5},{5,4},{6,7},{7,6},{8,9},{9,8},{10,11... | collective-permute-start | bytes 712712 | tf_op jit(solution)/shard_map/ppermute | solution.py:706
  2.9 2.6 %collective-permute-start = (f32[58,8,128]{2,1,0:T(8,128)S(1)}, f32[58,8,128]{2,1,0:T(8,128)S(1)}, u32[]{:S(2)}, u32[]{:S(2)}) collective-permute-start(f32[58,8,128]{2,1,0:T(8,128)S(1)} %get-tuple-element.41.z), channel_id=1, source_target_pairs={{0,16},{1,4},{2,18},{3,6},{4,1},{5,8},{6,3},{7,10},{8,5},{9,12},{1... | collective-permute-start | bytes 712712 | tf_op jit(solution)/shard_map/ppermute | solution.py:706
  5.5 0.0 collective-permute-done.1.r
  5.5 0.1 join.1
  5.6 1.6 %collective-permute-start.2 = (f32[26,8,128]{2,1,0:T(8,128)S(1)}, f32[26,8,128]{2,1,0:T(8,128)S(1)}, u32[]{:S(2)}, u32[]{:S(2)}) collective-permute-start(f32[26,8,128]{2,1,0:T(8,128)S(1)} %get-tuple-element.51), channel_id=1, source_target_pairs={{0,2},{1,3},{2,0},{3,1},{4,6},{5,7},{6,4},{7,5},{8,10},{9,11},{10,... | collective-permute-start | bytes 319496 | tf_op jit(solution)/shard_map/ppermute | solution.py:706
  7.2 1.4 %collective-permute-start.3 = (f32[5,8,128]{2,1,0:T(8,128)S(1)}, f32[5,8,128]{2,1,0:T(8,128)S(1)}, u32[]{:S(2)}, u32[]{:S(2)}) collective-permute-start(f32[5,8,128]{2,1,0:T(8,128)S(1)} %get-tuple-element.52), channel_id=1, source_target_pairs={{0,16},{1,6},{2,18},{3,4},{4,3},{5,10},{6,1},{7,8},{8,7},{9,14},{1... | collective-permute-start | bytes 61448 | tf_op jit(solution)/shard_map/ppermute | solution.py:706
  8.6 0.6 %spread.1 = (bf16[192,576]{1,0:T(8,128)(2,1)S(1)}, bf16[384,128]{1,0:T(8,128)(2,1)S(1)}) custom-call(f32[24,24]{1,0:T(8,128)S(1)} %get-tuple-element.47.rates), custom_call_target="tpu_custom_call" | custom-call | tf_op jit(solution)/shard_map/spread/pallas_call | solution.py:686
  9.2 0.4 %collective-permute-done.z = f32[58,8,128]{2,1,0:T(8,128)S(1)} collective-permute-done((f32[58,8,128]{2,1,0:T(8,128)S(1)}, f32[58,8,128]{2,1,0:T(8,128)S(1)}, u32[]{:S(2)}, u32[]{:S(2)}) %collective-permute-start) | collective-permute-done | bytes 237600 | tf_op jit(solution)/shard_map/ppermute | solution.py:706
  9.6 0.7 %own.1 = (f32[7,8,16,256]{3,2,1,0:T(8,128)S(1)}, f32[7,8,8,128]{3,2,1,0:T(8,128)S(1)}, f32[3,8,16,256]{3,2,1,0:T(8,128)S(1)}, f32[2,8,16,128]{3,2,1,0:T(8,128)S(1)}, f32[3,4,8,256]{3,2,1,0:T(8,128)S(1)}) custom-call(f32[24,8,128]{2,1,0:T(8,128)S(1)} %get-tuple-element.37.rates, f32[4,4,8,256]{3,2,1,0:T(8,128)S(1)} %get-tuple-element.38.f, ...), custom_call_target="tpu_custom_call" | custom-call | tf_op jit(solution)/shard_map/own/pallas_call | solution.py:686
  10.3 0.7 %collective-permute-done.3.refs_7_ = f32[5,8,128]{2,1,0:T(8,128)S(1)} collective-permute-done((f32[5,8,128]{2,1,0:T(8,128)S(1)}, f32[5,8,128]{2,1,0:T(8,128)S(1)}, u32[]{:S(2)}, u32[]{:S(2)}) %collective-permute-start.3) | collective-permute-done | bytes 20512 | tf_op jit(solution)/shard_map/ppermute | solution.py:706
  11.0 0.0 collective-permute-done.2.refs_6_
  11.0 0.8 %flow.1 = (f32[7,8,16,256]{3,2,1,0:T(8,128)S(1)}, f32[7,8,8,128]{3,2,1,0:T(8,128)S(1)}, f32[8,8,128]{2,1,0:T(8,128)S(1)}, f32[2,8,128]{2,1,0:T(8,128)S(1)}, f32[...) custom-call(f32[7,8,16,256]{3,2,1,0:T(8,128)S(1)} %get-tuple-element.43.refs_, ...), custom_call_target="tpu_custom_call", output_to_operand_aliasing={{0}: (0, {}), {1}: (1, {})} | custom-call | tf_op jit(solution)/shard_map/flow/pallas_call | solution.py:686
  11.8 1.5 %collective-permute-start.4 = (f32[2,4,8,128]{3,2,1,0:T(8,128)S(1)}, f32[2,4,8,128]{3,2,1,0:T(8,128)S(1)}, u32[]{:S(2)}, u32[]{:S(2)}) collective-permute-start(f32[2,4,8,128]{3,2,1,0:T(8,128)S(1)} %get-tuple-element.59), channel_id=1, source_target_pairs={{0,2},{1,3},{2,0},{3,1},{4,6},{5,7},{6,4},{7,5},{8,10},{9,11},{10,... | collective-permute-start | bytes 98312 | tf_op jit(solution)/shard_map/ppermute | solution.py:706
  13.3 2.5 %tracers.1.refs_0_ = f32[24,8,8,128]{3,2,1,0:T(8,128)S(1)} custom-call(f32[24,8,8,128]{3,2,1,0:T(8,128)S(1)} %get-tuple-element.35.c, f32[8,8,128]{2,1,0:T(8,128)S(1)} %get-tuple-element.36.edges, f32[8,8,128]{2,1,0:T(8,128)S(1)} %get-tuple-element.53.ends, f32[2,8,128]{2,1,0:T(8,128)S(1)} %get-tuple-element.54.rims, ...), custom_call_target="tpu_custom_call" | custom-call | tf_op jit(solution)/shard_map/tracers/pallas_call | solution.py:686
  15.9 0.0 collective-permute-done.4.refs_3_
  15.9 1.0 %last.1 = (f32[24,8,8,128]{3,2,1,0:T(8,128)}, f32[4,8,256]{2,1,0:T(8,128)}, f32[4,8,256]{2,1,0:T(8,128)}, f32[4,8,256]{2,1,0:T(8,128)}, f32[4,8,256]{2,1,0:T(8,128)}) custom-call(f32[24,8,8,128]{3,2,1,0:T(8,128)S(1)} %tracers.1.refs_0_, f32[3,4,8,256]{3,2,1,0:T(8,128)S(1)} %get-tuple-element.57.refs_1_, f32[2,8,8,128]{3,2,1,0:T(8,128)S(1)} %get-tuple-element.58.refs_2_, ...), custom_call_target="tpu_custom_call" | custom-call | tf_op jit(solution)/shard_map/last/pallas_call | solution.py:686
Async XLA Ops:
  2.4 3.1 %collective-permute-start.1 = (f32[58,8,128]{2,1,0:T(8,128)S(1)}, f32[58,8,128]{2,1,0:T(8,128)S(1)}, u32[]{:S(2)}, u32[]{:S(2)}) collective-permute-start(f32[58,8,128]{2,1,0:T(8,128)S(1)} %get-tuple-element.42), channel_id=1, source_target_pairs={{0,1},{1,0},{2,3},{3,2},{4,5},{5,4},{6,7},{7,6},{8,9},{9,8},{10,11... | collective-permute-start | bytes 712712 | tf_op jit(solution)/shard_map/ppermute | solution.py:706
  2.9 6.7 %collective-permute-start = (f32[58,8,128]{2,1,0:T(8,128)S(1)}, f32[58,8,128]{2,1,0:T(8,128)S(1)}, u32[]{:S(2)}, u32[]{:S(2)}) collective-permute-start(f32[58,8,128]{2,1,0:T(8,128)S(1)} %get-tuple-element.41.z), channel_id=1, source_target_pairs={{0,16},{1,4},{2,18},{3,6},{4,1},{5,8},{6,3},{7,10},{8,5},{9,12},{1... | collective-permute-start | bytes 712712 | tf_op jit(solution)/shard_map/ppermute | solution.py:706
  5.6 5.3 %collective-permute-start.2 = (f32[26,8,128]{2,1,0:T(8,128)S(1)}, f32[26,8,128]{2,1,0:T(8,128)S(1)}, u32[]{:S(2)}, u32[]{:S(2)}) collective-permute-start(f32[26,8,128]{2,1,0:T(8,128)S(1)} %get-tuple-element.51), channel_id=1, source_target_pairs={{0,2},{1,3},{2,0},{3,1},{4,6},{5,7},{6,4},{7,5},{8,10},{9,11},{10,... | collective-permute-start | bytes 319496 | tf_op jit(solution)/shard_map/ppermute | solution.py:706
  7.2 3.8 %collective-permute-start.3 = (f32[5,8,128]{2,1,0:T(8,128)S(1)}, f32[5,8,128]{2,1,0:T(8,128)S(1)}, u32[]{:S(2)}, u32[]{:S(2)}) collective-permute-start(f32[5,8,128]{2,1,0:T(8,128)S(1)} %get-tuple-element.52), channel_id=1, source_target_pairs={{0,16},{1,6},{2,18},{3,4},{4,3},{5,10},{6,1},{7,8},{8,7},{9,14},{1... | collective-permute-start | bytes 61448 | tf_op jit(solution)/shard_map/ppermute | solution.py:706
  11.8 4.1 %collective-permute-start.4 = (f32[2,4,8,128]{3,2,1,0:T(8,128)S(1)}, f32[2,4,8,128]{3,2,1,0:T(8,128)S(1)}, u32[]{:S(2)}, u32[]{:S(2)}) collective-permute-start(f32[2,4,8,128]{3,2,1,0:T(8,128)S(1)} %get-tuple-element.59), channel_id=1, source_target_pairs={{0,2},{1,3},{2,0},{3,1},{4,6},{5,7},{6,4},{7,5},{8,10},{9,11},{10,... | collective-permute-start | bytes 98312 | tf_op jit(solution)/shard_map/ppermute | solution.py:706
